TPU v7x, 32 devices: a whole 2x2x4 slice. The times are simulated.
32 devices in a mesh: rep: 4 (over z), fsdp: 8 (over y, x, core).
Axes of the slice: x: 2, y: 2, z: 4, core: 2. Of those that a mesh axis runs over, the one named last changes fastest.
Arguments:
- tokens: bfloat16 [32, 1024, 640], P(('rep', 'fsdp')), may hold values from -6 to 6
- masked: int32 [32, 1024], P(('rep', 'fsdp')), may hold values from 0 to 1, as said below
- cotangent: bfloat16 [32, 1024, 640], P(('rep', 'fsdp')), may hold values from -6 to 6
- norm1_gain: bfloat16 [640], P('fsdp'), may hold values from 0.5 to 1.5
- norm1_shift: bfloat16 [640], P('fsdp'), may hold values from -1.75 to 1.75
- w_qkv: bfloat16 [640, 1920], P('fsdp'), may hold values from -0.3125 to 0.3125
- bias_query: bfloat16 [640], P('fsdp'), may hold values from -3 to 3
- bias_value: bfloat16 [640], P('fsdp'), may hold values from -3 to 3
- w_out: bfloat16 [640, 640], P('fsdp'), may hold values from -2 to 2
- bias_out: bfloat16 [640], P('fsdp'), may hold values from -3 to 3
- norm2_gain: bfloat16 [640], P('fsdp'), may hold values from 0.5 to 1.5
- norm2_shift: bfloat16 [640], P('fsdp'), may hold values from -1.75 to 1.75
- w_up: bfloat16 [640, 5120], P('fsdp'), may hold values from -0.25 to 0.25
- bias_up: bfloat16 [5120], P('fsdp'), may hold values from -3 to 3
- w_down: bfloat16 [5120, 640], P('fsdp'), may hold values from -0.15625 to 0.15625
- bias_down: bfloat16 [640], P('fsdp'), may hold values from -3 to 3
Outputs:
- result: bfloat16 [32, 1024, 640], P(('rep', 'fsdp'))
- grad_tokens: bfloat16 [32, 1024, 640], P(('rep', 'fsdp'))
- grad_norm1_gain: float32 [640], P('fsdp')
- grad_norm1_shift: float32 [640], P('fsdp')
- grad_w_qkv: float32 [640, 1920], P('fsdp')
- grad_bias_query: float32 [640], P('fsdp')
- grad_bias_value: float32 [640], P('fsdp')
- grad_w_out: float32 [640, 640], P('fsdp')
- grad_bias_out: float32 [640], P('fsdp')
- grad_norm2_gain: float32 [640], P('fsdp')
- grad_norm2_shift: float32 [640], P('fsdp')
- grad_w_up: float32 [640, 5120], P('fsdp')
- grad_bias_up: float32 [5120], P('fsdp')
- grad_w_down: float32 [5120, 640], P('fsdp')
- grad_bias_down: float32 [640], P('fsdp')
Inputs may be any that keep to these rules, and one draw needn't show every extreme that they name: Each sequence has its own rate of masked positions, between 5 and 30 in 100; positions are masked independently at that rate, so the number of masked positions in a sequence is random and not bounded by the rate.
All inputs are finite; a program needn't handle non-finite values.
Results may differ from a plain program's by a relative error of at most 0.015.
Values may be sent and summed in bfloat16 or wider, within the bound.
A program may use at most 192 MiB of HBM per device.

v0:
```python
import jax
import jax.numpy as jnp
from jax import lax
from jax.sharding import PartitionSpec as P

HEADS = 20
HEAD_DIM = 32


def layer_norm(values, gain, shift):
    mean = jnp.mean(values, axis=-1, keepdims=True)
    centred = values - mean
    variance = jnp.mean(centred * centred, axis=-1, keepdims=True)
    return centred * lax.rsqrt(variance + 1e-05) * gain + shift


def exact_gelu(values):
    return jax.nn.gelu(values, approximate=False)


def split_heads(block, seqs, length):
    return block.reshape(seqs, length, HEADS, HEAD_DIM).transpose(2, 0, 1, 3)


def join_heads(block):
    heads, seqs, length, size = block.shape
    return block.transpose(1, 2, 0, 3).reshape(seqs * length, heads * size)


def local(
    tokens,
    masked,
    cotangent,
    norm1_gain,
    norm1_shift,
    w_qkv,
    bias_query,
    bias_value,
    w_out,
    bias_out,
    norm2_gain,
    norm2_shift,
    w_up,
    bias_up,
    w_down,
    bias_down,
):
    single_float32 = jnp.float32
    brain_float16 = jnp.bfloat16
    seqs, length, width = tokens.shape
    rows = seqs * length
    score_scale = HEAD_DIM ** (-0.5)
    inputs = tokens.reshape(rows, width).astype(single_float32)
    attn_set = (
        lax.all_gather(norm1_gain, "fsdp", axis=0, tiled=True),
        lax.all_gather(norm1_shift, "fsdp", axis=0, tiled=True),
        lax.all_gather(w_qkv, "fsdp", axis=0, tiled=True),
        lax.all_gather(bias_query, "fsdp", axis=0, tiled=True),
        lax.all_gather(bias_value, "fsdp", axis=0, tiled=True),
        lax.all_gather(w_out, "fsdp", axis=0, tiled=True),
        lax.all_gather(bias_out, "fsdp", axis=0, tiled=True),
    )
    gain_one, shift_one, weight_qkv, query_bias, value_bias, weight_out, out_bias = attn_set
    normed1 = layer_norm(
        inputs, gain_one.astype(single_float32), shift_one.astype(single_float32)
    ).astype(brain_float16)
    full_bias = jnp.concatenate([query_bias, jnp.zeros_like(query_bias), value_bias]).astype(
        single_float32
    )
    projected = (
        jnp.dot(normed1, weight_qkv, preferred_element_type=single_float32) + full_bias
    ).astype(brain_float16)
    queries = split_heads(projected[:, :width], seqs, length)
    keys_all = split_heads(projected[:, width : 2 * width], seqs, length)
    values_all = split_heads(projected[:, 2 * width :], seqs, length)

    def head_forward(operands):
        query_rows, key_rows, value_rows = operands
        attention_logits = (
            jnp.einsum("fep,fwp->few", query_rows, key_rows, preferred_element_type=single_float32)
            * score_scale
        )
        highest = jnp.max(attention_logits, axis=-1, keepdims=True)
        expo = jnp.exp(attention_logits - highest)
        total = jnp.sum(expo, axis=-1, keepdims=True)
        attention_probs = (expo / total).astype(brain_float16)
        layer_output = jnp.einsum(
            "fbn,fna->fba", attention_probs, value_rows, preferred_element_type=single_float32
        ).astype(brain_float16)
        return (layer_output, (highest + jnp.log(total))[..., 0])

    heads_out, log_total = lax.map(head_forward, (queries, keys_all, values_all))
    joined = join_heads(heads_out)
    middle = (
        inputs
        + jnp.dot(joined, weight_out, preferred_element_type=single_float32)
        + out_bias.astype(single_float32)
    )
    ffn_set = (
        lax.all_gather(norm2_gain, "fsdp", axis=0, tiled=True),
        lax.all_gather(norm2_shift, "fsdp", axis=0, tiled=True),
        lax.all_gather(w_up, "fsdp", axis=0, tiled=True),
        lax.all_gather(bias_up, "fsdp", axis=0, tiled=True),
        lax.all_gather(w_down, "fsdp", axis=0, tiled=True),
        lax.all_gather(bias_down, "fsdp", axis=0, tiled=True),
    )
    gain_two, shift_two, weight_up, up_bias, weight_down, down_bias = ffn_set
    normed2 = layer_norm(
        middle, gain_two.astype(single_float32), shift_two.astype(single_float32)
    ).astype(brain_float16)
    hidden = jnp.dot(normed2, weight_up, preferred_element_type=single_float32) + up_bias.astype(
        single_float32
    )
    active = exact_gelu(hidden).astype(brain_float16)
    layer_output = (
        middle
        + jnp.dot(active, weight_down, preferred_element_type=single_float32)
        + down_bias.astype(single_float32)
    )
    result = layer_output.astype(brain_float16).reshape(seqs, length, width)
    back_gain2, back_shift2, back_up, back_down = (
        lax.all_gather(norm2_gain, "fsdp", axis=0, tiled=True),
        lax.all_gather(norm2_shift, "fsdp", axis=0, tiled=True),
        lax.all_gather(w_up, "fsdp", axis=0, tiled=True),
        lax.all_gather(w_down, "fsdp", axis=0, tiled=True),
    )
    mask_rows = masked.reshape(rows, 1).astype(single_float32)
    grad_out = cotangent.reshape(rows, width).astype(single_float32) * mask_rows
    grad_low = grad_out.astype(brain_float16)
    grad_w_down = jnp.einsum("rf,rd->fd", active, grad_low, preferred_element_type=single_float32)
    grad_bias_down = jnp.sum(grad_low.astype(single_float32), axis=0)
    grad_active = jnp.einsum(
        "rd,fd->rf", grad_low, back_down, preferred_element_type=single_float32
    )
    _, gelu_back = jax.vjp(exact_gelu, hidden)
    grad_hidden = gelu_back(grad_active)[0].astype(brain_float16)
    grad_w_up = jnp.einsum("rd,rf->df", normed2, grad_hidden, preferred_element_type=single_float32)
    grad_bias_up = jnp.sum(grad_hidden.astype(single_float32), axis=0)
    grad_normed2 = jnp.einsum(
        "rf,df->rd", grad_hidden, back_up, preferred_element_type=single_float32
    )
    _, norm_two_back = jax.vjp(
        layer_norm, middle, back_gain2.astype(single_float32), back_shift2.astype(single_float32)
    )
    grad_middle_part, grad_gain_two, grad_shift_two = norm_two_back(grad_normed2)
    grad_middle = grad_out + grad_middle_part
    ffn_shares = (
        lax.psum_scatter(grad_gain_two, "fsdp", scatter_dimension=0, tiled=True),
        lax.psum_scatter(grad_shift_two, "fsdp", scatter_dimension=0, tiled=True),
        lax.psum_scatter(grad_w_up, "fsdp", scatter_dimension=0, tiled=True),
        lax.psum_scatter(grad_bias_up, "fsdp", scatter_dimension=0, tiled=True),
        lax.psum_scatter(grad_w_down, "fsdp", scatter_dimension=0, tiled=True),
        lax.psum_scatter(grad_bias_down, "fsdp", scatter_dimension=0, tiled=True),
    )
    back_gain1, back_shift1, back_qkv, back_out = (
        lax.all_gather(norm1_gain, "fsdp", axis=0, tiled=True),
        lax.all_gather(norm1_shift, "fsdp", axis=0, tiled=True),
        lax.all_gather(w_qkv, "fsdp", axis=0, tiled=True),
        lax.all_gather(w_out, "fsdp", axis=0, tiled=True),
    )
    grad_attn = grad_middle.astype(brain_float16)
    grad_w_out = jnp.einsum("rd,re->de", joined, grad_attn, preferred_element_type=single_float32)
    grad_bias_out = jnp.sum(grad_attn.astype(single_float32), axis=0)
    grad_joined = jnp.einsum(
        "re,de->rd", grad_attn, back_out, preferred_element_type=single_float32
    ).astype(brain_float16)
    grad_heads = split_heads(grad_joined, seqs, length)

    def head_backward(operands):
        query_rows, key_rows, value_rows, gradient_per_head, log_sum = operands
        attention_logits = (
            jnp.einsum("fep,fwp->few", query_rows, key_rows, preferred_element_type=single_float32)
            * score_scale
        )
        attend_full = jnp.exp(attention_logits - log_sum[..., None])
        attention_probs = attend_full.astype(brain_float16)
        gradient_values_rows = jnp.einsum(
            "cpg,cpi->cgi",
            attention_probs,
            gradient_per_head,
            preferred_element_type=single_float32,
        )
        gradient_probs = jnp.einsum(
            "fep,fwp->few", gradient_per_head, value_rows, preferred_element_type=single_float32
        )
        inner = jnp.sum(attend_full * gradient_probs, axis=-1, keepdims=True)
        gradient_logits = (attend_full * (gradient_probs - inner)).astype(brain_float16)
        grad_query = (
            jnp.einsum(
                "fbn,fna->fba", gradient_logits, key_rows, preferred_element_type=single_float32
            )
            * score_scale
        )
        grad_key = (
            jnp.einsum(
                "cpg,cpi->cgi", gradient_logits, query_rows, preferred_element_type=single_float32
            )
            * score_scale
        )
        return (grad_query, grad_key, gradient_values_rows)

    grad_query, grad_key, gradient_values_rows = lax.map(
        head_backward, (queries, keys_all, values_all, grad_heads, log_total)
    )
    grad_proj = jnp.concatenate(
        [join_heads(grad_query), join_heads(grad_key), join_heads(gradient_values_rows)], axis=1
    ).astype(brain_float16)
    grad_w_qkv = jnp.einsum("rd,re->de", normed1, grad_proj, preferred_element_type=single_float32)
    column_sums = jnp.sum(grad_proj.astype(single_float32), axis=0)
    grad_bias_query = column_sums[:width]
    grad_bias_value = column_sums[2 * width :]
    grad_normed1 = jnp.einsum(
        "re,de->rd", grad_proj, back_qkv, preferred_element_type=single_float32
    )
    _, norm_one_back = jax.vjp(
        layer_norm, inputs, back_gain1.astype(single_float32), back_shift1.astype(single_float32)
    )
    grad_input_part, grad_gain_one, grad_shift_one = norm_one_back(grad_normed1)
    grad_tokens = (grad_middle + grad_input_part).astype(brain_float16).reshape(seqs, length, width)
    attn_shares = (
        lax.psum_scatter(grad_gain_one, "fsdp", scatter_dimension=0, tiled=True),
        lax.psum_scatter(grad_shift_one, "fsdp", scatter_dimension=0, tiled=True),
        lax.psum_scatter(grad_w_qkv, "fsdp", scatter_dimension=0, tiled=True),
        lax.psum_scatter(grad_bias_query, "fsdp", scatter_dimension=0, tiled=True),
        lax.psum_scatter(grad_bias_value, "fsdp", scatter_dimension=0, tiled=True),
        lax.psum_scatter(grad_w_out, "fsdp", scatter_dimension=0, tiled=True),
        lax.psum_scatter(grad_bias_out, "fsdp", scatter_dimension=0, tiled=True),
    )
    summed = (
        lax.psum(attn_shares[0].astype(jnp.bfloat16), "rep").astype(jnp.float32),
        lax.psum(attn_shares[1].astype(jnp.bfloat16), "rep").astype(jnp.float32),
        lax.psum(attn_shares[2].astype(jnp.bfloat16), "rep").astype(jnp.float32),
        lax.psum(attn_shares[3].astype(jnp.bfloat16), "rep").astype(jnp.float32),
        lax.psum(attn_shares[4].astype(jnp.bfloat16), "rep").astype(jnp.float32),
        lax.psum(attn_shares[5].astype(jnp.bfloat16), "rep").astype(jnp.float32),
        lax.psum(attn_shares[6].astype(jnp.bfloat16), "rep").astype(jnp.float32),
        lax.psum(ffn_shares[0].astype(jnp.bfloat16), "rep").astype(jnp.float32),
        lax.psum(ffn_shares[1].astype(jnp.bfloat16), "rep").astype(jnp.float32),
        lax.psum(ffn_shares[2].astype(jnp.bfloat16), "rep").astype(jnp.float32),
        lax.psum(ffn_shares[3].astype(jnp.bfloat16), "rep").astype(jnp.float32),
        lax.psum(ffn_shares[4].astype(jnp.bfloat16), "rep").astype(jnp.float32),
        lax.psum(ffn_shares[5].astype(jnp.bfloat16), "rep").astype(jnp.float32),
    )
    return (
        result,
        grad_tokens,
        summed[0],
        summed[1],
        summed[2],
        summed[3],
        summed[4],
        summed[5],
        summed[6],
        summed[7],
        summed[8],
        summed[9],
        summed[10],
        summed[11],
        summed[12],
    )


def solution(mesh):
    in_specs = (
        P(("rep", "fsdp"), None, None),
        P(("rep", "fsdp"), None),
        P(("rep", "fsdp"), None, None),
        P("fsdp"),
        P("fsdp"),
        P("fsdp", None),
        P("fsdp"),
        P("fsdp"),
        P("fsdp", None),
        P("fsdp"),
        P("fsdp"),
        P("fsdp"),
        P("fsdp", None),
        P("fsdp"),
        P("fsdp", None),
        P("fsdp"),
    )
    out_specs = (
        P(("rep", "fsdp"), None, None),
        P(("rep", "fsdp"), None, None),
        P("fsdp"),
        P("fsdp"),
        P("fsdp", None),
        P("fsdp"),
        P("fsdp"),
        P("fsdp", None),
        P("fsdp"),
        P("fsdp"),
        P("fsdp"),
        P("fsdp", None),
        P("fsdp"),
        P("fsdp", None),
        P("fsdp"),
    )
    return jax.shard_map(local, mesh=mesh, in_specs=in_specs, out_specs=out_specs, check_vma=False)
```

profile of v0, /device:TPU:0, one launch (start us, length us, event | category | flops | bytes accessed | tf_op | source)
XLA Modules:
  0.0 930.8 jit_solution(3195141907307543401)
XLA Ops:
  18.2 26.4 %all-reduce.18 = (bf16[640]{0:T(1024)(128)(2,1)}, bf16[640]{0:T(1024)(128)(2,1)}, bf16[640]{0:T(1024)(128)(2,1)S(1)}, bf16[640]{0:T(1024)(128)(2,1)S(1)}, bf16[6...) all-reduce(bf16[640]{0:T(1024)(128)(2,1)S(1)} %dynamic-update-slice, ...), channel_id=1, replica_groups=mesh['rep'=4,'fsdp'=8] {'fsdp'}, use_global_device_ids=true, to_apply=%add.3 | all-reduce | flops 5120 | bytes 20480
  47.7 11.5 %all_gather.50 = bf16[640,640]{1,0:T(8,128)(2,1)S(1)} all-gather(bf16[80,640]{1,0:T(8,128)(2,1)S(1)} %copy-done.26), channel_id=1, replica_groups=mesh['rep'=4,'fsdp'=8] {'fsdp'}, dimensions={0}, use_global_device_ids=true | all-gather | bytes 921600 | tf_op jit(solution)/shard_map/all_gather | solution.py:60
  61.3 9.8 %all-gather = bf16[8,1,640]{2,1,0:T(2,128)(2,1)S(1)} all-gather(bf16[1,1,640]{2,1,0:T(2,128)(2,1)S(1)} %reshape.311), channel_id=1, replica_groups=mesh['rep'=4,'fsdp'=8] {'fsdp'}, dimensions={0}, use_global_device_ids=true | all-gather | bytes 11520 | tf_op jit(solution)/shard_map/all_gather | solution.py:103
  74.6 5.7 add_convert_fusion.1
  84.0 4.1 copy.67
  89.6 4.1 copy.68
  95.3 4.1 copy.69
  99.4 112.8 %while.26 = (s32[]{:T(128)}, bf16[20,1,1024,32]{2,3,1,0:T(8,128)(2,1)}, f32[20,1,1024]{2,1,0:T(1,128)}, bf16[20,1,1024,32]{3,2,1,0:T(8,128)(2,1)}, bf16[20,1,102...) while((s32[]{:T(128)}, bf16[20,1,1024,32]{2,3,1,0:T(8,128)(2,1)}, ...), condition=%wide.region_5.6_spmd, body=%wide.region_2.5_spmd.sunk | while | flops 143686656 | bytes 13478477 | solution.py:92
  216.9 56.5 %multiply_convert_fusion.1 = (bf16[1024,5120]{1,0:T(8,128)(2,1)}, f32[1024,5120]{1,0:T(8,128)}, f32[1024,5120]{1,0:T(8,128)}) fusion(f32[5120]{0:T(1024)S(1)} %bitcast.209, bf16[640,5120]{1,0:T(8,128)(2,1)} %all-gather.7.cloned.1.call-done, bf16[1024,640]{0,1:T(8,128)(2,1)S(1)} %add_convert_fusion.6.clone.4), kind=kOutput, calls=%fused_computation.60 | convolution fusion | flops 7056916480 | bytes 60313600 | tf_op jit(solution)/shard_map/dot_general | solution.py:111
  273.4 24.5 %convert_reduce_fusion = (f32[5120]{0:T(1024)S(1)}, bf16[1024,5120]{1,0:T(8,128)(2,1)}) fusion(f32[1024,5120]{1,0:T(8,128)} %get-tuple-element.246, bf16[5120,640]{1,0:T(8,128)(2,1)} %all-gather.9.cloned.1.call-done, bf16[1,1024,640]{1,2,0:T(8,128)(2,1)S(1)} %copy-done.9, f32[1024]{0:T(1024)S(1)} %bitcast.205, f32[1024,5120]{1,0:T(8,128)} %get-tuple-element.261, ...), kind=kOutput, calls=%fused_computation.58 | convolution fusion | flops 6801976320 | bytes 60338176 | tf_op jit(solution)/shard_map/rd,fd->rf/dot_general | solution.py:132
  297.9 12.5 %fusion.95 = (f32[640]{0:T(1024)S(1)}, f32[1024,640]{1,0:T(8,128)}) fusion(bf16[1024,5120]{1,0:T(8,128)(2,1)} %get-tuple-element.267, bf16[640,5120]{1,0:T(8,128)(2,1)S(1)} %copy-done.46), kind=kOutput, calls=%fused_computation.142 | convolution fusion | flops 6711541248 | bytes 19663360 | tf_op jit(solution)/shard_map/rf,df->rd/dot_general | solution.py:139
  318.7 3.8 fusion.96
  324.8 5.3 copy.73
  330.2 236.0 %while.27 = (s32[]{:T(128)}, bf16[20,1,1024,32]{2,3,1,0:T(8,128)(2,1)S(1)}, bf16[20,1,1024,32]{2,3,1,0:T(8,128)(2,1)}, bf16[20,1,1024,32]{2,3,1,0:T(8,128)(2,1)}...) while((s32[]{:T(128)}, ...), condition=%wide.region_12.13_spmd, body=%wide.region_10.12_spmd.sunk | while | flops 348191744 | bytes 33719400 | solution.py:202
  566.3 7.5 fusion.81
  574.4 13.8 %fusion.85 = f32[640,5120]{1,0:T(8,128)} fusion(bf16[1024,5120]{1,0:T(8,128)(2,1)} %get-tuple-element.267, f32[1024,640]{0,1:T(8,128)} %copy-done.2, f32[640]{0:T(1024)S(1)} %copy-done.42, f32[640]{0:T(1024)S(1)} %copy-done.31, f32[1024]{0:T(1024)S(1)} %copy-done.33, f32[1024]{0:T(1024)S(1)} %copy-done.25), kind=kOutput, calls=%fused_computation.134 | convolution fusion | flops 6714163200 | bytes 26227712 | tf_op jit(solution)/shard_map/rd,rf->df/dot_general | solution.py:137
  589.6 13.9 %fusion.75 = f32[5120,640]{1,0:T(8,128)} fusion(bf16[1024,5120]{1,0:T(8,128)(2,1)} %get-tuple-element.245, bf16[1,1024,640]{1,2,0:T(8,128)(2,1)S(1)} %copy-done.11, f32[1024]{0:T(1024)S(1)} %bitcast.207), kind=kOutput, calls=%fused_computation.110 | convolution fusion | flops 6712852480 | bytes 24907776 | tf_op jit(solution)/shard_map/rf,rd->fd/dot_general | solution.py:130
  604.9 7.8 fusion.94
  630.9 97.3 %reduce-scatter.9.cloned.1.call-done = f32[80,5120]{1,0:T(8,128)} async-done(((f32[640,5120]{1,0:T(8,128)}), f32[80,5120]{1,0:T(8,128)}) %reduce-scatter.9.cloned.1.call-update) | async-done | bytes 1638416 | tf_op jit(solution)/shard_map/reduce_scatter | solution.py:150
  730.6 96.8 %reduce-scatter.11.cloned.1.call-done = f32[640,640]{1,0:T(8,128)} async-done(((f32[5120,640]{1,0:T(8,128)}), f32[640,640]{1,0:T(8,128)}) %reduce-scatter.11.cloned.1.call-update) | async-done | bytes 1638416 | tf_op jit(solution)/shard_map/reduce_scatter | solution.py:152
  829.9 24.6 %all-reduce.17 = (bf16[640]{0:T(1024)(128)(2,1)S(1)}, bf16[640]{0:T(1024)(128)(2,1)S(1)}, bf16[640]{0:T(1024)(128)(2,1)S(1)}, bf16[640]{0:T(1024)(128)(2,1)S(1)}...) all-reduce(f32[640]{0:T(1024)S(1)} %get-tuple-element.179, ...), channel_id=2, replica_groups=mesh['rep'=4,'fsdp'=8] {'fsdp'}, use_global_device_ids=true, to_apply=%region_16.17.clone | all-reduce | flops 10240 | bytes 61440
  855.1 13.3 %all-reduce.19 = (bf16[80]{0:T(256)(128)(2,1)S(1)}, bf16[80]{0:T(256)(128)(2,1)S(1)}, bf16[80]{0:T(256)(128)(2,1)S(1)}, bf16[80]{0:T(256)(128)(2,1)S(1)}, bf16[8...) all-reduce(bf16[80]{0:T(256)(128)(2,1)S(1)} %dynamic-slice.43, ...), channel_id=1, replica_groups=mesh['rep'=4,'fsdp'=8] {'rep'}, use_global_device_ids=true, to_apply=%region_17.18 | all-reduce | flops 1280 | bytes 5120 | tf_op jit(solution)/shard_map/psum | solution.py:230
  875.6 12.5 %fusion.73 = bf16[1,1024,640]{1,2,0:T(8,128)(2,1)} fusion(f32[1024,640]{0,1:T(8,128)S(1)} %copy-done.4, bf16[1024,5120]{1,0:T(8,128)(2,1)} %get-tuple-element.245, bf16[5120,640]{1,0:T(8,128)(2,1)} %all-gather.9.cloned.1.call-done, f32[640]{0:T(1024)S(1)} %convert_element_type.203), kind=kOutput, calls=%fused_computation.108 | convolution fusion | flops 6712852480 | bytes 20974080 | tf_op jit(solution)/shard_map/dot_general | solution.py:117
  890.5 27.8 %all-reduce.23.cloned.1.call-done = (bf16[80,1920]{1,0:T(8,128)(2,1)}, bf16[80,640]{1,0:T(8,128)(2,1)}, bf16[80,5120]{1,0:T(8,128)(2,1)}, bf16[640,640]{1,0:T(8,128)(2,1)}) async-done(((bf16[80,1920]{1,0:T(8,128)(2,1)}, bf16[80,640]{1,0:T(8,128)(2,1)}, bf16[80,5120]{1,0:T(8,128)(2,1)}, bf16[640,640]{1,0:T(8,128)(2,1)}), (bf16[80,1920]{1,0:T(8,128)(2,1)}, bf16[80,640]{1,0:T(8,128)(2,1)}, ...) | async-done | bytes 2048016 | tf_op jit(solution)/shard_map/psum | solution.py:232
  (446 shorter events, 429.6 us)
Async XLA Ops:
  7.2 38.0 %copy-start.12 = (bf16[1,1024,640]{2,1,0:T(8,128)(2,1)S(1)}, bf16[1,1024,640]{2,1,0:T(8,128)(2,1)}, u32[]{:S(2)}) copy-start(bf16[1,1024,640]{2,1,0:T(8,128)(2,1)} %param.20) | copy-start | bytes 3932164
  7.2 67.4 %all-gather.5.cloned.1.call-start = ((), (), s32[]{:S(2)}) async-start(), calls=%async_computation.4 | async-start | bytes 2764800 | tf_op jit(solution)/shard_map/all_gather | solution.py:57
  7.9 208.9 %all-gather.7.cloned.1.call-start = ((), (), s32[]{:S(2)}) async-start(), calls=%async_computation.5 | async-start | bytes 7372800 | tf_op jit(solution)/shard_map/all_gather | solution.py:102
  8.7 264.7 %all-gather.9.cloned.1.call-start = ((), (), s32[]{:S(2)}) async-start(), calls=%async_computation.6 | async-start | bytes 7372800 | tf_op jit(solution)/shard_map/all_gather | solution.py:104
  9.4 615.6 %reduce-scatter.7.cloned.1.call-start = ((), (), s32[]{:S(2)}) async-start(), calls=%async_computation.8 | async-start | bytes 1843200 | tf_op jit(solution)/shard_map/reduce_scatter | solution.py:226
  45.9 166.3 %copy-start = (bf16[1,1024,640]{1,2,0:T(8,128)(2,1)}, bf16[1,1024,640]{1,2,0:T(8,128)(2,1)S(1)}, u32[]{:S(2)}) copy-start(bf16[1,1024,640]{1,2,0:T(8,128)(2,1)S(1)} %copy.63) | copy-start | bytes 3932164
  59.2 153.0 %copy-start.18 = (bf16[640,640]{1,0:T(8,128)(2,1)}, bf16[640,640]{1,0:T(8,128)(2,1)S(1)}, u32[]{:S(2)}) copy-start(bf16[640,640]{1,0:T(8,128)(2,1)S(1)} %all_gather.50) | copy-start | bytes 2457604
  59.9 155.4 %copy-start.30 = (f32[640]{0:T(1024)}, f32[640]{0:T(1024)S(1)}, u32[]{:S(2)}) copy-start(f32[640]{0:T(1024)S(1)} %convert_element_type.198) | copy-start | bytes 7684
  60.6 154.7 %copy-start.41 = (f32[640]{0:T(1024)}, f32[640]{0:T(1024)S(1)}, u32[]{:S(2)}) copy-start(f32[640]{0:T(1024)S(1)} %convert_element_type.199) | copy-start | bytes 7684
  99.4 112.8 %copy-start.44 = (f32[640]{0:T(1024)S(1)}, f32[640]{0:T(1024)}, u32[]{:S(2)}) copy-start(f32[640]{0:T(1024)} %convert_element_type.197) | copy-start | bytes 7684
  215.3 58.1 %copy-start.39 = (f32[1024]{0:T(1024)}, f32[1024]{0:T(1024)S(1)}, u32[]{:S(2)}) copy-start(f32[1024]{0:T(1024)S(1)} %multiply_reduce_fusion.4) | copy-start | bytes 12292
  216.4 57.0 %copy-start.32 = (f32[1024]{0:T(1024)}, f32[1024]{0:T(1024)S(1)}, u32[]{:S(2)}) copy-start(f32[1024]{0:T(1024)S(1)} %fusion.80) | copy-start | bytes 12292
  216.8 56.6 %copy-start.9 = (bf16[1,1024,640]{1,2,0:T(8,128)(2,1)S(1)}, bf16[1,1024,640]{1,2,0:T(8,128)(2,1)}, u32[]{:S(2)}) copy-start(bf16[1,1024,640]{1,2,0:T(8,128)(2,1)} %copy.71) | copy-start | bytes 3932164
  216.8 56.6 %copy-start.34 = (f32[1,1024]{1,0:T(1,128)S(1)}, f32[1,1024]{1,0:T(1,128)}, u32[]{:S(2)}) copy-start(f32[1,1024]{1,0:T(1,128)} %convert_element_type.207) | copy-start | bytes 12292
  324.7 304.4 %reduce-scatter.5.cloned.1.call-start = ((), (), s32[]{:S(2)}) async-start(), calls=%async_computation.7 | async-start | bytes 5529600 | tf_op jit(solution)/shard_map/reduce_scatter | solution.py:223
  330.1 236.1 %copy-start.1 = (bf16[1,1024,640]{1,2,0:T(8,128)(2,1)S(1)}, bf16[1,1024,640]{1,2,0:T(8,128)(2,1)}, u32[]{:S(2)}) copy-start(bf16[1,1024,640]{1,2,0:T(8,128)(2,1)} %copy-done) | copy-start | bytes 3932164
  330.2 236.1 %copy-start.23 = (f32[1024]{0:T(1024)S(1)}, f32[1024]{0:T(1024)}, u32[]{:S(2)}) copy-start(f32[1024]{0:T(1024)} %copy-done.22) | copy-start | bytes 12292
  330.2 236.1 %copy-start.29 = (f32[640]{0:T(1024)S(1)}, f32[640]{0:T(1024)}, u32[]{:S(2)}) copy-start(f32[640]{0:T(1024)} %copy-done.28) | copy-start | bytes 7684
  330.2 236.1 %copy-start.36 = (f32[1024]{0:T(1024)S(1)}, f32[1024]{0:T(1024)}, u32[]{:S(2)}) copy-start(f32[1024]{0:T(1024)} %copy-done.35) | copy-start | bytes 12292
  330.2 236.1 %copy-start.43 = (f32[640]{0:T(1024)S(1)}, f32[640]{0:T(1024)}, u32[]{:S(2)}) copy-start(f32[640]{0:T(1024)} %convert_element_type.193) | copy-start | bytes 7684
  573.8 154.4 %reduce-scatter.9.cloned.1.call-start = ((), (), s32[]{:S(2)}) async-start(), calls=%async_computation.9 | async-start | bytes 14745600 | tf_op jit(solution)/shard_map/reduce_scatter | solution.py:150
  588.2 239.2 %reduce-scatter.11.cloned.1.call-start = ((), (), s32[]{:S(2)}) async-start(), calls=%async_computation.10 | async-start | bytes 14745600 | tf_op jit(solution)/shard_map/reduce_scatter | solution.py:152
  603.5 314.8 %all-reduce.23.cloned.1.call-start = ((), (), s32[]{:S(2)}) async-start(), calls=%async_computation.11 | async-start | bytes 4096000 | tf_op jit(solution)/shard_map/psum | solution.py:232
  829.8 45.7 %copy-start.4 = (f32[1024,640]{0,1:T(8,128)S(1)}, f32[1024,640]{0,1:T(8,128)}, u32[]{:S(2)}) copy-start(f32[1024,640]{0,1:T(8,128)} %copy-done.2) | copy-start | bytes 7864324
  (31 other events, 217.7 us)
Sparse Core Ops, SparseCore 0:
  9.9 32.2 all-gather.4
  44.1 47.8 all-gather.6
  94.0 46.6 all-gather.8
  324.9 39.1 reduce-scatter.6
  573.9 55.1 reduce-scatter.4
  633.0 95.1 reduce-scatter.8
  732.2 95.1 reduce-scatter.10
  831.4 86.8 all-reduce.22
where the time goes:
time: 940 us; the launch traced here: 931 us
  matrix products  447 us (48%)
  waiting for transfers between devices  227 us (24%)
  blocking collectives  85.6 us (9%)
  local copies, waits for them, and re-layouts  78.9 us (8%)
  other arithmetic  74.4 us (8%)
  between operations  16.9 us (2%)
    reduce_scatter x1, waiting for transfers between devices, local(): lax.psum_scatter(grad_w_up, 'fsdp', scatter_dimension=0, tiled=True)  97.3 us
    reduce_scatter x1, waiting for transfers between devices, local(): lax.psum_scatter(grad_w_down, 'fsdp', scatter_dimension=0, tiled=True)  96.8 us
    dot_general x1, matrix products, local(): jnp.dot(normed2, weight_up, preferred_element_type=single_float32)  56.5 us
    unnamed x2, blocking collectives  51 us
    dot_general x20, matrix products, head_forward(): jnp.einsum('fbn,fna->fba', attention_probs, value_rows, preferred_element...  50.8 us
    dot_general x20, matrix products, head_backward(): jnp.einsum('cpg,cpi->cgi', attention_probs, gradient_per_head, preferred_...  48.2 us
    dot_general x20, matrix products, head_backward(): jnp.einsum('cpg,cpi->cgi', gradient_logits, query_rows, preferred_element...  46.1 us
    dot_general x20, matrix products, head_backward(): jnp.einsum('fep,fwp->few', gradient_per_head, value_rows, preferred_eleme...  40 us
  transfers between devices with their start and end apart: 8, of which 4 were waited for; matrix products, arithmetic and copies ran while one was open for 58% of the time, Pallas kernels for 0%

commit v1 on v0

v1 whole, which is shorter than its diff:
```python
import functools

import jax
import jax.numpy as jnp
from jax import lax
from jax.experimental import pallas as pl
from jax.experimental.pallas import tpu as pltpu
from jax.sharding import PartitionSpec as P

HEADS = 20
HEAD_DIM = 32
GROUP = 4
LANES = 128
SCALE = HEAD_DIM ** (-0.5)
LOG2E = 1.4426950408889634
FEW = 384
F32 = jnp.float32
BF16 = jnp.bfloat16
MB = 1024 * 1024

NN = (((1,), (0,)), ((), ()))
NT = (((1,), (1,)), ((), ()))


def dot(a, b, dims=NN):
    return lax.dot_general(a, b, dims, preferred_element_type=F32)


def norm_stats(x):
    mean = jnp.mean(x, axis=-1, keepdims=True)
    centred = x - mean
    variance = jnp.mean(centred * centred, axis=-1, keepdims=True)
    rstd = lax.rsqrt(variance + 1e-05)
    return centred * rstd, rstd


def norm_back(grad, xhat, rstd, gain):
    dxhat = grad * gain
    first = jnp.mean(dxhat, axis=-1, keepdims=True)
    second = jnp.mean(dxhat * xhat, axis=-1, keepdims=True)
    return rstd * (dxhat - first - xhat * second)


def cdf_parts(u):
    z = jnp.abs(u)
    t = 1.0 / (1.0 + 0.23164189 * z)
    e = jnp.exp2(u * u * (-0.5 * LOG2E))
    poly = t * (
        0.127414796 + t * (-0.142248368 + t * (0.7107068705 + t * (-0.7265760135 + t * 0.5307027145)))
    )
    tail = poly * e
    return jnp.where(u < 0, tail, 1.0 - tail), e


def one_hot_rows(slot, start, size):
    length = slot.shape[1]
    rows = lax.broadcasted_iota(jnp.int32, (size, length), 0).astype(F32) + start
    return jnp.where(rows == slot, 1.0, 0.0)


def unpermute(slot, src_ref, out_ref):
    length = slot.shape[1]
    wide = jnp.transpose(jnp.broadcast_to(slot, (LANES, length)))
    step = 256
    for start in range(0, length, step):
        col = wide[start : start + step, :1]
        cols = lax.broadcasted_iota(jnp.int32, (step, length), 1).astype(F32)
        pick = jnp.where(cols == col, 1.0, 0.0).astype(BF16)
        out_ref[start : start + step, :] = dot(pick, src_ref[...]).astype(BF16)


def attn_kernel(
    tokens_ref, mask_ref, vec_ref, wqkv_ref, wout_ref,
    slot_ref, xp_ref, h1_ref, qkv_ref, o_ref, lse_ref, x1_ref,
):
    length, width = tokens_ref.shape
    step = 256
    mask8 = jnp.broadcast_to(mask_ref[...], (8, length))
    cum = []
    for start in range(0, length, step):
        up = lax.broadcasted_iota(jnp.int32, (length, step), 0)
        to = lax.broadcasted_iota(jnp.int32, (length, step), 1) + start
        cum.append(dot(mask8.astype(BF16), jnp.where(up <= to, 1.0, 0.0).astype(BF16)))
    cum = jnp.concatenate(cum, axis=1)
    count = jnp.sum(mask8, axis=1, keepdims=True)
    pos = lax.broadcasted_iota(jnp.int32, (8, length), 1).astype(F32)
    slot = jnp.where(mask8 > 0.5, cum - 1.0, count + pos - cum)
    slot_ref[...] = slot
    gain = vec_ref[0:1, :]
    shift = vec_ref[1:2, :]
    bq = vec_ref[2:3, :]
    bv = vec_ref[3:4, :]
    bout = vec_ref[4:5, :]

    def project(i, _):
        rows = pl.ds(pl.multiple_of(i * step, step), step)
        pick = one_hot_rows(slot[:1], (i * step).astype(F32), step).astype(BF16)
        x = dot(pick, tokens_ref[...])
        xp_ref[rows, :] = x.astype(BF16)
        xhat, _ = norm_stats(x)
        h1 = (xhat * gain + shift).astype(BF16)
        h1_ref[rows, :] = h1
        qkv_ref[rows, :width] = (dot(h1, wqkv_ref[:, :width]) + bq).astype(BF16)
        qkv_ref[rows, width : 2 * width] = dot(h1, wqkv_ref[:, width : 2 * width]).astype(BF16)
        qkv_ref[rows, 2 * width :] = (dot(h1, wqkv_ref[:, 2 * width :]) + bv).astype(BF16)
        return 0

    lax.fori_loop(0, length // step, project, 0)

    c = SCALE * LOG2E
    lane = lax.broadcasted_iota(jnp.int32, (step, LANES), 1)

    def attend(n, _):
        t = n // (length // step)
        i = n % (length // step)
        rows = pl.ds(pl.multiple_of(i * step, step), step)
        q = qkv_ref[rows, pl.ds(pl.multiple_of(t * LANES, LANES), LANES)]
        k = qkv_ref[:, pl.ds(pl.multiple_of(width + t * LANES, LANES), LANES)]
        v = qkv_ref[:, pl.ds(pl.multiple_of(2 * width + t * LANES, LANES), LANES)]
        vo = jnp.concatenate([v, jnp.ones_like(v)], axis=1)
        out = jnp.zeros((step, LANES), F32)
        lses = jnp.zeros((step, LANES), F32)
        for h in range(GROUP):
            mine = lane // HEAD_DIM == h
            s = dot(jnp.where(mine, q, jnp.zeros_like(q)), k, NT)
            top = jnp.max(s, axis=-1, keepdims=True)
            p = jnp.exp2((s - top) * c).astype(BF16)
            ov = dot(p, vo)
            total = ov[:, LANES:]
            out = jnp.where(mine, ov[:, :LANES] / total, out)
            lses = jnp.where(lane == h, top * c + jnp.log2(total), lses)
        o_ref[rows, pl.ds(pl.multiple_of(t * LANES, LANES), LANES)] = out.astype(BF16)
        lse_ref[pl.ds(pl.multiple_of(t * 8, 8), 8), rows] = jnp.transpose(lses)[:8, :]
        return 0

    lax.fori_loop(0, (width // LANES) * (length // step), attend, 0)

    def join(i, _):
        rows = pl.ds(pl.multiple_of(i * step, step), step)
        x1_ref[rows, :] = xp_ref[rows, :].astype(F32) + dot(o_ref[rows, :], wout_ref[...]) + bout
        return 0

    lax.fori_loop(0, length // step, join, 0)


def attn_forward(tokens, mask, vecs, wqkv, wout):
    length, width = tokens.shape
    sds = jax.ShapeDtypeStruct
    groups = width // LANES
    return pl.pallas_call(
        attn_kernel,
        out_shape=(
            sds((8, length), F32),
            sds((length, width), BF16),
            sds((length, width), BF16),
            sds((length, 3 * width), BF16),
            sds((length, width), BF16),
            sds((8 * groups, length), F32),
            sds((length, width), F32),
        ),
        compiler_params=pltpu.CompilerParams(vmem_limit_bytes=56 * MB),
        name="attn_forward",
    )(tokens, mask, vecs, wqkv, wout)


def ffn_kernel(
    few,
    x1_ref, cot_ref, slot_ref, mask_ref, vec_ref, bup_ref, wup_ref, wdn_ref, wout_ref, o_ref,
    res_ref, gup_ref, gdn_ref, gbup_ref, g1_ref, do_ref, gout_ref, small_ref,
    acc, h2, h2t, gy, gyt, dh2, outp,
):
    j = pl.program_id(0)
    last = pl.num_programs(0) - 1
    length, width = x1_ref.shape
    gain = vec_ref[5:6, :]
    shift = vec_ref[6:7, :]
    bdown = vec_ref[7:8, :]
    blocks = []
    start = 0
    part = few if few <= 384 else 256
    while start < few:
        blocks.append((start, part, True))
        start += part
    while start < length:
        size = min(320, length - start)
        blocks.append((start, size, False))
        start += size

    @pl.when(j == 0)
    def _():
        for start, size, back in blocks:
            rows = slice(start, start + size)
            x1 = x1_ref[rows, :]
            xhat, _ = norm_stats(x1)
            hidden = (xhat * gain + shift).astype(BF16)
            h2[rows, :] = hidden
            acc[rows, :] = x1 + bdown
            if back:
                h2t[:, rows] = jnp.transpose(hidden)
                pick = one_hot_rows(slot_ref[0:1, :], float(start), size) * mask_ref[...]
                g = dot(pick.astype(BF16), cot_ref[...])
                gy[rows, :] = g.astype(BF16)
                gyt[:, rows] = jnp.transpose(g.astype(BF16))
                dh2[rows, :] = jnp.zeros((size, width), F32)

    gup = gdn = gbup = None
    for start, size, back in blocks:
        rows = slice(start, start + size)
        u = dot(h2[rows, :], wup_ref[...]) + bup_ref[...]
        cdf, e = cdf_parts(u)
        a = (u * cdf).astype(BF16)
        acc[rows, :] += dot(a, wdn_ref[...])
        if back:
            da = dot(gy[rows, :], wdn_ref[...], NT)
            du = ((cdf + u * e * 0.3989422804014327) * da).astype(BF16)
            p_up = dot(h2t[:, rows], du)
            p_dn = dot(gyt[:, rows], a)
            p_b = jnp.sum(du.astype(F32), axis=0, keepdims=True)
            gup = p_up if gup is None else gup + p_up
            gdn = p_dn if gdn is None else gdn + p_dn
            gbup = p_b if gbup is None else gbup + p_b
            dh2[rows, :] += dot(du, wup_ref[...], NT)
    gup_ref[...] = gup.astype(BF16)
    gdn_ref[...] = gdn.astype(BF16)
    gbup_ref[...] = gbup

    @pl.when(j == last)
    def _():
        ggain = gshift = gbdown = gbout = gout = jnp.zeros((1, 1), F32)
        for start, size, back in blocks:
            rows = slice(start, start + size)
            outp[rows, :] = acc[rows, :].astype(BF16)
            if back:
                xhat, rstd = norm_stats(x1_ref[rows, :])
                d = dh2[rows, :]
                g = gy[rows, :].astype(F32)
                g1 = g + norm_back(d, xhat, rstd, gain)
                g1_ref[rows, :] = g1
                g1b = g1.astype(BF16)
                do_ref[rows, :] = dot(g1b, wout_ref[...], NT).astype(BF16)
                gout = gout + dot(jnp.transpose(o_ref[rows, :]), g1b)
                ggain = ggain + jnp.sum(d * xhat, axis=0, keepdims=True)
                gshift = gshift + jnp.sum(d, axis=0, keepdims=True)
                gbdown = gbdown + jnp.sum(g, axis=0, keepdims=True)
                gbout = gbout + jnp.sum(g1b.astype(F32), axis=0, keepdims=True)
        gout_ref[...] = gout.astype(BF16)
        small_ref[0:1, :] = gbout
        small_ref[1:2, :] = ggain
        small_ref[2:3, :] = gshift
        small_ref[3:4, :] = gbdown
        small_ref[4:8, :] = jnp.zeros((4, width), F32)
        unpermute(slot_ref[0:1, :], outp, res_ref)


def feed_forward(few, x1, cot, slot, mask, vecs, bup, wup, wdn, wout, o):
    length, width = x1.shape
    hidden = wup.shape[1]
    fc = 512
    sds = jax.ShapeDtypeStruct
    whole = lambda *shape: pl.BlockSpec(shape, lambda j: (0,) * len(shape))
    return pl.pallas_call(
        functools.partial(ffn_kernel, few),
        grid=(hidden // fc,),
        in_specs=[
            whole(length, width),
            whole(length, width),
            whole(8, length),
            whole(1, length),
            whole(8, width),
            pl.BlockSpec((1, fc), lambda j: (0, j)),
            pl.BlockSpec((width, fc), lambda j: (0, j)),
            pl.BlockSpec((fc, width), lambda j: (j, 0)),
            whole(width, width),
            whole(few, width),
        ],
        out_specs=[
            whole(length, width),
            pl.BlockSpec((width, fc), lambda j: (0, j)),
            pl.BlockSpec((width, fc), lambda j: (0, j)),
            pl.BlockSpec((1, fc), lambda j: (0, j)),
            whole(few, width),
            whole(few, width),
            whole(width, width),
            whole(8, width),
        ],
        out_shape=(
            sds((length, width), BF16),
            sds((width, hidden), BF16),
            sds((width, hidden), BF16),
            sds((1, hidden), F32),
            sds((few, width), F32),
            sds((few, width), BF16),
            sds((width, width), BF16),
            sds((8, width), F32),
        ),
        scratch_shapes=[
            pltpu.VMEM((length, width), F32),
            pltpu.VMEM((length, width), BF16),
            pltpu.VMEM((width, few), BF16),
            pltpu.VMEM((few, width), BF16),
            pltpu.VMEM((width, few), BF16),
            pltpu.VMEM((few, width), F32),
            pltpu.VMEM((length, width), BF16),
        ],
        compiler_params=pltpu.CompilerParams(vmem_limit_bytes=56 * MB),
        name="feed_forward",
    )(x1, cot, slot, mask, vecs, bup, wup, wdn, wout, o)


def back_kernel(
    few,
    q_ref, k_ref, v_ref, do_ref, o_ref, lse_ref, h1_ref, xp_ref, vec_ref,
    wq_ref, wk_ref, wv_ref, g1_ref, slot_ref,
    gtok_ref, gq_ref, gk_ref, gv_ref, small_ref,
    h1t, dh1, dqt, dkv, gtp,
):
    t = pl.program_id(0)
    last = pl.num_programs(0) - 1
    length, width = h1_ref.shape
    groups = width // LANES
    step = 256
    c = SCALE * LOG2E
    gain = vec_ref[0:1, :]

    @pl.when(t == 0)
    def _():
        for start in range(0, length, step):
            h1t[:, start : start + step] = jnp.transpose(h1_ref[start : start + step, :])
        dh1[...] = jnp.zeros_like(dh1)

    q = q_ref[...]
    do = do_ref[...]
    lane = lax.broadcasted_iota(jnp.int32, (few, LANES), 1)
    head = lax.broadcasted_iota(jnp.int32, (8, LANES), 0)
    lane8 = lax.broadcasted_iota(jnp.int32, (8, LANES), 1)
    pick = jnp.where(lane8 // HEAD_DIM == head, 1.0, 0.0)
    delta = lax.dot_general(
        pick, do.astype(F32) * o_ref[...].astype(F32), NT,
        precision=lax.Precision.HIGHEST, preferred_element_type=F32,
    )
    dqt[...] = jnp.zeros_like(dqt)
    zero = jnp.zeros_like(q)
    qs = [jnp.where(lane // HEAD_DIM == h, q, zero) for h in range(GROUP)]
    dos = [jnp.where(lane // HEAD_DIM == h, do, zero) for h in range(GROUP)]

    def keys(i, _):
        rows = pl.ds(pl.multiple_of(i * step, step), step)
        k = k_ref[rows, :]
        v = v_ref[rows, :]
        kt = jnp.transpose(k)
        dk = jnp.zeros((step, LANES), F32)
        dv = jnp.zeros((step, LANES), F32)
        for h in range(GROUP):
            s = dot(k, qs[h], NT)
            p = jnp.exp2(s * c - lse_ref[h : h + 1, :])
            dp = dot(v, dos[h], NT)
            ds = (p * (dp - delta[h : h + 1, :])).astype(BF16)
            dv = dv + dot(p.astype(BF16), dos[h])
            dk = dk + dot(ds, qs[h])
            part = slice(h * HEAD_DIM, (h + 1) * HEAD_DIM)
            dqt[part, :] += dot(kt[part, :], ds)
        dkv[rows, :LANES] = (dk * SCALE).astype(BF16)
        dkv[rows, LANES:] = dv.astype(BF16)
        return 0

    lax.fori_loop(0, length // step, keys, 0)
    dq = (jnp.transpose(dqt[...]) * SCALE).astype(BF16)
    gq_ref[...] = dot(h1t[:, :few], dq).astype(BF16)
    gkv = dot(h1t[...], dkv[...]).astype(BF16)
    gk_ref[...] = gkv[:, :LANES]
    gv_ref[...] = gkv[:, LANES:]
    small_ref[0:1, :] = jnp.zeros((1, LANES), F32)
    small_ref[2:3, :] = jnp.sum(dq.astype(F32), axis=0, keepdims=True)
    small_ref[3:4, :] = jnp.sum(dkv[:, LANES:].astype(F32), axis=0, keepdims=True)
    wkv = jnp.concatenate([wk_ref[...], wv_ref[...]], axis=1)
    for start in range(0, length, step):
        rows = slice(start, start + step)
        dh1[rows, :] += dot(dkv[rows, :], wkv, NT)
    dh1[:few, :] += dot(dq, wq_ref[...], NT)


def back_finish(
    few,
    dh1_ref, xp_ref, vec_ref, g1_ref, slot_ref, gtok_ref, small_ref, gtp,
):
    length, width = xp_ref.shape
    gain = vec_ref[0:1, :]
    step = 128
    ggain = gshift = jnp.zeros((1, width), F32)
    for start in range(0, length, step):
        rows = slice(start, start + step)
        xhat, rstd = norm_stats(xp_ref[rows, :].astype(F32))
        d = dh1_ref[rows, :]
        g = norm_back(d, xhat, rstd, gain)
        if start < few:
            g = g + g1_ref[rows, :]
        gtp[rows, :] = g.astype(BF16)
        ggain = ggain + jnp.sum(d * xhat, axis=0, keepdims=True)
        gshift = gshift + jnp.sum(d, axis=0, keepdims=True)
    small_ref[0:1, :] = ggain
    small_ref[1:2, :] = gshift
    unpermute(slot_ref[0:1, :], gtp, gtok_ref)


def back_all(few, *refs):
    (q, k, v, do, o, lse, h1, xp, vec, wq, wk, wv, g1, slot,
     gtok, gq, gk, gv, small, norms, h1t, dh1, dqt, dkv, gtp) = refs
    back_kernel(few, q, k, v, do, o, lse, h1, xp, vec, wq, wk, wv, g1, slot,
                gtok, gq, gk, gv, small, h1t, dh1, dqt, dkv, gtp)

    @pl.when(pl.program_id(0) == pl.num_programs(0) - 1)
    def _():
        norms[...] = jnp.zeros_like(norms)
        back_finish(few, dh1, xp, vec, g1, slot, gtok, norms, gtp)


def attn_backward(few, qkv, do, o, lse, h1, xp, vecs, wqkv, g1, slot):
    length, width = h1.shape
    groups = width // LANES
    sds = jax.ShapeDtypeStruct
    whole = lambda *shape: pl.BlockSpec(shape, lambda t: (0,) * len(shape))
    cols = lambda rows, first: pl.BlockSpec((rows, LANES), lambda t: (0, first + t))
    return pl.pallas_call(
        functools.partial(back_all, few),
        grid=(groups,),
        in_specs=[
            cols(few, 0),
            cols(length, groups),
            cols(length, 2 * groups),
            cols(few, 0),
            cols(few, 0),
            pl.BlockSpec((8, few), lambda t: (t, 0)),
            whole(length, width),
            whole(length, width),
            whole(8, width),
            cols(width, 0),
            cols(width, groups),
            cols(width, 2 * groups),
            whole(few, width),
            whole(8, length),
        ],
        out_specs=[
            whole(length, width),
            cols(width, 0),
            cols(width, 0),
            cols(width, 0),
            cols(8, 0),
            whole(8, width),
        ],
        out_shape=(
            sds((length, width), BF16),
            sds((width, width), BF16),
            sds((width, width), BF16),
            sds((width, width), BF16),
            sds((8, width), F32),
            sds((8, width), F32),
        ),
        scratch_shapes=[
            pltpu.VMEM((width, length), BF16),
            pltpu.VMEM((length, width), F32),
            pltpu.VMEM((LANES, few), F32),
            pltpu.VMEM((length, 2 * LANES), BF16),
            pltpu.VMEM((length, width), BF16),
        ],
        compiler_params=pltpu.CompilerParams(vmem_limit_bytes=56 * MB),
        name="attn_backward",
    )(qkv, qkv, qkv, do, o, lse, h1, xp, vecs, wqkv, wqkv, wqkv, g1, slot)


def local(
    tokens, masked, cotangent, norm1_gain, norm1_shift, w_qkv, bias_query, bias_value, w_out,
    bias_out, norm2_gain, norm2_shift, w_up, bias_up, w_down, bias_down,
):
    seqs, length, width = tokens.shape
    hidden = w_up.shape[1]
    share = w_qkv.shape[0]
    x = tokens.reshape(seqs * length, width)
    cot = cotangent.reshape(seqs * length, width)
    mask = masked.astype(F32)
    most = lax.pmax(jnp.sum(masked), ("rep", "fsdp"))
    packed = jnp.stack(
        [norm1_gain, norm1_shift, bias_query, bias_value, bias_out, norm2_gain, norm2_shift, bias_down]
    )
    vecs = lax.all_gather(packed, "fsdp", axis=1, tiled=True).astype(F32)
    bup = lax.all_gather(bias_up, "fsdp", axis=0, tiled=True).astype(F32).reshape(1, hidden)
    gather = lambda w: lax.all_gather(w, "fsdp", axis=0, tiled=True)
    wqkv, wout, wup, wdn = gather(w_qkv), gather(w_out), gather(w_up), gather(w_down)

    slot, xp, h1, qkv, o, lse, x1 = attn_forward(x, mask, vecs, wqkv, wout)

    def backward(few):
        def run():
            res, gup, gdn, gbup, g1, do, gout, small2 = feed_forward(
                few, x1, cot, slot, mask, vecs, bup, wup, wdn, wout, o
            )
            gtok, gq, gk, gv, small1, norms = attn_backward(
                few, qkv, do, o, lse, h1, xp, vecs, wqkv, g1, slot
            )
            small = jnp.concatenate(
                [norms[:2], small1[2:4], small2[:4], gbup.reshape(8, width)], axis=0
            )
            return res, gtok, gup, gdn, gout, gq, gk, gv, small

        return run

    res, gtok, gup, gdn, gout, gq, gk, gv, small = lax.cond(
        most <= FEW, backward(FEW), backward(length)
    )

    def scatter(g, dim):
        part = lax.psum_scatter(g, "fsdp", scatter_dimension=dim, tiled=True)
        return lax.psum(part, "rep").astype(F32)

    gup = scatter(gup, 0)
    gdn = jnp.transpose(scatter(gdn, 1))
    gattn = scatter(jnp.concatenate([gout, gq, gk, gv], axis=1), 0)
    gout, gqkv = gattn[:, :width], gattn[:, width:]
    small = lax.psum(small, ("rep", "fsdp"))
    me = lax.axis_index("fsdp")
    mine = lax.dynamic_slice_in_dim(small[:8], me * share, share, axis=1)
    gbup = lax.dynamic_slice_in_dim(small[8:].reshape(hidden), me * bias_up.shape[0], bias_up.shape[0])
    return (
        res.reshape(seqs, length, width),
        gtok.reshape(seqs, length, width),
        mine[0], mine[1], gqkv, mine[2], mine[3], gout, mine[4], mine[5], mine[6],
        gup, gbup, gdn, mine[7],
    )


def solution(mesh):
    rows3 = P(("rep", "fsdp"), None, None)
    vec = P("fsdp")
    mat = P("fsdp", None)
    in_specs = (
        rows3, P(("rep", "fsdp"), None), rows3,
        vec, vec, mat, vec, vec, mat, vec, vec, vec, mat, vec, mat, vec,
    )
    out_specs = (rows3, rows3, vec, vec, mat, vec, vec, mat, vec, vec, vec, mat, vec, mat, vec)
    return jax.shard_map(local, mesh=mesh, in_specs=in_specs, out_specs=out_specs, check_vma=False)
```

time: 940 us -> 545 us (0.58)
  matrix products: 447 us -> 0 us
  Pallas kernels: 0 us -> 151 us
  other arithmetic: 74.4 us -> 8.98 us
  local copies, waits for them, and re-layouts: 78.9 us -> 18 us
  blocking collectives: 85.6 us -> 118 us
    dot_general x152 -> x0, matrix products: 447 us -> none  [the longest x1 56.5 us: local(): jnp.dot(normed2, weight_up, preferred_element_type=single_float32)]
    pallas_call x0 -> x3, Pallas kernels: none -> 151 us  [the longest x1 55 us: feed_forward(): pl.pallas_call(functools.partial(ffn_kernel, few), grid=(hidden // fc,),...]
    unnamed x2 -> x0, blocking collectives: 51 us -> none
    convert_element_type x47 -> x2, other arithmetic: 46.7 us -> 3.84 us  [the longest x1 2.43 us: scatter(): return lax.psum(part, 'rep').astype(F32)]
    pmax x0 -> x1, blocking collectives: none -> 42.2 us  [local(): most = lax.pmax(jnp.sum(masked), ('rep', 'fsdp'))]
    psum x1, blocking collectives: 13.3 us -> 42.8 us  [local(): small = lax.psum(small, ('rep', 'fsdp'))]
    reduce_scatter x4 -> x3, waiting for transfers between devices: 197 us -> 170 us  [scatter(): part = lax.psum_scatter(g, 'fsdp', scatter_dimension=dim, tiled=True)]
    reduce_sum x29 -> x0, other arithmetic: 25 us -> none  [the longest x20 14.7 us: head_forward(): total = jnp.sum(expo, axis=-1, keepdims=True)]
  transfers between devices with their start and end apart: 8 -> 7, of which waited for: 4 -> 5; matrix products, arithmetic and copies ran while one was open for 58% -> 3% of each run, Pallas kernels for 0% -> 10%
where the time goes in v1:
time: 545 us; the launch traced here: 539 us
  waiting for transfers between devices  220 us (40%)
  Pallas kernels  151 us (28%)
  blocking collectives  118 us (22%)
  local copies, waits for them, and re-layouts  18 us (3%)
  between operations  15.1 us (3%)
  other arithmetic  8.98 us (2%)
  loops' own time  6.9 us (1%)
    reduce_scatter x3, waiting for transfers between devices, scatter(): part = lax.psum_scatter(g, 'fsdp', scatter_dimension=dim, tiled=True)  170 us
    pallas_call x1, Pallas kernels, feed_forward(): pl.pallas_call(functools.partial(ffn_kernel, few), grid=(hidden // fc,),...  55 us
    pallas_call x1, Pallas kernels, attn_forward(): pl.pallas_call(attn_kernel, out_shape=(sds((8, length), F32), sds((length...  51.9 us
    psum x1, waiting for transfers between devices, scatter(): return lax.psum(part, 'rep').astype(F32)  45.5 us
    pallas_call x1, Pallas kernels, attn_backward(): pl.pallas_call(functools.partial(back_all, few), grid=(groups,), in_specs...  44.5 us
    psum x1, blocking collectives, local(): small = lax.psum(small, ('rep', 'fsdp'))  42.8 us
    pmax x1, blocking collectives, local(): most = lax.pmax(jnp.sum(masked), ('rep', 'fsdp'))  42.2 us
    all_gather x1, blocking collectives, local(): gather = lambda w: lax.all_gather(w, 'fsdp', axis=0, tiled=True)  14.9 us
  transfers between devices with their start and end apart: 7, of which 5 were waited for; matrix products, arithmetic and copies ran while one was open for 3% of the time, Pallas kernels for 10%

profile of v1, /device:TPU:0, one launch (start us, length us, event | category | flops | bytes accessed | tf_op | source)
XLA Modules:
  0.0 538.9 jit_solution(18038585812571523917)
XLA Ops:
  9.4 1.4 fusion.1
  10.8 42.2 %pmax.7 = s32[]{:T(128)} all-reduce(s32[]{:T(128)} %get-tuple-element.179), channel_id=1, replica_groups=mesh['rep'=4,'fsdp'=8] {'rep','fsdp'}, use_global_device_ids=true, to_apply=%region_1.0 | all-reduce | flops 1 | bytes 8 | tf_op jit(solution)/shard_map/pmax | solution.py:480
  53.0 0.8 stack.35
  53.8 9.9 %all-gather = bf16[8,80,8]{1,2,0:T(8,128)(2,1)S(1)} all-gather(bf16[1,80,8]{1,2,0:T(8,128)(2,1)S(1)} %bitcast.45), channel_id=1, replica_groups=mesh['rep'=4,'fsdp'=8] {'fsdp'}, dimensions={0}, use_global_device_ids=true | all-gather | bytes 11520 | tf_op jit(solution)/shard_map/all_gather | solution.py:484
  64.5 8.1 %all-gather.1 = bf16[8,1,640]{2,1,0:T(2,128)(2,1)S(1)} all-gather(bf16[1,1,640]{2,1,0:T(2,128)(2,1)S(1)} %reshape.68), channel_id=1, replica_groups=mesh['rep'=4,'fsdp'=8] {'fsdp'}, dimensions={0}, use_global_device_ids=true | all-gather | bytes 11520 | tf_op jit(solution)/shard_map/all_gather | solution.py:485
  73.3 14.9 %all_gather.20.wout_ref = bf16[640,640]{1,0:T(8,128)(2,1)S(1)} all-gather(bf16[80,640]{1,0:T(8,128)(2,1)} %param.26), channel_id=1, replica_groups=mesh['rep'=4,'fsdp'=8] {'fsdp'}, dimensions={0}, use_global_device_ids=true | all-gather | bytes 921600 | tf_op jit(solution)/shard_map/all_gather | solution.py:486
  88.2 51.9 %attn_forward.1 = (f32[8,1024]{1,0:T(8,128)S(1)}, bf16[1024,640]{1,0:T(8,128)(2,1)}, bf16[1024,640]{1,0:T(8,128)(2,1)}, bf16[1024,1920]{1,0:T(8,128)(2,1)}, bf16...) custom-call(bf16[1024,640]{1,0:T(8,128)(2,1)} %bitcast.39, ...), custom_call_target="tpu_custom_call" | custom-call | tf_op jit(solution)/shard_map/attn_forward/pallas_call | solution.py:150
  140.0 2.6 all-gather.8.cloned.1.call-done
  142.7 109.1 %conditional.1 = (bf16[1024,640]{1,0:T(8,128)(2,1)}, bf16[1024,640]{1,0:T(8,128)(2,1)}, bf16[640,5120]{1,0:T(8,128)(2,1)}, bf16[640,5120]{1,0:T(8,128)(2,1)}, bf...) conditional(s32[]{:T(128)} %convert_element_type.17, ...), branch_computations={%region_2.0_spmd, %region_3.0_spmd} | conditional | flops 30720 | bytes 16097448 | solution.py:506
  149.2 55.0 %feed_forward.3 = (bf16[1024,640]{1,0:T(8,128)(2,1)}, bf16[640,5120]{1,0:T(8,128)(2,1)}, bf16[640,5120]{1,0:T(8,128)(2,1)}, f32[1,5120]{1,0:T(1,128)}, f32[384,6...) custom-call(f32[1024,640]{1,0:T(8,128)} %get-tuple-element.89.x1_ref, ...), custom_call_target="tpu_custom_call" | custom-call | tf_op jit(solution)/shard_map/cond/branch_1_fun/feed_forward/pallas_call | solution.py:261
  204.3 44.5 %attn_backward.3 = (bf16[1024,640]{1,0:T(8,128)(2,1)}, bf16[640,640]{1,0:T(8,128)(2,1)S(1)}, bf16[640,640]{1,0:T(8,128)(2,1)}, bf16[640,640]{1,0:T(8,128)(2,1)}, f32[8,640]{1,0:T(8,128)}, /*index=5*/f32[8,640]{1,0:T(8,128)}) custom-call(bf16[1024,1920]{1,0:T(8,128)(2,1)S(1)} %copy-done.1, bf16[1024,1920]{1,0:T(8,128)(2,1)S(1)} %copy-done.1, ...), custom_call_target="tpu_custom_call" | custom-call | tf_op jit(solution)/shard_map/cond/branch_1_fun/attn_backward/pallas_call | solution.py:423
  248.8 0.7 slice.39
  249.5 0.7 slice.40
  251.8 3.1 pad_maximum_fusion.2
  255.0 9.6 %copy.34 = bf16[640,5120]{0,1:T(8,128)(2,1)} copy(bf16[640,5120]{1,0:T(8,128)(2,1)} %get-tuple-element.164) | data formatting | bytes 13107200 | tf_op jit(solution)/shard_map/cond | solution.py:506
  265.3 36.7 %reduce-scatter.4.cloned.1.call-done = bf16[80,2560]{1,0:T(8,128)(2,1)} async-done(((bf16[640,2560]{1,0:T(8,128)(2,1)}), bf16[80,2560]{1,0:T(8,128)(2,1)}) %reduce-scatter.4.cloned.1.call-update) | async-done | bytes 409616 | tf_op jit(solution)/shard_map/reduce_scatter | solution.py:511
  302.0 66.3 %reduce-scatter.8.cloned.1.call-done = bf16[640,640]{0,1:T(8,128)(2,1)} async-done(((bf16[640,5120]{0,1:T(8,128)(2,1)}), bf16[640,640]{0,1:T(8,128)(2,1)}) %reduce-scatter.8.cloned.1.call-update) | async-done | bytes 819216 | tf_op jit(solution)/shard_map/reduce_scatter | solution.py:511
  368.3 66.7 %reduce-scatter.6.cloned.1.call-done = bf16[80,5120]{1,0:T(8,128)(2,1)} async-done(((bf16[640,5120]{1,0:T(8,128)(2,1)}), bf16[80,5120]{1,0:T(8,128)(2,1)}) %reduce-scatter.6.cloned.1.call-update) | async-done | bytes 819216 | tf_op jit(solution)/shard_map/reduce_scatter | solution.py:511
  435.1 42.8 %psum.28 = f32[16,640]{1,0:T(8,128)S(1)} all-reduce(f32[16,640]{1,0:T(8,128)S(1)} %get-tuple-element.158), channel_id=1, replica_groups=mesh['rep'=4,'fsdp'=8] {'rep','fsdp'}, use_global_device_ids=true, to_apply=%region_4.0 | all-reduce | flops 10240 | bytes 81920 | tf_op jit(solution)/shard_map/psum | solution.py:518
  479.2 45.5 %all-reduce.3.cloned.1.call-done = (bf16[80,2560]{1,0:T(8,128)(2,1)}, bf16[80,5120]{1,0:T(8,128)(2,1)}, bf16[640,640]{1,0:T(8,128)(2,1)}) async-done(((bf16[80,2560]{1,0:T(8,128)(2,1)}, bf16[80,5120]{1,0:T(8,128)(2,1)}, bf16[640,640]{1,0:T(8,128)(2,1)}), (bf16[80,2560]{1,0:T(8,128)(2,1)}, bf16[80,5120]{1,0:T(8,128)(2,1)}, bf16[640,640]{1,0:T(8,128)(2,1)})) %all-reduce.3.cloned.1.call-update) | async-done | bytes 2048016 | tf_op jit(solution)/shard_map/psum | solution.py:512
  524.6 1.9 slice.67
  526.5 1.6 slice.68
  528.1 2.4 convert_element_type.21
  530.6 1.3 transpose.7
  (40 shorter events, 6.3 us)
Async XLA Ops:
  7.2 81.0 %all-gather.6.cloned.1.call-start = ((), (), s32[]{:S(2)}) async-start(), calls=%async_computation.3 | async-start | bytes 2764800 | tf_op jit(solution)/shard_map/all_gather | solution.py:486
  7.9 132.1 %all-gather.10.cloned.1.call-start = ((), (), s32[]{:S(2)}) async-start(), calls=%async_computation.5 | async-start | bytes 7372800 | tf_op jit(solution)/shard_map/all_gather | solution.py:486
  8.7 134.0 %all-gather.8.cloned.1.call-start = ((), (), s32[]{:S(2)}) async-start(), calls=%async_computation.4 | async-start | bytes 7372800 | tf_op jit(solution)/shard_map/all_gather | solution.py:486
  9.4 292.6 %reduce-scatter.4.cloned.1.call-start = ((), (), s32[]{:S(2)}) async-start(), calls=%async_computation.6 | async-start | bytes 3686400 | tf_op jit(solution)/shard_map/reduce_scatter | solution.py:511
  88.2 54.5 %copy-start.2 = (bf16[640,1920]{1,0:T(8,128)(2,1)S(1)}, bf16[640,1920]{1,0:T(8,128)(2,1)}, u32[]{:S(2)}) copy-start(bf16[640,1920]{1,0:T(8,128)(2,1)} %all-gather.6.cloned.1.call-done.wqkv_ref) | copy-start | bytes 7372804
  149.2 55.1 %copy-start.1 = (bf16[1024,1920]{1,0:T(8,128)(2,1)S(1)}, bf16[1024,1920]{1,0:T(8,128)(2,1)}, u32[]{:S(2)}) copy-start(bf16[1024,1920]{1,0:T(8,128)(2,1)} %get-tuple-element.100.refs_0_.refs_1_.refs_2_) | copy-start | bytes 11796484 | tf_op jit(solution)/shard_map/cond
  204.3 46.5 %copy-start.5 = (f32[1,5120]{1,0:T(1,128)S(1)}, f32[1,5120]{1,0:T(1,128)}, u32[]{:S(2)}) copy-start(f32[1,5120]{1,0:T(1,128)} %get-tuple-element.117) | copy-start | bytes 61444 | tf_op jit(solution)/shard_map/cond
  204.3 47.2 %copy-start.7 = (f32[8,640]{1,0:T(8,128)S(1)}, f32[8,640]{1,0:T(8,128)}, u32[]{:S(2)}) copy-start(f32[8,640]{1,0:T(8,128)} %get-tuple-element.116) | copy-start | bytes 61444 | tf_op jit(solution)/shard_map/cond
  255.0 113.4 %reduce-scatter.8.cloned.1.call-start = ((), (), s32[]{:S(2)}) async-start(), calls=%async_computation.8 | async-start | bytes 7372800 | tf_op jit(solution)/shard_map/reduce_scatter | solution.py:511
  264.7 170.4 %reduce-scatter.6.cloned.1.call-start = ((), (), s32[]{:S(2)}) async-start(), calls=%async_computation.7 | async-start | bytes 7372800 | tf_op jit(solution)/shard_map/reduce_scatter | solution.py:511
  265.2 259.4 %all-reduce.3.cloned.1.call-start = ((), (), s32[]{:S(2)}) async-start(), calls=%async_computation.9 | async-start | bytes 4096000 | tf_op jit(solution)/shard_map/psum | solution.py:512
  524.6 5.9 %copy-start.3 = (bf16[640,640]{1,0:T(8,128)(2,1)S(1)}, bf16[640,640]{1,0:T(8,128)(2,1)}, u32[]{:S(2)}) copy-start(bf16[640,640]{1,0:T(8,128)(2,1)} %get-tuple-element.167) | copy-start | bytes 2457604
Sparse Core Ops, SparseCore 0:
  9.9 32.1 all-gather.5
  44.0 50.0 all-gather.9
  96.0 46.6 all-gather.7
  255.1 46.8 reduce-scatter.3
  305.3 62.9 reduce-scatter.7
  372.0 62.9 reduce-scatter.5
  437.7 86.9 all-reduce.2

commit v2 on v1

--- a/solution.py
+++ b/solution.py
@@ -69,11 +69,8 @@
         out_ref[start : start + step, :] = dot(pick, src_ref[...]).astype(BF16)
 
 
-def attn_kernel(
-    tokens_ref, mask_ref, vec_ref, wqkv_ref, wout_ref,
-    slot_ref, xp_ref, h1_ref, qkv_ref, o_ref, lse_ref, x1_ref,
-):
-    length, width = tokens_ref.shape
+def slots_of(mask_ref):
+    length = mask_ref.shape[1]
     step = 256
     mask8 = jnp.broadcast_to(mask_ref[...], (8, length))
     cum = []
@@ -84,33 +81,60 @@
     cum = jnp.concatenate(cum, axis=1)
     count = jnp.sum(mask8, axis=1, keepdims=True)
     pos = lax.broadcasted_iota(jnp.int32, (8, length), 1).astype(F32)
-    slot = jnp.where(mask8 > 0.5, cum - 1.0, count + pos - cum)
-    slot_ref[...] = slot
+    return jnp.where(mask8 > 0.5, cum - 1.0, count + pos - cum), count
+
+
+def permute_rows(tokens_ref, slot, xp_ref):
+    step = 256
+
+    def body(i, _):
+        rows = pl.ds(pl.multiple_of(i * step, step), step)
+        pick = one_hot_rows(slot[:1], (i * step).astype(F32), step).astype(BF16)
+        xp_ref[rows, :] = dot(pick, tokens_ref[...]).astype(BF16)
+        return 0
+
+    lax.fori_loop(0, tokens_ref.shape[0] // step, body, 0)
+
+
+def first_norm(xp_ref, vec_ref, h1_ref):
+    step = 128
     gain = vec_ref[0:1, :]
     shift = vec_ref[1:2, :]
+
+    def body(i, _):
+        rows = pl.ds(pl.multiple_of(i * step, step), step)
+        xhat, _ = norm_stats(xp_ref[rows, :].astype(F32))
+        h1_ref[rows, :] = (xhat * gain + shift).astype(BF16)
+        return 0
+
+    lax.fori_loop(0, xp_ref.shape[0] // step, body, 0)
+
+
+def project(h1_ref, vec_ref, wqkv_ref, qkv_ref):
+    length, width = h1_ref.shape
+    step = 256
     bq = vec_ref[2:3, :]
     bv = vec_ref[3:4, :]
-    bout = vec_ref[4:5, :]
-
-    def project(i, _):
+
+    def body(i, _):
         rows = pl.ds(pl.multiple_of(i * step, step), step)
-        pick = one_hot_rows(slot[:1], (i * step).astype(F32), step).astype(BF16)
-        x = dot(pick, tokens_ref[...])
-        xp_ref[rows, :] = x.astype(BF16)
-        xhat, _ = norm_stats(x)
-        h1 = (xhat * gain + shift).astype(BF16)
-        h1_ref[rows, :] = h1
+        h1 = h1_ref[rows, :]
         qkv_ref[rows, :width] = (dot(h1, wqkv_ref[:, :width]) + bq).astype(BF16)
         qkv_ref[rows, width : 2 * width] = dot(h1, wqkv_ref[:, width : 2 * width]).astype(BF16)
         qkv_ref[rows, 2 * width :] = (dot(h1, wqkv_ref[:, 2 * width :]) + bv).astype(BF16)
         return 0
 
-    lax.fori_loop(0, length // step, project, 0)
-
+    lax.fori_loop(0, length // step, body, 0)
+
+
+def attend(qkv_ref, o_ref, lse_ref, beside):
+    length, width = o_ref.shape
+    step = 256
     c = SCALE * LOG2E
     lane = lax.broadcasted_iota(jnp.int32, (step, LANES), 1)
 
-    def attend(n, _):
+    def body(n, _):
+        beside(n)
         t = n // (length // step)
         i = n % (length // step)
         rows = pl.ds(pl.multiple_of(i * step, step), step)
@@ -133,14 +157,234 @@
         lse_ref[pl.ds(pl.multiple_of(t * 8, 8), 8), rows] = jnp.transpose(lses)[:8, :]
         return 0
 
-    lax.fori_loop(0, (width // LANES) * (length // step), attend, 0)
-
-    def join(i, _):
+    lax.fori_loop(0, (width // LANES) * (length // step), body, 0)
+
+
+def join(xp_ref, o_ref, wout_ref, vec_ref, x1_ref):
+    step = 256
+    bout = vec_ref[4:5, :]
+
+    def body(i, _):
         rows = pl.ds(pl.multiple_of(i * step, step), step)
         x1_ref[rows, :] = xp_ref[rows, :].astype(F32) + dot(o_ref[rows, :], wout_ref[...]) + bout
         return 0
 
-    lax.fori_loop(0, length // step, join, 0)
+    lax.fori_loop(0, xp_ref.shape[0] // step, body, 0)
+
+
+def attn_kernel(
+    tokens_ref, mask_ref, vec_ref, wqkv_ref, wout_ref,
+    slot_ref, xp_ref, h1_ref, qkv_ref, o_ref, lse_ref, x1_ref,
+):
+    slot, _ = slots_of(mask_ref)
+    slot_ref[...] = slot
+    permute_rows(tokens_ref, slot, xp_ref)
+    first_norm(xp_ref, vec_ref, h1_ref)
+    project(h1_ref, vec_ref, wqkv_ref, qkv_ref)
+    attend(qkv_ref, o_ref, lse_ref, lambda n: None)
+    join(xp_ref, o_ref, wout_ref, vec_ref, x1_ref)
+
+
+class Place:
+    def __init__(self):
+        self.me = me = lax.axis_index("fsdp")
+        core = me % 2
+        x = me // 2 % 2
+        y = me // 4
+        self.sib = me + 1 - 2 * core
+        self.xn = me + 2 - 4 * x
+        self.yn = me + 4 - 8 * y
+        self.dg = me + 6 - 4 * x - 8 * y
+
+
+def remote(src, dst, send, recv, to):
+    return pltpu.make_async_remote_copy(
+        src_ref=src, dst_ref=dst, send_sem=send, recv_sem=recv,
+        device_id=to, device_id_type=pl.DeviceIdType.MESH,
+    )
+
+
+class Gather:
+    def __init__(self, place, own, full, cut, send, recv, local):
+        self.place = place
+        rows = own.shape[0]
+        at = lambda s, lo=0, hi=rows: full.at[pl.ds(pl.multiple_of(s * rows + lo, 16), hi - lo), :]
+        me, sib, xn, yn, dg = place.me, place.sib, place.xn, place.yn, place.dg
+        moves = [
+            (own, at(me), sib), (own, at(me), xn), (own, at(me), yn),
+            (at(xn), at(xn), sib), (at(yn), at(yn), sib),
+            (at(xn, 0, cut), at(xn, 0, cut), yn), (at(yn, cut), at(yn, cut), xn),
+            (at(dg, 0, cut), at(dg, 0, cut), sib), (at(dg, cut), at(dg, cut), sib),
+        ]
+        self.copies = [
+            remote(src, dst, send.at[i], recv.at[i], {"fsdp": to}) for i, (src, dst, to) in enumerate(moves)
+        ]
+        self.local = pltpu.make_async_copy(own, at(me), local)
+
+    def first(self):
+        self.copies[1].start()
+        self.copies[2].start()
+        self.copies[0].start()
+        self.local.start()
+
+    def second(self):
+        self.copies[1].wait_recv()
+        self.copies[5].start()
+        self.copies[3].start()
+        self.copies[2].wait_recv()
+        self.copies[6].start()
+        self.copies[4].start()
+
+    def third(self):
+        self.copies[5].wait_recv()
+        self.copies[7].start()
+        self.copies[6].wait_recv()
+        self.copies[8].start()
+
+    def finish(self):
+        for i in (0, 3, 4, 7, 8):
+            self.copies[i].wait_recv()
+        self.local.wait()
+        for copy in self.copies:
+            copy.wait_send()
+
+
+def gather_attn_kernel(
+    reps,
+    tokens_ref, mask_ref, pack_ref, wqkv_in, wout_in, wup_in, wdn_in,
+    slot_ref, xp_ref, h1_ref, qkv_ref, o_ref, lse_ref, x1_ref, vec_ref, bup_ref, over_ref,
+    wqkv_ref, wout_ref, wup_ref, wdn_ref,
+    packs, overs, send, recv, local, psend, precv, rsend, rrecv,
+):
+    width = tokens_ref.shape[1]
+    share = wqkv_in.shape[0]
+    place = Place()
+    me = place.me
+    rep = lax.axis_index("rep")
+    shards = packs.shape[0]
+    barrier = pltpu.get_barrier_semaphore()
+    for d in range(1, shards):
+        pl.semaphore_signal(
+            barrier, inc=1, device_id={"fsdp": (me + d) % shards}, device_id_type=pl.DeviceIdType.MESH
+        )
+    for d in range(1, reps):
+        pl.semaphore_signal(
+            barrier, inc=1, device_id={"rep": (rep + d) % reps}, device_id_type=pl.DeviceIdType.MESH
+        )
+    slot, count = slots_of(mask_ref)
+    slot_ref[...] = slot
+    row = lax.broadcasted_iota(jnp.int32, (16, LANES), 0)
+    over = jnp.where(count[:1] > FEW, 1.0, 0.0)
+    packs[me] = jnp.where(row == 13, over, pack_ref[...].astype(F32)).astype(BF16)
+    pl.semaphore_wait(barrier, shards + reps - 2)
+
+    gathers = []
+    for n, (own, full, cut) in enumerate(
+        ((wqkv_in, wqkv_ref, 48), (wout_in, wout_ref, 32), (wup_in, wup_ref, 48), (wdn_in, wdn_ref, 320))
+    ):
+        gathers.append(Gather(place, own, full, cut, send.at[n], recv.at[n], local.at[n]))
+    qkv, out, up, down = gathers
+    vectors = []
+    for d in range(1, shards):
+        copy = remote(
+            packs.at[me], packs.at[me], psend.at[d - 1], precv.at[d - 1], {"fsdp": (me + d) % shards}
+        )
+        copy.start()
+        vectors.append(copy)
+    qkv.first()
+    permute_rows(tokens_ref, slot, xp_ref)
+    for copy in vectors:
+        copy.wait_recv()
+    all_over = packs[0]
+    for s in range(1, shards):
+        all_over = jnp.maximum(all_over, packs[s])
+    overs[rep] = all_over
+    flags = []
+    for d in range(1, reps):
+        copy = remote(overs.at[rep], overs.at[rep], rsend.at[d - 1], rrecv.at[d - 1], {"rep": (rep + d) % reps})
+        copy.start()
+        flags.append(copy)
+    qkv.second()
+    out.first()
+    up.first()
+    vecs = jnp.zeros((16, width), F32)
+    for s in range(shards):
+        pack = packs[s]
+        lane = lax.broadcasted_iota(jnp.int32, (LANES, width), 0)
+        col = lax.broadcasted_iota(jnp.int32, (LANES, width), 1) - s * share
+        spot = jnp.where((lane == col) & (lane < share), 1.0, 0.0).astype(BF16)
+        vecs = vecs + dot(pack, spot)
+        wide = pack.astype(F32)
+        for r in range(width // LANES):
+            bup_ref[0:1, s * width + r * LANES : s * width + (r + 1) * LANES] = wide[8 + r : 9 + r, :]
+    vec_ref[...] = vecs[:8]
+    first_norm(xp_ref, vec_ref, h1_ref)
+    qkv.third()
+    qkv.finish()
+    project(h1_ref, vec_ref, wqkv_ref, qkv_ref)
+
+    def beside(n):
+        for at, step in (
+            (0, out.second), (2, out.third), (4, up.second), (5, down.first), (9, up.third), (14, down.second),
+            (18, down.third),
+        ):
+            pl.when(n == at)(step)
+
+    attend(qkv_ref, o_ref, lse_ref, beside)
+    out.finish()
+    join(xp_ref, o_ref, wout_ref, vec_ref, x1_ref)
+    for copy in flags:
+        copy.wait()
+    for copy in vectors:
+        copy.wait_send()
+    worst = overs[0]
+    for z in range(1, reps):
+        worst = jnp.maximum(worst, overs[z])
+    over_ref[...] = worst[13:14, :].astype(F32)
+    up.finish()
+    down.finish()
+
+
+def gather_attn(reps, shards, tokens, mask, pack, w_qkv, w_out, w_up, w_down):
+    length, width = tokens.shape
+    hidden = w_up.shape[1]
+    sds = jax.ShapeDtypeStruct
+    groups = width // LANES
+    vmem = pl.BlockSpec(memory_space=pltpu.VMEM)
+    hbm = pl.BlockSpec(memory_space=pl.ANY)
+    dma = pltpu.SemaphoreType.DMA
+    return pl.pallas_call(
+        functools.partial(gather_attn_kernel, reps),
+        in_specs=[vmem] * 3 + [hbm] * 4,
+        out_specs=[vmem] * 12 + [hbm] * 2,
+        out_shape=(
+            sds((8, length), F32),
+            sds((length, width), BF16),
+            sds((length, width), BF16),
+            sds((length, 3 * width), BF16),
+            sds((length, width), BF16),
+            sds((8 * groups, length), F32),
+            sds((length, width), F32),
+            sds((8, width), F32),
+            sds((1, hidden), F32),
+            sds((1, LANES), F32),
+            sds((width, 3 * width), BF16),
+            sds((width, width), BF16),
+            sds((width, hidden), BF16),
+            sds((hidden, width), BF16),
+        ),
+        scratch_shapes=[
+            pltpu.VMEM((shards, 16, LANES), BF16),
+            pltpu.VMEM((reps, 16, LANES), BF16),
+            dma((4, 9)), dma((4, 9)), dma((4,)),
+            dma((shards - 1,)), dma((shards - 1,)),
+            dma((reps - 1,)), dma((reps - 1,)),
+        ],
+        compiler_params=pltpu.CompilerParams(
+            vmem_limit_bytes=56 * MB, collective_id=0, has_side_effects=True
+        ),
+        name="gather_attn",
+    )(tokens, mask, pack, w_qkv, w_out, w_up, w_down)
 
 
 def attn_forward(tokens, mask, vecs, wqkv, wout):
@@ -468,25 +712,43 @@
 
 
 def local(
+    reps, shards,
     tokens, masked, cotangent, norm1_gain, norm1_shift, w_qkv, bias_query, bias_value, w_out,
     bias_out, norm2_gain, norm2_shift, w_up, bias_up, w_down, bias_down,
 ):
     seqs, length, width = tokens.shape
     hidden = w_up.shape[1]
     share = w_qkv.shape[0]
+    close = shards == 8 and share % 16 == 0 and share <= LANES and w_down.shape[0] == width
     x = tokens.reshape(seqs * length, width)
     cot = cotangent.reshape(seqs * length, width)
     mask = masked.astype(F32)
-    most = lax.pmax(jnp.sum(masked), ("rep", "fsdp"))
-    packed = jnp.stack(
-        [norm1_gain, norm1_shift, bias_query, bias_value, bias_out, norm2_gain, norm2_shift, bias_down]
-    )
-    vecs = lax.all_gather(packed, "fsdp", axis=1, tiled=True).astype(F32)
-    bup = lax.all_gather(bias_up, "fsdp", axis=0, tiled=True).astype(F32).reshape(1, hidden)
-    gather = lambda w: lax.all_gather(w, "fsdp", axis=0, tiled=True)
-    wqkv, wout, wup, wdn = gather(w_qkv), gather(w_out), gather(w_up), gather(w_down)
-
-    slot, xp, h1, qkv, o, lse, x1 = attn_forward(x, mask, vecs, wqkv, wout)
+    if close:
+        pack = jnp.concatenate(
+            [
+                jnp.pad(
+                    jnp.stack(
+                        [norm1_gain, norm1_shift, bias_query, bias_value, bias_out, norm2_gain, norm2_shift, bias_down]
+                    ),
+                    ((0, 0), (0, LANES - share)),
+                ),
+                jnp.pad(bias_up.reshape(-1, LANES), ((0, 3), (0, 0))),
+            ]
+        )
+        slot, xp, h1, qkv, o, lse, x1, vecs, bup, over, wqkv, wout, wup, wdn = gather_attn(
+            reps, shards, x, mask, pack, w_qkv, w_out, w_up, w_down
+        )
+        small_enough = over[0, 0] < 0.5
+    else:
+        small_enough = lax.pmax(jnp.sum(masked), ("rep", "fsdp")) <= FEW
+        packed = jnp.stack(
+            [norm1_gain, norm1_shift, bias_query, bias_value, bias_out, norm2_gain, norm2_shift, bias_down]
+        )
+        vecs = lax.all_gather(packed, "fsdp", axis=1, tiled=True).astype(F32)
+        bup = lax.all_gather(bias_up, "fsdp", axis=0, tiled=True).astype(F32).reshape(1, hidden)
+        gather = lambda w: lax.all_gather(w, "fsdp", axis=0, tiled=True)
+        wqkv, wout, wup, wdn = gather(w_qkv), gather(w_out), gather(w_up), gather(w_down)
+        slot, xp, h1, qkv, o, lse, x1 = attn_forward(x, mask, vecs, wqkv, wout)
 
     def backward(few):
         def run():
@@ -504,7 +766,7 @@
         return run
 
     res, gtok, gup, gdn, gout, gq, gk, gv, small = lax.cond(
-        most <= FEW, backward(FEW), backward(length)
+        small_enough, backward(FEW), backward(length)
     )
 
     def scatter(g, dim):
@@ -536,4 +798,5 @@
         vec, vec, mat, vec, vec, mat, vec, vec, vec, mat, vec, mat, vec,
     )
     out_specs = (rows3, rows3, vec, vec, mat, vec, vec, mat, vec, vec, vec, mat, vec, mat, vec)
-    return jax.shard_map(local, mesh=mesh, in_specs=in_specs, out_specs=out_specs, check_vma=False)
+    body = functools.partial(local, mesh.shape["rep"], mesh.shape["fsdp"])
+    return jax.shard_map(body, mesh=mesh, in_specs=in_specs, out_specs=out_specs, check_vma=False)

time: 545 us -> 492 us (0.903); the launches traced: 539 us -> 492 us
  blocking collectives: 118 us -> 42.6 us
  Pallas kernels: 151 us -> 191 us
  loops' own time: 6.9 us -> 0.6 us
    pmax x1 -> x0, blocking collectives: 42.2 us -> none  [local(): most = lax.pmax(jnp.sum(masked), ('rep', 'fsdp'))]
    pallas_call x1, Pallas kernels: 51.9 us -> 91.9 us  [gather_attn(): pl.pallas_call(functools.partial(gather_attn_kernel, reps), in_specs=[vme...]
    all_gather x3 -> x0, blocking collectives: 32.9 us -> none  [the longest x1 14.9 us: local(): gather = lambda w: lax.all_gather(w, 'fsdp', axis=0, tiled=True)]
    another operation x1, loops' own time: 6.9 us -> 0.6 us  [local(): lax.cond(small_enough, backward(FEW), backward(length))]
  transfers between devices with their start and end apart: 7 -> 4, of which waited for: 5 -> 4; matrix products, arithmetic and copies ran while one was open for 3% -> 2% of each run, Pallas kernels for 10% -> 0%
where the time goes in v2:
time: 492 us
  waiting for transfers between devices  215 us (44%)
  Pallas kernels  191 us (39%)
  blocking collectives  42.6 us (9%)
  local copies, waits for them, and re-layouts  17.4 us (4%)
  between operations  14.5 us (3%)
  other arithmetic  9.65 us (2%)
    reduce_scatter x3, waiting for transfers between devices, scatter(): part = lax.psum_scatter(g, 'fsdp', scatter_dimension=dim, tiled=True)  169 us
    pallas_call x1, Pallas kernels, gather_attn(): pl.pallas_call(functools.partial(gather_attn_kernel, reps), in_specs=[vme...  91.9 us
    pallas_call x1, Pallas kernels, feed_forward(): pl.pallas_call(functools.partial(ffn_kernel, few), grid=(hidden // fc,),...  55 us
    psum x1, waiting for transfers between devices, scatter(): return lax.psum(part, 'rep').astype(F32)  45.5 us
    pallas_call x1, Pallas kernels, attn_backward(): pl.pallas_call(functools.partial(back_all, few), grid=(groups,), in_specs...  44.5 us
    psum x1, blocking collectives, local(): small = lax.psum(small, ('rep', 'fsdp'))  42.6 us
  transfers between devices with their start and end apart: 4, of which 4 were waited for; matrix products, arithmetic and copies ran while one was open for 2% of the time, Pallas kernels for 0%

profile of v2, /device:TPU:0, one launch (start us, length us, event | category | flops | bytes accessed | tf_op | source)
XLA Modules:
  0.0 491.6 jit_solution(11121668856122470733)
XLA Ops:
  7.2 0.7 convert_element_type.20.mask_ref
  7.9 0.8 stack.35
  8.7 1.3 fusion.2.pack_ref
  10.0 91.9 %gather_attn.1 = (f32[8,1024]{1,0:T(8,128)S(1)}, bf16[1024,640]{1,0:T(8,128)(2,1)}, bf16[1024,640]{1,0:T(8,128)(2,1)}, bf16[1024,1920]{1,0:T(8,128)(2,1)S(1)}, b...) custom-call(bf16[1024,640]{1,0:T(8,128)(2,1)} %bitcast.34, ...), custom_call_target="tpu_custom_call" | custom-call | tf_op jit(solution)/shard_map/gather_attn/pallas_call | solution.py:356
  102.5 102.8 %conditional.1 = (bf16[1024,640]{1,0:T(8,128)(2,1)}, bf16[1024,640]{1,0:T(8,128)(2,1)}, bf16[640,5120]{1,0:T(8,128)(2,1)}, bf16[640,5120]{1,0:T(8,128)(2,1)}, bf...) conditional(s32[]{:T(128)} %bitcast.10, ...), branch_computations={%region_0.1_spmd, %region_1.2_spmd} | conditional | flops 30720 | bytes 368780 | solution.py:768
  102.7 55.0 %feed_forward.3 = (bf16[1024,640]{1,0:T(8,128)(2,1)}, bf16[640,5120]{1,0:T(8,128)(2,1)}, bf16[640,5120]{1,0:T(8,128)(2,1)}, f32[1,5120]{1,0:T(1,128)}, f32[384,6...) custom-call(f32[1024,640]{1,0:T(8,128)} %get-tuple-element.89.x1_ref, ...), custom_call_target="tpu_custom_call" | custom-call | tf_op jit(solution)/shard_map/cond/branch_1_fun/feed_forward/pallas_call | solution.py:505
  157.8 44.5 %attn_backward.3 = (bf16[1024,640]{1,0:T(8,128)(2,1)}, bf16[640,640]{1,0:T(8,128)(2,1)}, bf16[640,640]{1,0:T(8,128)(2,1)}, bf16[640,640]{1,0:T(8,128)(2,1)}, f32[8,640]{1,0:T(8,128)}, /*index=5*/f32[8,640]{1,0:T(8,128)}) custom-call(bf16[1024,1920]{1,0:T(8,128)(2,1)S(1)} %get-tuple-element.100.refs_0_.refs_1_.refs_2_, ...), custom_call_target="tpu_custom_call" | custom-call | tf_op jit(solution)/shard_map/cond/branch_1_fun/attn_backward/pallas_call | solution.py:667
  202.3 0.7 slice.41
  203.0 0.7 slice.42
  204.3 0.7 reduce.7
  205.3 3.3 pad_maximum_fusion.2
  208.7 9.8 %copy.31 = bf16[640,5120]{0,1:T(8,128)(2,1)} copy(bf16[640,5120]{1,0:T(8,128)(2,1)} %get-tuple-element.178) | data formatting | bytes 13107200 | tf_op jit(solution)/shard_map/cond | solution.py:768
  218.5 0.7 reduce-scatter.6.cloned.1.call-update
  219.3 35.8 %reduce-scatter.4.cloned.1.call-done = bf16[80,2560]{1,0:T(8,128)(2,1)} async-done(((bf16[640,2560]{1,0:T(8,128)(2,1)}), bf16[80,2560]{1,0:T(8,128)(2,1)}) %reduce-scatter.4.cloned.1.call-update) | async-done | bytes 409616 | tf_op jit(solution)/shard_map/reduce_scatter | solution.py:773
  255.0 66.5 %reduce-scatter.8.cloned.1.call-done = bf16[640,640]{0,1:T(8,128)(2,1)} async-done(((bf16[640,5120]{0,1:T(8,128)(2,1)}), bf16[640,640]{0,1:T(8,128)(2,1)}) %reduce-scatter.8.cloned.1.call-update) | async-done | bytes 819216 | tf_op jit(solution)/shard_map/reduce_scatter | solution.py:773
  321.5 66.9 %reduce-scatter.6.cloned.1.call-done = bf16[80,5120]{1,0:T(8,128)(2,1)} async-done(((bf16[640,5120]{1,0:T(8,128)(2,1)}), bf16[80,5120]{1,0:T(8,128)(2,1)}) %reduce-scatter.6.cloned.1.call-update) | async-done | bytes 819216 | tf_op jit(solution)/shard_map/reduce_scatter | solution.py:773
  388.4 42.6 %psum.28 = f32[16,640]{1,0:T(8,128)S(1)} all-reduce(f32[16,640]{1,0:T(8,128)S(1)} %get-tuple-element.172), channel_id=1, replica_groups=mesh['rep'=4,'fsdp'=8] {'rep','fsdp'}, use_global_device_ids=true, to_apply=%region_2.3 | all-reduce | flops 10240 | bytes 81920 | tf_op jit(solution)/shard_map/psum | solution.py:780
  431.1 0.7 dynamic_slice.7
  431.8 0.5 slice_bitcast_fusion
  432.4 45.5 %all-reduce.5.cloned.1.call-done = (bf16[80,2560]{1,0:T(8,128)(2,1)}, bf16[80,5120]{1,0:T(8,128)(2,1)}, bf16[640,640]{1,0:T(8,128)(2,1)}) async-done(((bf16[80,2560]{1,0:T(8,128)(2,1)}, bf16[80,5120]{1,0:T(8,128)(2,1)}, bf16[640,640]{1,0:T(8,128)(2,1)}), (bf16[80,2560]{1,0:T(8,128)(2,1)}, bf16[80,5120]{1,0:T(8,128)(2,1)}, bf16[640,640]{1,0:T(8,128)(2,1)})) %all-reduce.5.cloned.1.call-update) | async-done | bytes 2048016 | tf_op jit(solution)/shard_map/psum | solution.py:774
  477.8 1.9 slice.71
  479.7 1.6 slice.72
  481.3 2.4 convert_element_type.24
  483.8 1.3 transpose.7
  (20 shorter events, 0.8 us)
Async XLA Ops:
  7.2 247.9 %reduce-scatter.4.cloned.1.call-start = ((), (), s32[]{:S(2)}) async-start(), calls=%async_computation.3 | async-start | bytes 3686400 | tf_op jit(solution)/shard_map/reduce_scatter | solution.py:773
  157.7 46.5 %copy-start.2 = (f32[1,5120]{1,0:T(1,128)S(1)}, f32[1,5120]{1,0:T(1,128)}, u32[]{:S(2)}) copy-start(f32[1,5120]{1,0:T(1,128)} %get-tuple-element.117) | copy-start | bytes 61444 | tf_op jit(solution)/shard_map/cond
  157.8 47.2 %copy-start.4 = (f32[8,640]{1,0:T(8,128)S(1)}, f32[8,640]{1,0:T(8,128)}, u32[]{:S(2)}) copy-start(f32[8,640]{1,0:T(8,128)} %get-tuple-element.116) | copy-start | bytes 61444 | tf_op jit(solution)/shard_map/cond
  208.6 112.9 %reduce-scatter.8.cloned.1.call-start = ((), (), s32[]{:S(2)}) async-start(), calls=%async_computation.5 | async-start | bytes 7372800 | tf_op jit(solution)/shard_map/reduce_scatter | solution.py:773
  218.5 169.9 %reduce-scatter.6.cloned.1.call-start = ((), (), s32[]{:S(2)}) async-start(), calls=%async_computation.4 | async-start | bytes 7372800 | tf_op jit(solution)/shard_map/reduce_scatter | solution.py:773
  219.2 258.6 %all-reduce.5.cloned.1.call-start = ((), (), s32[]{:S(2)}) async-start(), calls=%async_computation.6 | async-start | bytes 4096000 | tf_op jit(solution)/shard_map/psum | solution.py:774
  477.8 5.9 %copy-start = (bf16[640,640]{1,0:T(8,128)(2,1)S(1)}, bf16[640,640]{1,0:T(8,128)(2,1)}, u32[]{:S(2)}) copy-start(bf16[640,640]{1,0:T(8,128)(2,1)} %get-tuple-element.181) | copy-start | bytes 2457604
Sparse Core Ops, SparseCore 0:
  208.7 46.2 reduce-scatter.3
  258.5 62.9 reduce-scatter.7
  325.4 62.9 reduce-scatter.5
  390.8 86.9 all-reduce.4

commit v3 on v2

--- a/solution.py
+++ b/solution.py
@@ -410,7 +410,7 @@
 def ffn_kernel(
     few,
     x1_ref, cot_ref, slot_ref, mask_ref, vec_ref, bup_ref, wup_ref, wdn_ref, wout_ref, o_ref,
-    res_ref, gup_ref, gdn_ref, gbup_ref, g1_ref, do_ref, gout_ref, small_ref,
+    res_ref, gup_ref, gdn_ref, g1_ref, do_ref, gout_ref, small_ref,
     acc, h2, h2t, gy, gyt, dh2, outp,
 ):
     j = pl.program_id(0)
@@ -465,8 +465,10 @@
             gbup = p_b if gbup is None else gbup + p_b
             dh2[rows, :] += dot(du, wup_ref[...], NT)
     gup_ref[...] = gup.astype(BF16)
-    gdn_ref[...] = gdn.astype(BF16)
-    gbup_ref[...] = gbup
+    for n in range(gdn_ref.shape[0]):
+        cols = slice(n * width, (n + 1) * width)
+        gdn_ref[n] = gdn[:, cols].astype(BF16)
+        small_ref[pl.ds(j * gdn_ref.shape[0] + n, 1), :] = gbup[:, cols]
 
     @pl.when(j == last)
     def _():
@@ -488,18 +490,18 @@
                 gbdown = gbdown + jnp.sum(g, axis=0, keepdims=True)
                 gbout = gbout + jnp.sum(g1b.astype(F32), axis=0, keepdims=True)
         gout_ref[...] = gout.astype(BF16)
-        small_ref[0:1, :] = gbout
-        small_ref[1:2, :] = ggain
-        small_ref[2:3, :] = gshift
-        small_ref[3:4, :] = gbdown
-        small_ref[4:8, :] = jnp.zeros((4, width), F32)
+        small_ref[8:9, :] = gbout
+        small_ref[9:10, :] = ggain
+        small_ref[10:11, :] = gshift
+        small_ref[11:12, :] = gbdown
+        small_ref[12:16, :] = jnp.zeros((4, width), F32)
         unpermute(slot_ref[0:1, :], outp, res_ref)
 
 
 def feed_forward(few, x1, cot, slot, mask, vecs, bup, wup, wdn, wout, o):
     length, width = x1.shape
     hidden = wup.shape[1]
-    fc = 512
+    fc = 2 * width
     sds = jax.ShapeDtypeStruct
     whole = lambda *shape: pl.BlockSpec(shape, lambda j: (0,) * len(shape))
     return pl.pallas_call(
@@ -520,22 +522,20 @@
         out_specs=[
             whole(length, width),
             pl.BlockSpec((width, fc), lambda j: (0, j)),
-            pl.BlockSpec((width, fc), lambda j: (0, j)),
-            pl.BlockSpec((1, fc), lambda j: (0, j)),
+            pl.BlockSpec((2, width, width), lambda j: (j, 0, 0)),
             whole(few, width),
             whole(few, width),
             whole(width, width),
-            whole(8, width),
+            whole(16, width),
         ],
         out_shape=(
             sds((length, width), BF16),
             sds((width, hidden), BF16),
-            sds((width, hidden), BF16),
-            sds((1, hidden), F32),
+            sds((hidden // width, width, width), BF16),
             sds((few, width), F32),
             sds((few, width), BF16),
             sds((width, width), BF16),
-            sds((8, width), F32),
+            sds((16, width), F32),
         ),
         scratch_shapes=[
             pltpu.VMEM((length, width), F32),
@@ -551,82 +551,72 @@
     )(x1, cot, slot, mask, vecs, bup, wup, wdn, wout, o)
 
 
-def back_kernel(
-    few,
-    q_ref, k_ref, v_ref, do_ref, o_ref, lse_ref, h1_ref, xp_ref, vec_ref,
-    wq_ref, wk_ref, wv_ref, g1_ref, slot_ref,
-    gtok_ref, gq_ref, gk_ref, gv_ref, small_ref,
-    h1t, dh1, dqt, dkv, gtp,
-):
-    t = pl.program_id(0)
-    last = pl.num_programs(0) - 1
-    length, width = h1_ref.shape
-    groups = width // LANES
+class Heads:
     step = 256
-    c = SCALE * LOG2E
-    gain = vec_ref[0:1, :]
-
-    @pl.when(t == 0)
-    def _():
-        for start in range(0, length, step):
-            h1t[:, start : start + step] = jnp.transpose(h1_ref[start : start + step, :])
-        dh1[...] = jnp.zeros_like(dh1)
-
-    q = q_ref[...]
-    do = do_ref[...]
-    lane = lax.broadcasted_iota(jnp.int32, (few, LANES), 1)
-    head = lax.broadcasted_iota(jnp.int32, (8, LANES), 0)
-    lane8 = lax.broadcasted_iota(jnp.int32, (8, LANES), 1)
-    pick = jnp.where(lane8 // HEAD_DIM == head, 1.0, 0.0)
-    delta = lax.dot_general(
-        pick, do.astype(F32) * o_ref[...].astype(F32), NT,
-        precision=lax.Precision.HIGHEST, preferred_element_type=F32,
-    )
-    dqt[...] = jnp.zeros_like(dqt)
-    zero = jnp.zeros_like(q)
-    qs = [jnp.where(lane // HEAD_DIM == h, q, zero) for h in range(GROUP)]
-    dos = [jnp.where(lane // HEAD_DIM == h, do, zero) for h in range(GROUP)]
-
-    def keys(i, _):
+
+    def __init__(self, few, q_ref, k_ref, v_ref, do_ref, o_ref, lse_ref, dqt, dkv):
+        self.k_ref, self.v_ref, self.lse_ref, self.dqt, self.dkv = k_ref, v_ref, lse_ref, dqt, dkv
+        q = q_ref[...]
+        do = do_ref[...]
+        lane = lax.broadcasted_iota(jnp.int32, (few, LANES), 1)
+        head = lax.broadcasted_iota(jnp.int32, (8, LANES), 0)
+        lane8 = lax.broadcasted_iota(jnp.int32, (8, LANES), 1)
+        pick = jnp.where(lane8 // HEAD_DIM == head, 1.0, 0.0)
+        self.delta = lax.dot_general(
+            pick, do.astype(F32) * o_ref[...].astype(F32), NT,
+            precision=lax.Precision.HIGHEST, preferred_element_type=F32,
+        )
+        dqt[...] = jnp.zeros_like(dqt)
+        zero = jnp.zeros_like(q)
+        self.qs = [jnp.where(lane // HEAD_DIM == h, q, zero) for h in range(GROUP)]
+        self.dos = [jnp.where(lane // HEAD_DIM == h, do, zero) for h in range(GROUP)]
+
+    def keys(self, i):
+        step = self.step
         rows = pl.ds(pl.multiple_of(i * step, step), step)
-        k = k_ref[rows, :]
-        v = v_ref[rows, :]
+        k = self.k_ref[rows, :]
+        v = self.v_ref[rows, :]
         kt = jnp.transpose(k)
         dk = jnp.zeros((step, LANES), F32)
         dv = jnp.zeros((step, LANES), F32)
         for h in range(GROUP):
-            s = dot(k, qs[h], NT)
-            p = jnp.exp2(s * c - lse_ref[h : h + 1, :])
-            dp = dot(v, dos[h], NT)
-            ds = (p * (dp - delta[h : h + 1, :])).astype(BF16)
-            dv = dv + dot(p.astype(BF16), dos[h])
-            dk = dk + dot(ds, qs[h])
+            s = dot(k, self.qs[h], NT)
+            p = jnp.exp2(s * (SCALE * LOG2E) - self.lse_ref[h : h + 1, :])
+            dp = dot(v, self.dos[h], NT)
+            ds = (p * (dp - self.delta[h : h + 1, :])).astype(BF16)
+            dv = dv + dot(p.astype(BF16), self.dos[h])
+            dk = dk + dot(ds, self.qs[h])
             part = slice(h * HEAD_DIM, (h + 1) * HEAD_DIM)
-            dqt[part, :] += dot(kt[part, :], ds)
-        dkv[rows, :LANES] = (dk * SCALE).astype(BF16)
-        dkv[rows, LANES:] = dv.astype(BF16)
-        return 0
-
-    lax.fori_loop(0, length // step, keys, 0)
+            self.dqt[part, :] += dot(kt[part, :], ds)
+        self.dkv[rows, :LANES] = (dk * SCALE).astype(BF16)
+        self.dkv[rows, LANES:] = dv.astype(BF16)
+
+
+def transpose_rows(src_ref, out_ref):
+    step = 256
+    for start in range(0, src_ref.shape[0], step):
+        out_ref[:, start : start + step] = jnp.transpose(src_ref[start : start + step, :])
+
+
+def group_weights(few, dqt, dkv, h1t, small_ref, cols):
     dq = (jnp.transpose(dqt[...]) * SCALE).astype(BF16)
-    gq_ref[...] = dot(h1t[:, :few], dq).astype(BF16)
+    gq = dot(h1t[:, :few], dq).astype(BF16)
     gkv = dot(h1t[...], dkv[...]).astype(BF16)
-    gk_ref[...] = gkv[:, :LANES]
-    gv_ref[...] = gkv[:, LANES:]
-    small_ref[0:1, :] = jnp.zeros((1, LANES), F32)
-    small_ref[2:3, :] = jnp.sum(dq.astype(F32), axis=0, keepdims=True)
-    small_ref[3:4, :] = jnp.sum(dkv[:, LANES:].astype(F32), axis=0, keepdims=True)
+    small_ref[2:3, cols] = jnp.sum(dq.astype(F32), axis=0, keepdims=True)
+    small_ref[3:4, cols] = jnp.sum(dkv[:, LANES:].astype(F32), axis=0, keepdims=True)
+    return dq, gq, gkv[:, :LANES], gkv[:, LANES:]
+
+
+def group_inputs(few, dq, dkv, wq_ref, wk_ref, wv_ref, dh1):
+    step = 256
     wkv = jnp.concatenate([wk_ref[...], wv_ref[...]], axis=1)
-    for start in range(0, length, step):
+    for start in range(0, dh1.shape[0], step):
         rows = slice(start, start + step)
         dh1[rows, :] += dot(dkv[rows, :], wkv, NT)
     dh1[:few, :] += dot(dq, wq_ref[...], NT)
 
 
-def back_finish(
-    few,
-    dh1_ref, xp_ref, vec_ref, g1_ref, slot_ref, gtok_ref, small_ref, gtp,
-):
+def back_finish(few, dh1_ref, xp_ref, vec_ref, g1_ref, small_ref, gtp):
     length, width = xp_ref.shape
     gain = vec_ref[0:1, :]
     step = 128
@@ -643,72 +633,380 @@
         gshift = gshift + jnp.sum(d, axis=0, keepdims=True)
     small_ref[0:1, :] = ggain
     small_ref[1:2, :] = gshift
-    unpermute(slot_ref[0:1, :], gtp, gtok_ref)
-
-
-def back_all(few, *refs):
-    (q, k, v, do, o, lse, h1, xp, vec, wq, wk, wv, g1, slot,
-     gtok, gq, gk, gv, small, norms, h1t, dh1, dqt, dkv, gtp) = refs
-    back_kernel(few, q, k, v, do, o, lse, h1, xp, vec, wq, wk, wv, g1, slot,
-                gtok, gq, gk, gv, small, h1t, dh1, dqt, dkv, gtp)
-
-    @pl.when(pl.program_id(0) == pl.num_programs(0) - 1)
+
+
+def back_kernel(
+    few,
+    q, k, v, do, o, lse, h1, xp, vec, wq, wk, wv, g1, slot,
+    gtok, gq_ref, gk_ref, gv_ref, small,
+    h1t, dh1, dqt, dkv, gtp,
+):
+    t = pl.program_id(0)
+    cols = pl.ds(pl.multiple_of(t * LANES, LANES), LANES)
+
+    @pl.when(t == 0)
     def _():
-        norms[...] = jnp.zeros_like(norms)
-        back_finish(few, dh1, xp, vec, g1, slot, gtok, norms, gtp)
+        transpose_rows(h1, h1t)
+        dh1[...] = jnp.zeros_like(dh1)
+        small[...] = jnp.zeros_like(small)
+
+    heads = Heads(few, q, k, v, do, o, lse, dqt, dkv)
+
+    def body(i, _):
+        heads.keys(i)
+        return 0
+
+    lax.fori_loop(0, h1.shape[0] // heads.step, body, 0)
+    dq, gq, gk, gv = group_weights(few, dqt, dkv, h1t, small, cols)
+    gq_ref[...] = gq
+    gk_ref[...] = gk
+    gv_ref[...] = gv
+    group_inputs(few, dq, dkv, wq, wk, wv, dh1)
+
+    @pl.when(t == pl.num_programs(0) - 1)
+    def _():
+        back_finish(few, dh1, xp, vec, g1, small, gtp)
+        unpermute(slot[0:1, :], gtp, gtok)
+
+
+def back_specs(few, length, width):
+    groups = width // LANES
+    whole = lambda *shape: pl.BlockSpec(shape, lambda t: (0,) * len(shape))
+    cols = lambda rows, first: pl.BlockSpec((rows, LANES), lambda t: (0, first + t))
+    in_specs = [
+        cols(few, 0),
+        cols(length, groups),
+        cols(length, 2 * groups),
+        cols(few, 0),
+        cols(few, 0),
+        pl.BlockSpec((8, few), lambda t: (t, 0)),
+        whole(length, width),
+        whole(length, width),
+        whole(8, width),
+        cols(width, 0),
+        cols(width, groups),
+        cols(width, 2 * groups),
+        whole(few, width),
+        whole(8, length),
+    ]
+    scratch = [
+        pltpu.VMEM((width, length), BF16),
+        pltpu.VMEM((length, width), F32),
+        pltpu.VMEM((LANES, few), F32),
+        pltpu.VMEM((length, 2 * LANES), BF16),
+        pltpu.VMEM((length, width), BF16),
+    ]
+    return whole, cols, in_specs, scratch
 
 
 def attn_backward(few, qkv, do, o, lse, h1, xp, vecs, wqkv, g1, slot):
     length, width = h1.shape
-    groups = width // LANES
     sds = jax.ShapeDtypeStruct
-    whole = lambda *shape: pl.BlockSpec(shape, lambda t: (0,) * len(shape))
-    cols = lambda rows, first: pl.BlockSpec((rows, LANES), lambda t: (0, first + t))
+    whole, cols, in_specs, scratch = back_specs(few, length, width)
     return pl.pallas_call(
-        functools.partial(back_all, few),
-        grid=(groups,),
-        in_specs=[
-            cols(few, 0),
-            cols(length, groups),
-            cols(length, 2 * groups),
-            cols(few, 0),
-            cols(few, 0),
-            pl.BlockSpec((8, few), lambda t: (t, 0)),
-            whole(length, width),
-            whole(length, width),
-            whole(8, width),
-            cols(width, 0),
-            cols(width, groups),
-            cols(width, 2 * groups),
-            whole(few, width),
-            whole(8, length),
-        ],
-        out_specs=[
-            whole(length, width),
-            cols(width, 0),
-            cols(width, 0),
-            cols(width, 0),
-            cols(8, 0),
-            whole(8, width),
-        ],
+        functools.partial(back_kernel, few),
+        grid=(width // LANES,),
+        in_specs=in_specs,
+        out_specs=[whole(length, width), cols(width, 0), cols(width, 0), cols(width, 0), whole(8, width)],
         out_shape=(
             sds((length, width), BF16),
             sds((width, width), BF16),
             sds((width, width), BF16),
             sds((width, width), BF16),
             sds((8, width), F32),
-            sds((8, width), F32),
         ),
-        scratch_shapes=[
-            pltpu.VMEM((width, length), BF16),
-            pltpu.VMEM((length, width), F32),
-            pltpu.VMEM((LANES, few), F32),
-            pltpu.VMEM((length, 2 * LANES), BF16),
-            pltpu.VMEM((length, width), BF16),
-        ],
+        scratch_shapes=scratch,
         compiler_params=pltpu.CompilerParams(vmem_limit_bytes=56 * MB),
         name="attn_backward",
     )(qkv, qkv, qkv, do, o, lse, h1, xp, vecs, wqkv, wqkv, wqkv, g1, slot)
+
+
+class Reduce:
+    def __init__(self, place, rep, reps, mine, other, acc, near, side, last, depth, fin, sems):
+        send, recv, local = sems
+        self.rep, self.reps = rep, reps
+        self.acc, self.near, self.side, self.last, self.depth, self.fin = acc, near, side, last, depth, fin
+        chip = place.me // 2
+        cx, cy, cd = place.xn // 2, place.yn // 2, place.dg // 2
+        self.chip, self.cx, self.cy = chip, cx, cy
+        fsdp = lambda d: {"fsdp": d}
+        low, high = slice(0, 2), slice(2, 4)
+        n = iter(range(100))
+        def copy(src, dst, to):
+            i = next(n)
+            return remote(src, dst, send.at[i], recv.at[i], to)
+        self.a = [copy(other[q], near.at[:, q], fsdp(place.sib)) for q in range(4)]
+        self.own = [pltpu.make_async_copy(mine[q], acc.at[:, q], local.at[q]) for q in range(4)]
+        self.b = [
+            copy(acc.at[cx, low], side.at[0], fsdp(place.xn)),
+            copy(acc.at[cy, high], side.at[2], fsdp(place.yn)),
+            copy(acc.at[cd, low], side.at[1], fsdp(place.xn)),
+            copy(acc.at[cd, high], side.at[3], fsdp(place.yn)),
+        ]
+        self.c = [
+            copy(acc.at[cy, low], last.at[0], fsdp(place.yn)),
+            copy(acc.at[cx, high], last.at[1], fsdp(place.xn)),
+        ]
+        peers = [(rep + d) % reps for d in range(1, reps)]
+        self.d = [copy(acc.at[chip, z], depth.at[i], {"rep": z}) for i, z in enumerate(peers)]
+        self.e = [copy(fin.at[rep], fin.at[rep], {"rep": z}) for z in peers]
+
+    COPIES = 16
+
+    def start(self):
+        for x in self.a + self.own:
+            x.start()
+
+    def near_sum(self):
+        for q in range(4):
+            self.own[q].wait()
+            self.a[q].wait_recv()
+            for c in range(4):
+                self.acc[c, q] = (self.acc[c, q].astype(F32) + self.near[c, q].astype(F32)).astype(BF16)
+        for x in self.b:
+            x.start()
+
+    def add(self, c, half, part):
+        for q in range(2):
+            self.acc[c, half + q] = (self.acc[c, half + q].astype(F32) + part[q].astype(F32)).astype(BF16)
+
+    def side_sum(self):
+        for x in self.b:
+            x.wait()
+        self.add(self.cy, 0, self.side.at[1])
+        self.c[0].start()
+        self.add(self.cx, 2, self.side.at[3])
+        self.c[1].start()
+        self.add(self.chip, 0, self.side.at[0])
+        self.add(self.chip, 2, self.side.at[2])
+
+    def last_sum(self):
+        for x in self.c:
+            x.wait()
+        self.add(self.chip, 0, self.last.at[0])
+        self.add(self.chip, 2, self.last.at[1])
+        for x in self.d:
+            x.start()
+
+    def depth_sum(self):
+        total = self.acc[self.chip, self.rep].astype(F32)
+        for i in range(self.reps - 1):
+            self.d[i].wait()
+            total = total + self.depth[i].astype(F32)
+        self.fin[self.rep] = total.astype(BF16)
+        for x in self.e:
+            x.start()
+
+    def finish(self):
+        for x in self.e:
+            x.wait()
+        for x in self.a:
+            x.wait_send()
+
+
+class Small:
+    def __init__(self, me, shards, rep, reps, rows, beside, depth, out, sems):
+        psend, precv, rsend, rrecv = sems
+        self.me, self.rep, self.rows, self.near, self.depth, self.out = me, rep, rows, beside, depth, out
+        self.first = [
+            remote(beside.at[me], beside.at[me], psend.at[d - 1], precv.at[d - 1], {"fsdp": (me + d) % shards})
+            for d in range(1, shards)
+        ]
+        self.second = [
+            remote(depth.at[rep], depth.at[rep], rsend.at[d - 1], rrecv.at[d - 1], {"rep": (rep + d) % reps})
+            for d in range(1, reps)
+        ]
+
+    def start(self):
+        self.near[self.me] = self.rows[...]
+        for x in self.first:
+            x.start()
+
+    def middle(self):
+        for x in self.first:
+            x.wait()
+        total = self.near[0]
+        for s in range(1, self.near.shape[0]):
+            total = total + self.near[s]
+        self.depth[self.rep] = total
+        for x in self.second:
+            x.start()
+
+    def finish(self):
+        for x in self.second:
+            x.wait()
+        total = self.depth[0]
+        for z in range(1, self.depth.shape[0]):
+            total = total + self.depth[z]
+        self.out[...] = total
+
+
+def reduce_back_kernel(
+    few, shards, reps,
+    q, k, v, do, o, lse, h1, xp, vec, wq, wk, wv, g1, slot, early_ref, gout_ref, gup_ref, gdn_ref,
+    gtok, gup_out, gdn_out, gqkv_out, gout_out, early_out, late_out,
+    h1t, dh1, dqt, dkv, gtp, late, gqkv, fin, acc, near, side, last, depth, send, recv, local,
+    enear, edepth, lnear, ldepth, es1, er1, es2, er2, ls1, lr1, ls2, lr2,
+):
+    t = pl.program_id(0)
+    cols = pl.ds(pl.multiple_of(t * LANES, LANES), LANES)
+    share = h1.shape[1] // shards
+    width = h1.shape[1]
+    place = Place()
+    rep = lax.axis_index("rep")
+    core = place.me % 2
+
+    def quarter(n, side):
+        u = n // 4
+        if u < 2:
+            return gup_ref.at[:, side, :, n * width : (n + 1) * width]
+        if u < 4:
+            return gdn_ref.at[:, side, (n - 8) * share : (n - 7) * share, :]
+        return gout_ref.at[:, side] if n == 16 else gqkv.at[n - 17, :, side]
+
+    units = []
+    for u in range(5):
+        sems = (send.at[u], recv.at[u], local.at[u])
+        units.append(
+            Reduce(
+                place, rep, reps,
+                [quarter(4 * u + n, core) for n in range(4)],
+                [quarter(4 * u + n, 1 - core) for n in range(4)],
+                acc.at[u], near.at[u], side.at[u], last.at[u], depth.at[u], fin.at[u], sems,
+            )
+        )
+    early = Small(place.me, shards, rep, reps, early_ref, enear, edepth, early_out, (es1, er1, es2, er2))
+    later = Small(place.me, shards, rep, reps, late, lnear, ldepth, late_out, (ls1, lr1, ls2, lr2))
+
+    @pl.when(t == 0)
+    def _():
+        barrier = pltpu.get_barrier_semaphore()
+        for d in range(1, shards):
+            pl.semaphore_signal(
+                barrier, inc=1, device_id={"fsdp": (place.me + d) % shards},
+                device_id_type=pl.DeviceIdType.MESH,
+            )
+        for d in range(1, reps):
+            pl.semaphore_signal(
+                barrier, inc=1, device_id={"rep": (rep + d) % reps}, device_id_type=pl.DeviceIdType.MESH
+            )
+        pl.semaphore_wait(barrier, shards + reps - 2)
+        for u in range(4):
+            units[u].start()
+        early.start()
+        transpose_rows(h1, h1t)
+        dh1[...] = jnp.zeros_like(dh1)
+        late[...] = jnp.zeros_like(late)
+
+    heads = Heads(few, q, k, v, do, o, lse, dqt, dkv)
+    blocks = h1.shape[0] // heads.step
+
+    plan = [
+        (1, units[0].near_sum), (2, units[1].near_sum), (3, units[2].near_sum), (4, units[3].near_sum),
+        (5, early.middle), (6, units[0].side_sum), (9, units[1].side_sum), (10, units[0].last_sum),
+        (11, early.finish), (13, units[2].side_sum), (14, units[1].last_sum), (15, units[0].depth_sum),
+        (17, units[3].side_sum), (18, units[2].last_sum), (19, units[1].depth_sum),
+    ]
+
+    def body(i, _):
+        for at, step in plan:
+            pl.when(t * blocks + i == at)(step)
+        heads.keys(i)
+        return 0
+
+    lax.fori_loop(0, blocks, body, 0)
+    dq, gq, gk, gv = group_weights(few, dqt, dkv, h1t, late, cols)
+    chips = shards // 2
+    for n, g in enumerate((gq, gk, gv)):
+        gqkv[n, :, :, :, cols] = g.reshape(chips, 2, share, LANES)
+    final = t == pl.num_programs(0) - 1
+    pl.when(final)(units[4].start)
+    group_inputs(few, dq, dkv, wq, wk, wv, dh1)
+
+    @pl.when(final)
+    def _():
+        units[4].near_sum()
+        units[3].last_sum()
+        units[2].depth_sum()
+        back_finish(few, dh1, xp, vec, g1, late, gtp)
+        later.start()
+        units[4].side_sum()
+        units[3].depth_sum()
+        units[4].last_sum()
+        later.middle()
+        unpermute(slot[0:1, :], gtp, gtok)
+        units[4].depth_sum()
+        for n in range(16):
+            if n % 4 == 0:
+                units[n // 4].finish()
+            part = fin[n // 4, n % 4].astype(F32)
+            if n < 8:
+                gup_out[:, n * width : (n + 1) * width] = part
+            else:
+                gdn_out[:, (n - 8) * share : (n - 7) * share] = jnp.transpose(part)
+        later.finish()
+        units[4].finish()
+        gout_out[...] = fin[4, 0].astype(F32)
+        for n in range(3):
+            gqkv_out[:, n * width : (n + 1) * width] = fin[4, 1 + n].astype(F32)
+
+
+def reduce_backward(few, shards, reps, ident, qkv, do, o, lse, h1, xp, vecs, wqkv, g1, slot, early, gout, gup, gdn):
+    length, width = h1.shape
+    share = width // shards
+    chips = shards // 2
+    sds = jax.ShapeDtypeStruct
+    whole, cols, in_specs, scratch = back_specs(few, length, width)
+    hbm = pl.BlockSpec(memory_space=pl.ANY)
+    dma = pltpu.SemaphoreType.DMA
+    block = (share, width)
+    copies = Reduce.COPIES
+    hidden = gup.shape[1]
+    return pl.pallas_call(
+        functools.partial(reduce_back_kernel, few, shards, reps),
+        grid=(width // LANES,),
+        in_specs=in_specs + [whole(16, width), hbm, hbm, hbm],
+        out_specs=[
+            whole(length, width), whole(share, hidden), whole(width, width), whole(share, 3 * width),
+            whole(share, width), whole(16, width), whole(8, width),
+        ],
+        out_shape=(
+            sds((length, width), BF16),
+            sds((share, hidden), F32),
+            sds((width, width), F32),
+            sds((share, 3 * width), F32),
+            sds((share, width), F32),
+            sds((16, width), F32),
+            sds((8, width), F32),
+        ),
+        scratch_shapes=scratch
+        + [
+            pltpu.VMEM((8, width), F32),
+            pltpu.VMEM((3, chips, 2) + block, BF16),
+            pltpu.VMEM((5, 4) + block, BF16),
+            pltpu.VMEM((5, chips, 4) + block, BF16),
+            pltpu.VMEM((5, chips, 4) + block, BF16),
+            pltpu.VMEM((5, 4, 2) + block, BF16),
+            pltpu.VMEM((5, 2, 2) + block, BF16),
+            pltpu.VMEM((5, reps - 1) + block, BF16),
+            dma((5, copies)), dma((5, copies)), dma((5, 4)),
+            pltpu.VMEM((shards, 16, width), F32),
+            pltpu.VMEM((reps, 16, width), F32),
+            pltpu.VMEM((shards, 8, width), F32),
+            pltpu.VMEM((reps, 8, width), F32),
+            dma((shards - 1,)), dma((shards - 1,)), dma((reps - 1,)), dma((reps - 1,)),
+            dma((shards - 1,)), dma((shards - 1,)), dma((reps - 1,)), dma((reps - 1,)),
+        ],
+        compiler_params=pltpu.CompilerParams(
+            vmem_limit_bytes=60 * MB, collective_id=ident, has_side_effects=True
+        ),
+        name="reduce_backward",
+    )(
+        qkv, qkv, qkv, do, o, lse, h1, xp, vecs, wqkv, wqkv, wqkv, g1, slot, early,
+        gout.reshape(chips, 2, share, width),
+        gup.reshape(chips, 2, share, hidden),
+        gdn.reshape(chips, 2, width, width),
+    )
 
 
 def local(
@@ -752,35 +1050,42 @@
 
     def backward(few):
         def run():
-            res, gup, gdn, gbup, g1, do, gout, small2 = feed_forward(
+            res, gup, gdn, g1, do, gout, early = feed_forward(
                 few, x1, cot, slot, mask, vecs, bup, wup, wdn, wout, o
             )
-            gtok, gq, gk, gv, small1, norms = attn_backward(
+            if close:
+                gtok, gup, gdn, gqkv, gout, early, late = reduce_backward(
+                    few, shards, reps, 1 if few == FEW else 2,
+                    qkv, do, o, lse, h1, xp, vecs, wqkv, g1, slot, early, gout, gup, gdn,
+                )
+                return res, gtok, gup, gdn, gqkv, gout, early, late
+            gtok, gq, gk, gv, late = attn_backward(
                 few, qkv, do, o, lse, h1, xp, vecs, wqkv, g1, slot
             )
-            small = jnp.concatenate(
-                [norms[:2], small1[2:4], small2[:4], gbup.reshape(8, width)], axis=0
-            )
-            return res, gtok, gup, gdn, gout, gq, gk, gv, small
+            return res, gtok, gup, gdn, jnp.concatenate([gout, gq, gk, gv], axis=1), early, late
 
         return run
 
-    res, gtok, gup, gdn, gout, gq, gk, gv, small = lax.cond(
-        small_enough, backward(FEW), backward(length)
-    )
-
-    def scatter(g, dim):
-        part = lax.psum_scatter(g, "fsdp", scatter_dimension=dim, tiled=True)
-        return lax.psum(part, "rep").astype(F32)
-
-    gup = scatter(gup, 0)
-    gdn = jnp.transpose(scatter(gdn, 1))
-    gattn = scatter(jnp.concatenate([gout, gq, gk, gv], axis=1), 0)
-    gout, gqkv = gattn[:, :width], gattn[:, width:]
-    small = lax.psum(small, ("rep", "fsdp"))
+    res, gtok, *grads, early, late = lax.cond(small_enough, backward(FEW), backward(length))
+
+    if close:
+        gup, gdn, gqkv, gout = grads
+    else:
+        def scatter(g, dim):
+            part = lax.psum_scatter(g, "fsdp", scatter_dimension=dim, tiled=True)
+            return lax.psum(part, "rep").astype(F32)
+
+        gup, gdn, gattn = grads
+        gup = scatter(gup, 0)
+        gdn = scatter(gdn.transpose(0, 2, 1).reshape(hidden, width), 0)
+        gattn = scatter(gattn, 0)
+        gout, gqkv = gattn[:, :width], gattn[:, width:]
+        early = lax.psum(early, ("rep", "fsdp"))
+        late = lax.psum(late, ("rep", "fsdp"))
     me = lax.axis_index("fsdp")
-    mine = lax.dynamic_slice_in_dim(small[:8], me * share, share, axis=1)
-    gbup = lax.dynamic_slice_in_dim(small[8:].reshape(hidden), me * bias_up.shape[0], bias_up.shape[0])
+    own = bias_up.shape[0]
+    gbup = lax.dynamic_slice_in_dim(early[:8].reshape(hidden), me * own, own)
+    mine = lax.dynamic_slice_in_dim(jnp.concatenate([late[:4], early[8:12]]), me * share, share, axis=1)
     return (
         res.reshape(seqs, length, width),
         gtok.reshape(seqs, length, width),

time: 492 us -> 315 us (0.64)
  waiting for transfers between devices: 215 us -> 0 us
  Pallas kernels: 191 us -> 287 us
  blocking collectives: 42.6 us -> 0 us
  between operations: 14.5 us -> 1.32 us
  loops' own time: 0.6 us -> 10 us
  other arithmetic: 9.65 us -> 2.64 us
  local copies, waits for them, and re-layouts: 17.4 us -> 11.6 us
    reduce_scatter x3 -> x0, waiting for transfers between devices: 169 us -> none  [scatter(): part = lax.psum_scatter(g, 'fsdp', scatter_dimension=dim, tiled=True)]
    pallas_call x1, Pallas kernels: 44.5 us -> 145 us  [reduce_backward(): pl.pallas_call(functools.partial(reduce_back_kernel, few, shards, reps),...]
    psum x1 -> x0, waiting for transfers between devices: 45.5 us -> none  [scatter(): return lax.psum(part, 'rep').astype(F32)]
    psum x1 -> x0, blocking collectives: 42.6 us -> none  [local(): small = lax.psum(small, ('rep', 'fsdp'))]
    cond x5 -> x4, local copies, waits for them, and re-layouts: 9.8 us -> 0.01 us  [the longest x1 9.79 us: local(): lax.cond(small_enough, backward(FEW), backward(length))]
    another operation x1, loops' own time: 0.6 us -> 10 us  [local(): lax.cond(small_enough, backward(FEW), backward(length))]
    unnamed x2 -> x15, local copies, waits for them, and re-layouts: 0.01 us -> 7.32 us
    pallas_call x1, Pallas kernels: 55 us -> 49.4 us  [feed_forward(): pl.pallas_call(functools.partial(ffn_kernel, few), grid=(hidden // fc,),...]
  transfers between devices with their start and end apart: 4 -> 0, of which waited for: 4 -> 0; matrix products, arithmetic and copies ran while one was open for 2% -> 0% of each run, Pallas kernels for 0% -> 0%
where the time goes in v3:
time: 315 us; the launch traced here: 312 us
  Pallas kernels  287 us (91%)
  local copies, waits for them, and re-layouts  11.6 us (4%)
  loops' own time  10 us (3%)
    pallas_call x1, Pallas kernels, reduce_backward(): pl.pallas_call(functools.partial(reduce_back_kernel, few, shards, reps),...  145 us
    pallas_call x1, Pallas kernels, gather_attn(): pl.pallas_call(functools.partial(gather_attn_kernel, reps), in_specs=[vme...  91.9 us
    pallas_call x1, Pallas kernels, feed_forward(): pl.pallas_call(functools.partial(ffn_kernel, few), grid=(hidden // fc,),...  49.4 us
    another operation x1, loops' own time, local(): lax.cond(small_enough, backward(FEW), backward(length))  10 us
    unnamed x15, local copies, waits for them, and re-layouts  7.32 us

profile of v3, /device:TPU:0, one launch (start us, length us, event | category | flops | bytes accessed | tf_op | source)
XLA Modules:
  0.0 312.1 jit_solution(1152179553992425458)
XLA Ops:
  0.6 1.3 convert_element_type.13.mask_ref
  1.9 0.8 stack.35
  2.7 1.3 fusion.2.pack_ref
  4.0 91.9 %gather_attn.1 = (f32[8,1024]{1,0:T(8,128)S(1)}, bf16[1024,640]{1,0:T(8,128)(2,1)}, bf16[1024,640]{1,0:T(8,128)(2,1)}, bf16[1024,1920]{1,0:T(8,128)(2,1)S(1)}, b...) custom-call(bf16[1024,640]{1,0:T(8,128)(2,1)} %bitcast.43, ...), custom_call_target="tpu_custom_call" | custom-call | tf_op jit(solution)/shard_map/gather_attn/pallas_call | solution.py:356
  96.6 0.0 copy-done.8
  96.6 204.7 %conditional.1 = (bf16[1024,640]{1,0:T(8,128)(2,1)}, bf16[1024,640]{1,0:T(8,128)(2,1)}, f32[80,5120]{1,0:T(8,128)}, f32[640,640]{1,0:T(8,128)}, f32[80,1920]{1,0...) conditional(s32[]{:T(128)} %bitcast.16, (f32[1024,640]{1,0:T(8,128)S(1)}, ...), branch_computations={%region_0.1_spmd, %region_1.2_spmd} | conditional | bytes 5324920 | solution.py:1069
  106.4 0.0 copy-start.1
  106.4 0.0 copy-start.6
  106.4 49.4 %feed_forward.3 = (bf16[1024,640]{1,0:T(8,128)(2,1)}, bf16[640,5120]{1,0:T(8,128)(2,1)}, bf16[8,640,640]{2,1,0:T(8,128)(2,1)}, f32[384,640]{1,0:T(8,128)}, bf16[...) custom-call(f32[1024,640]{1,0:T(8,128)S(1)} %get-tuple-element.89.x1_ref, ...), custom_call_target="tpu_custom_call" | custom-call | tf_op jit(solution)/shard_map/cond/branch_1_fun/feed_forward/pallas_call | solution.py:507
  155.8 0.0 copy-done.1
  155.8 0.0 copy-done.6
  155.8 145.2 %reduce_backward.3 = (bf16[1024,640]{1,0:T(8,128)(2,1)}, f32[80,5120]{1,0:T(8,128)}, f32[640,640]{1,0:T(8,128)}, f32[80,1920]{1,0:T(8,128)}, f32[80,640]{1,0:T(8...) custom-call(bf16[1024,1920]{1,0:T(8,128)(2,1)S(1)} %get-tuple-element.100.q.k.v, ...), custom_call_target="tpu_custom_call" | custom-call | tf_op jit(solution)/shard_map/cond/branch_1_fun/reduce_backward/pallas_call | solution.py:965
  301.3 0.8 slice.37
  302.0 0.7 slice.38
  302.8 0.1 fusion.3
  302.9 0.5 slice_bitcast_fusion
  303.4 0.7 slice.46
  304.1 0.7 dynamic_slice.7
  304.8 2.6 copy.52
  307.4 0.8 copy.53
  308.3 0.7 copy.54
  308.9 1.2 copy.55
  310.1 0.9 copy-done.3
  311.0 1.2 copy.56
  (9 shorter events, 0.0 us)
Async XLA Ops:
  4.0 92.6 %copy-start.8 = (f32[1,1024]{1,0:T(1,128)S(1)}, f32[1,1024]{1,0:T(1,128)}, u32[]{:S(2)}) copy-start(f32[1,1024]{1,0:T(1,128)} %convert_element_type.13.mask_ref) | copy-start | bytes 12292
  106.4 49.4 %copy-start.1 = (bf16[1024,640]{1,0:T(8,128)(2,1)}, bf16[1024,640]{1,0:T(8,128)(2,1)S(1)}, u32[]{:S(2)}) copy-start(bf16[1024,640]{1,0:T(8,128)(2,1)S(1)} %get-tuple-element.98.o_ref.o) | copy-start | bytes 3932164 | tf_op jit(solution)/shard_map/cond
  106.4 49.4 %copy-start.6 = (f32[8,640]{1,0:T(8,128)}, f32[8,640]{1,0:T(8,128)S(1)}, u32[]{:S(2)}) copy-start(f32[8,640]{1,0:T(8,128)S(1)} %get-tuple-element.93.vec_ref.vec) | copy-start | bytes 61444 | tf_op jit(solution)/shard_map/cond
  301.2 6.2 %copy-start.4 = (f32[80,1920]{1,0:T(8,128)S(1)}, f32[80,1920]{1,0:T(8,128)}, u32[]{:S(2)}) copy-start(f32[80,1920]{1,0:T(8,128)} %get-tuple-element.220) | copy-start | bytes 1843204
  304.8 3.5 %copy-start.7 = (f32[80,640]{1,0:T(8,128)S(1)}, f32[80,640]{1,0:T(8,128)}, u32[]{:S(2)}) copy-start(f32[80,640]{1,0:T(8,128)} %get-tuple-element.223) | copy-start | bytes 614404
  304.8 4.1 %copy-start.2 = (f32[80,5120]{1,0:T(8,128)S(1)}, f32[80,5120]{1,0:T(8,128)}, u32[]{:S(2)}) copy-start(f32[80,5120]{1,0:T(8,128)} %get-tuple-element.227) | copy-start | bytes 4915204
  308.9 2.0 copy-start.3

commit v4 on v3

--- a/solution.py
+++ b/solution.py
@@ -407,6 +407,85 @@
     )(tokens, mask, vecs, wqkv, wout)
 
 
+def ffn_blocks(few, length):
+    part = few if few <= 384 else 256
+    blocks = [(start, part, True) for start in range(0, few, part)]
+    start = few
+    while start < length:
+        size = min(320, length - start)
+        blocks.append((start, size, False))
+        start += size
+    return blocks
+
+
+def ffn_start(blocks, x1_ref, cot_ref, slot_ref, mask_ref, vec_ref, acc, h2, h2t, gy, gyt, dh2):
+    gain = vec_ref[5:6, :]
+    shift = vec_ref[6:7, :]
+    bdown = vec_ref[7:8, :]
+    for start, size, back in blocks:
+        rows = slice(start, start + size)
+        x1 = x1_ref[rows, :]
+        xhat, _ = norm_stats(x1)
+        hidden = (xhat * gain + shift).astype(BF16)
+        h2[rows, :] = hidden
+        acc[rows, :] = x1 + bdown
+        if back:
+            h2t[:, rows] = jnp.transpose(hidden)
+            pick = one_hot_rows(slot_ref[0:1, :], float(start), size) * mask_ref[...]
+            g = dot(pick.astype(BF16), cot_ref[...])
+            gy[rows, :] = g.astype(BF16)
+            gyt[:, rows] = jnp.transpose(g.astype(BF16))
+            dh2[rows, :] = jnp.zeros_like(g)
+
+
+def ffn_block(block, wup, wdn, bup, acc, h2, h2t, gy, gyt, dh2):
+    start, size, back = block
+    rows = slice(start, start + size)
+    u = dot(h2[rows, :], wup) + bup
+    cdf, e = cdf_parts(u)
+    a = (u * cdf).astype(BF16)
+    acc[rows, :] += dot(a, wdn)
+    if not back:
+        return None
+    da = dot(gy[rows, :], wdn, NT)
+    du = ((cdf + u * e * 0.3989422804014327) * da).astype(BF16)
+    dh2[rows, :] += dot(du, wup, NT)
+    return (
+        dot(h2t[:, rows], du),
+        dot(gyt[:, rows], a),
+        jnp.sum(du.astype(F32), axis=0, keepdims=True),
+    )
+
+
+def ffn_end(blocks, x1_ref, slot_ref, vec_ref, wout_ref, o_ref, acc, gy, dh2, outp, res_ref, g1_ref, do_ref, small_ref):
+    gain = vec_ref[5:6, :]
+    ggain = gshift = gbdown = gbout = gout = None
+    plus = lambda a, b: b if a is None else a + b
+    for start, size, back in blocks:
+        rows = slice(start, start + size)
+        outp[rows, :] = acc[rows, :].astype(BF16)
+        if back:
+            xhat, rstd = norm_stats(x1_ref[rows, :])
+            d = dh2[rows, :]
+            g = gy[rows, :].astype(F32)
+            g1 = g + norm_back(d, xhat, rstd, gain)
+            g1_ref[rows, :] = g1
+            g1b = g1.astype(BF16)
+            do_ref[rows, :] = dot(g1b, wout_ref[...], NT).astype(BF16)
+            gout = plus(gout, dot(jnp.transpose(o_ref[rows, :]), g1b))
+            ggain = plus(ggain, jnp.sum(d * xhat, axis=0, keepdims=True))
+            gshift = plus(gshift, jnp.sum(d, axis=0, keepdims=True))
+            gbdown = plus(gbdown, jnp.sum(g, axis=0, keepdims=True))
+            gbout = plus(gbout, jnp.sum(g1b.astype(F32), axis=0, keepdims=True))
+    small_ref[8:9, :] = gbout
+    small_ref[9:10, :] = ggain
+    small_ref[10:11, :] = gshift
+    small_ref[11:12, :] = gbdown
+    small_ref[12:16, :] = jnp.zeros((4, outp.shape[1]), F32)
+    unpermute(slot_ref[0:1, :], outp, res_ref)
+    return gout
+
+
 def ffn_kernel(
     few,
     x1_ref, cot_ref, slot_ref, mask_ref, vec_ref, bup_ref, wup_ref, wdn_ref, wout_ref, o_ref,
@@ -414,88 +493,31 @@
     acc, h2, h2t, gy, gyt, dh2, outp,
 ):
     j = pl.program_id(0)
-    last = pl.num_programs(0) - 1
     length, width = x1_ref.shape
-    gain = vec_ref[5:6, :]
-    shift = vec_ref[6:7, :]
-    bdown = vec_ref[7:8, :]
-    blocks = []
-    start = 0
-    part = few if few <= 384 else 256
-    while start < few:
-        blocks.append((start, part, True))
-        start += part
-    while start < length:
-        size = min(320, length - start)
-        blocks.append((start, size, False))
-        start += size
+    blocks = ffn_blocks(few, length)
 
     @pl.when(j == 0)
     def _():
-        for start, size, back in blocks:
-            rows = slice(start, start + size)
-            x1 = x1_ref[rows, :]
-            xhat, _ = norm_stats(x1)
-            hidden = (xhat * gain + shift).astype(BF16)
-            h2[rows, :] = hidden
-            acc[rows, :] = x1 + bdown
-            if back:
-                h2t[:, rows] = jnp.transpose(hidden)
-                pick = one_hot_rows(slot_ref[0:1, :], float(start), size) * mask_ref[...]
-                g = dot(pick.astype(BF16), cot_ref[...])
-                gy[rows, :] = g.astype(BF16)
-                gyt[:, rows] = jnp.transpose(g.astype(BF16))
-                dh2[rows, :] = jnp.zeros((size, width), F32)
-
-    gup = gdn = gbup = None
-    for start, size, back in blocks:
-        rows = slice(start, start + size)
-        u = dot(h2[rows, :], wup_ref[...]) + bup_ref[...]
-        cdf, e = cdf_parts(u)
-        a = (u * cdf).astype(BF16)
-        acc[rows, :] += dot(a, wdn_ref[...])
-        if back:
-            da = dot(gy[rows, :], wdn_ref[...], NT)
-            du = ((cdf + u * e * 0.3989422804014327) * da).astype(BF16)
-            p_up = dot(h2t[:, rows], du)
-            p_dn = dot(gyt[:, rows], a)
-            p_b = jnp.sum(du.astype(F32), axis=0, keepdims=True)
-            gup = p_up if gup is None else gup + p_up
-            gdn = p_dn if gdn is None else gdn + p_dn
-            gbup = p_b if gbup is None else gbup + p_b
-            dh2[rows, :] += dot(du, wup_ref[...], NT)
+        ffn_start(blocks, x1_ref, cot_ref, slot_ref, mask_ref, vec_ref, acc, h2, h2t, gy, gyt, dh2)
+
+    total = None
+    for block in blocks:
+        part = ffn_block(block, wup_ref[...], wdn_ref[...], bup_ref[...], acc, h2, h2t, gy, gyt, dh2)
+        if part is not None:
+            total = part if total is None else [x + y for x, y in zip(total, part)]
+    gup, gdn, gbup = total
     gup_ref[...] = gup.astype(BF16)
     for n in range(gdn_ref.shape[0]):
         cols = slice(n * width, (n + 1) * width)
         gdn_ref[n] = gdn[:, cols].astype(BF16)
         small_ref[pl.ds(j * gdn_ref.shape[0] + n, 1), :] = gbup[:, cols]
 
-    @pl.when(j == last)
+    @pl.when(j == pl.num_programs(0) - 1)
     def _():
-        ggain = gshift = gbdown = gbout = gout = jnp.zeros((1, 1), F32)
-        for start, size, back in blocks:
-            rows = slice(start, start + size)
-            outp[rows, :] = acc[rows, :].astype(BF16)
-            if back:
-                xhat, rstd = norm_stats(x1_ref[rows, :])
-                d = dh2[rows, :]
-                g = gy[rows, :].astype(F32)
-                g1 = g + norm_back(d, xhat, rstd, gain)
-                g1_ref[rows, :] = g1
-                g1b = g1.astype(BF16)
-                do_ref[rows, :] = dot(g1b, wout_ref[...], NT).astype(BF16)
-                gout = gout + dot(jnp.transpose(o_ref[rows, :]), g1b)
-                ggain = ggain + jnp.sum(d * xhat, axis=0, keepdims=True)
-                gshift = gshift + jnp.sum(d, axis=0, keepdims=True)
-                gbdown = gbdown + jnp.sum(g, axis=0, keepdims=True)
-                gbout = gbout + jnp.sum(g1b.astype(F32), axis=0, keepdims=True)
+        gout = ffn_end(
+            blocks, x1_ref, slot_ref, vec_ref, wout_ref, o_ref, acc, gy, dh2, outp, res_ref, g1_ref, do_ref, small_ref
+        )
         gout_ref[...] = gout.astype(BF16)
-        small_ref[8:9, :] = gbout
-        small_ref[9:10, :] = ggain
-        small_ref[10:11, :] = gshift
-        small_ref[11:12, :] = gbdown
-        small_ref[12:16, :] = jnp.zeros((4, width), F32)
-        unpermute(slot_ref[0:1, :], outp, res_ref)
 
 
 def feed_forward(few, x1, cot, slot, mask, vecs, bup, wup, wdn, wout, o):
@@ -1009,6 +1031,464 @@
     )
 
 
+class Unit:
+    COPIES = 13
+
+    def __init__(self, place, rep, reps, other, acc, near, side, last, depth, fin, send, recv):
+        self.rep, self.reps = rep, reps
+        self.acc, self.near, self.side, self.last, self.depth, self.fin = acc, near, side, last, depth, fin
+        chip = place.me // 2
+        cx, cy, cd = place.xn // 2, place.yn // 2, place.dg // 2
+        self.chip, self.cx, self.cy = chip, cx, cy
+        self.rows = rows = acc.shape[1]
+        half, self.quarter = rows // 2, rows // 4
+        low, high = pl.ds(0, half), pl.ds(half, half)
+        self.low, self.high = low, high
+        fsdp = lambda d: {"fsdp": d}
+
+        def copy(i, src, dst, to):
+            return remote(src, dst, send.at[i], recv.at[i], to)
+
+        if other is not None:
+            self.a = copy(0, other, near, fsdp(place.sib))
+        if side is not None:
+            self.b = [
+                copy(1, acc.at[cd, low], side.at[1], fsdp(place.xn)),
+                copy(2, acc.at[cd, high], side.at[3], fsdp(place.yn)),
+                copy(3, acc.at[cx, low], side.at[0], fsdp(place.xn)),
+                copy(4, acc.at[cy, high], side.at[2], fsdp(place.yn)),
+            ]
+            self.c = [
+                copy(5, acc.at[cy, low], last.at[0], fsdp(place.yn)),
+                copy(6, acc.at[cx, high], last.at[1], fsdp(place.xn)),
+            ]
+        if depth is not None:
+            peers = [(rep + d) % reps for d in range(1, reps)]
+            own = acc.at[chip] if other is not None or side is not None else acc.at[0]
+            self.own = own
+            self.d = [copy(7 + i, own.at[self.part(z)], depth.at[i], {"rep": z}) for i, z in enumerate(peers)]
+            self.e = [
+                copy(10 + i, fin.at[self.part(rep)], fin.at[self.part(rep)], {"rep": z})
+                for i, z in enumerate(peers)
+            ]
+
+    def part(self, z):
+        return pl.ds(pl.multiple_of(z * self.quarter, 16), self.quarter)
+
+    def near_start(self):
+        self.a.start()
+
+    def near_add(self):
+        self.a.wait_recv()
+        for c in range(self.acc.shape[0]):
+            self.acc[c] = self.acc[c] + self.near[c]
+
+    def side_start(self):
+        for x in self.b:
+            x.start()
+
+    def near_sum(self):
+        self.near_add()
+        self.side_start()
+
+    def add(self, c, half, ref):
+        self.acc[c, half, :] = self.acc[c, half, :] + ref[...]
+
+    def side_sum(self):
+        self.b[0].wait()
+        self.add(self.cy, self.low, self.side.at[1])
+        self.c[0].start()
+        self.b[1].wait()
+        self.add(self.cx, self.high, self.side.at[3])
+        self.c[1].start()
+        self.b[2].wait()
+        self.add(self.chip, self.low, self.side.at[0])
+        self.b[3].wait()
+        self.add(self.chip, self.high, self.side.at[2])
+
+    def last_add(self):
+        for x in self.c:
+            x.wait()
+        self.add(self.chip, self.low, self.last.at[0])
+        self.add(self.chip, self.high, self.last.at[1])
+
+    def depth_start(self):
+        for x in self.d:
+            x.start()
+
+    def last_sum(self):
+        self.last_add()
+        self.depth_start()
+
+    def depth_sum(self):
+        mine = self.part(self.rep)
+        total = self.own[mine, :].astype(F32)
+        for i in range(self.reps - 1):
+            self.d[i].wait()
+            total = total + self.depth[i].astype(F32)
+        self.fin[mine, :] = total.astype(BF16)
+        for x in self.e:
+            x.start()
+
+    def finish(self):
+        for x in self.e:
+            x.wait()
+
+
+def greet(me, shards, rep, reps):
+    barrier = pltpu.get_barrier_semaphore()
+    mesh = pl.DeviceIdType.MESH
+    for d in range(1, shards):
+        pl.semaphore_signal(barrier, inc=1, device_id={"fsdp": (me + d) % shards}, device_id_type=mesh)
+    for d in range(1, reps):
+        pl.semaphore_signal(barrier, inc=1, device_id={"rep": (rep + d) % reps}, device_id_type=mesh)
+    pl.semaphore_wait(barrier, shards + reps - 2)
+
+
+CHUNKS = 5
+
+
+def ffn_reduce_kernel(
+    few, shards, reps,
+    x1_ref, cot_ref, slot_ref, mask_ref, vec_ref, wout_ref, o_ref, *refs,
+):
+    bups, wups, wdns = refs[:shards], refs[shards : 2 * shards], refs[2 * shards : 3 * shards]
+    (
+        res_ref, g1_ref, do_ref, gout_ref, small_ref, fin_ref, own_ref, plane_ref,
+        acc, h2, h2t, gy, gyt, dh2, outp, g, near, side, last, depth, fin, send, recv,
+    ) = refs[3 * shards :]
+    j = pl.program_id(0)
+    length, width = x1_ref.shape
+    share = width // shards
+    blocks = ffn_blocks(few, length)
+    place = Place()
+    rep = lax.axis_index("rep")
+    core = place.me % 2
+    units = []
+    for u in range(CHUNKS):
+        z = u < 2
+        xy = u < 4
+        units.append(
+            Unit(
+                place, rep, reps, g.at[u, 1 - core], g.at[u, core], near.at[u],
+                side.at[u] if xy else None, last.at[u] if xy else None,
+                depth.at[u] if z else None, fin.at[u] if z else None, send.at[u], recv.at[u],
+            )
+        )
+
+    def at(step, *acts):
+        @pl.when(j == step)
+        def _():
+            for act in acts:
+                act()
+
+    @pl.when(j == 0)
+    def _():
+        greet(place.me, shards, rep, reps)
+        ffn_start(blocks, x1_ref, cot_ref, slot_ref, mask_ref, vec_ref, acc, h2, h2t, gy, gyt, dh2)
+
+    at(2, units[0].last_sum)
+    at(3, units[1].last_sum, units[0].depth_sum)
+    at(4, units[2].last_add, units[1].depth_sum)
+    wup = jnp.concatenate([w[...] for w in wups], axis=1)
+    wdn = jnp.concatenate([w[...] for w in wdns], axis=0)
+    bup = jnp.concatenate([b[...] for b in bups], axis=1)
+    cols = pl.ds(pl.multiple_of(j * LANES, LANES), LANES)
+    for n, block in enumerate(blocks):
+        part = ffn_block(block, wup, wdn, bup, acc, h2, h2t, gy, gyt, dh2)
+        if n == 0:
+            gup, gdn, gbup = part
+            for s in range(shards):
+                mine = slice(s * share, (s + 1) * share)
+                lanes = slice(s * LANES, (s + 1) * LANES)
+                for b in range(shards):
+                    g[j, s % 2, s // 2, b * share : (b + 1) * share, :] = gup[
+                        mine, b * LANES : (b + 1) * LANES
+                    ].astype(BF16)
+                g[j, s % 2, s // 2, width:, :] = gdn[:, lanes].astype(BF16)
+                small_ref[s : s + 1, cols] = gbup[:, lanes]
+            for u in range(CHUNKS):
+                at(u, units[u].near_start)
+        if n == 1:
+            for u in range(4):
+                at(u + 1, units[u].side_sum)
+        if n == 2:
+            for u in range(4):
+                at(u, units[u].near_sum)
+
+    @pl.when(j == CHUNKS - 1)
+    def _():
+        gout = ffn_end(
+            blocks, x1_ref, slot_ref, vec_ref, wout_ref, o_ref, acc, gy, dh2, outp, res_ref, g1_ref, do_ref, small_ref
+        )
+        for s in range(shards):
+            for b in range(CHUNKS):
+                gout_ref[s % 2, s // 2, b * share : (b + 1) * share, :] = gout[
+                    s * share : (s + 1) * share, b * LANES : (b + 1) * LANES
+                ].astype(BF16)
+            spare = gout_ref.shape[2] - CHUNKS * share
+            gout_ref[s % 2, s // 2, CHUNKS * share :, :] = jnp.zeros((spare, LANES), BF16)
+        units[4].near_add()
+        plane_ref[...] = g[4, core]
+        units[3].last_add()
+        for n, u in enumerate((2, 3)):
+            own_ref[n] = g[u, core, units[u].chip]
+        for u in range(2):
+            units[u].finish()
+            fin_ref[u] = fin[u]
+        for u in range(CHUNKS):
+            units[u].a.wait_send()
+
+
+def ffn_reduce(few, shards, reps, x1, cot, slot, mask, vecs, bup, wup, wdn, wout, o):
+    length, width = x1.shape
+    share = width // shards
+    chips = shards // 2
+    rows = 2 * width
+    spare = 448
+    sds = jax.ShapeDtypeStruct
+    whole = lambda *shape: pl.BlockSpec(shape, lambda j: (0,) * len(shape))
+    pick = lambda s, shape, across: pl.BlockSpec(
+        shape, lambda j: (0, s * CHUNKS + j) if across else (s * CHUNKS + j, 0)
+    )
+    dma = pltpu.SemaphoreType.DMA
+    return pl.pallas_call(
+        functools.partial(ffn_reduce_kernel, few, shards, reps),
+        grid=(CHUNKS,),
+        in_specs=[
+            whole(length, width), whole(length, width), whole(8, length), whole(1, length), whole(8, width),
+            whole(width, width), whole(few, width),
+        ]
+        + [pick(s, (1, LANES), True) for s in range(shards)]
+        + [pick(s, (width, LANES), True) for s in range(shards)]
+        + [pick(s, (LANES, width), False) for s in range(shards)],
+        out_specs=[
+            whole(length, width), whole(few, width), whole(few, width), whole(2, chips, spare, LANES),
+            whole(16, width), whole(2, rows, LANES), whole(2, rows, LANES), whole(chips, rows, LANES),
+        ],
+        out_shape=(
+            sds((length, width), BF16),
+            sds((few, width), F32),
+            sds((few, width), BF16),
+            sds((2, chips, spare, LANES), BF16),
+            sds((16, width), F32),
+            sds((2, rows, LANES), BF16),
+            sds((2, rows, LANES), BF16),
+            sds((chips, rows, LANES), BF16),
+        ),
+        scratch_shapes=[
+            pltpu.VMEM((length, width), F32),
+            pltpu.VMEM((length, width), BF16),
+            pltpu.VMEM((width, few), BF16),
+            pltpu.VMEM((few, width), BF16),
+            pltpu.VMEM((width, few), BF16),
+            pltpu.VMEM((few, width), F32),
+            pltpu.VMEM((length, width), BF16),
+            pltpu.VMEM((CHUNKS, 2, chips, rows, LANES), BF16),
+            pltpu.VMEM((CHUNKS, chips, rows, LANES), BF16),
+            pltpu.VMEM((4, 4, rows // 2, LANES), BF16),
+            pltpu.VMEM((4, 2, rows // 2, LANES), BF16),
+            pltpu.VMEM((2, reps - 1, rows // 4, LANES), BF16),
+            pltpu.VMEM((2, rows, LANES), BF16),
+            dma((CHUNKS, Unit.COPIES)), dma((CHUNKS, Unit.COPIES)),
+        ],
+        compiler_params=pltpu.CompilerParams(
+            vmem_limit_bytes=60 * MB, collective_id=3, has_side_effects=True
+        ),
+        name="ffn_reduce",
+    )(x1, cot, slot, mask, vecs, wout, o, *[bup] * shards, *[wup] * shards, *[wdn] * shards)
+
+
+GROUP_ROWS = 256
+
+
+def back_reduce_kernel(
+    few, shards, reps,
+    q, k, v, do, o, lse, h1, xp, vec, wq, wk, wv, g1, slot, early_ref, done_ref, own_in, plane_in, gout_in,
+    gtok, gup_out, gdn_out, gqkv_out, gout_out, early_out, late_out,
+    h1t, dh1, dqt, dkv, gtp, late,
+    own, plane, fside, flast, fdepth, ffin,
+    onear, oacc, oside, olast, odepth, ofin,
+    gg, gnear, gside, glast, gdepth, gfin,
+    send, recv, local,
+    enear, edepth, lnear, ldepth, es1, er1, es2, er2, ls1, lr1, ls2, lr2,
+):
+    t = pl.program_id(0)
+    groups = pl.num_programs(0)
+    length, width = h1.shape
+    share = width // shards
+    chips = shards // 2
+    cols = pl.ds(pl.multiple_of(t * LANES, LANES), LANES)
+    place = Place()
+    rep = lax.axis_index("rep")
+    core = place.me % 2
+    sems = lambda n: (send.at[n], recv.at[n])
+    make = functools.partial(Unit, place, rep, reps)
+    u2 = make(None, own.at[pl.ds(0, 1)], None, None, None, fdepth.at[0], ffin.at[0], *sems(0))
+    u3 = make(None, own.at[pl.ds(1, 1)], None, None, None, fdepth.at[1], ffin.at[1], *sems(1))
+    u4 = make(None, plane, None, fside, flast, fdepth.at[2], ffin.at[2], *sems(2))
+    uo = make(gout_in.at[1 - core], oacc, onear, oside, olast, odepth, ofin, *sems(3))
+    parts = []
+    for n in range(5):
+        parts.append(
+            make(
+                gg.at[n, 1 - core], gg.at[n, core], gnear.at[n], gside.at[n], glast.at[n], gdepth.at[n],
+                gfin.at[n], *sems(4 + n)
+            )
+        )
+    loads = [
+        pltpu.make_async_copy(own_in, own, local.at[0]),
+        pltpu.make_async_copy(plane_in, plane, local.at[1]),
+        pltpu.make_async_copy(gout_in.at[core], oacc, local.at[2]),
+    ]
+    early = Small(place.me, shards, rep, reps, early_ref, enear, edepth, early_out, (es1, er1, es2, er2))
+    later = Small(place.me, shards, rep, reps, late, lnear, ldepth, late_out, (ls1, lr1, ls2, lr2))
+
+    @pl.when(t == 0)
+    def _():
+        for x in loads:
+            x.start()
+        transpose_rows(h1, h1t)
+        dh1[...] = jnp.zeros_like(dh1)
+        late[...] = jnp.zeros_like(late)
+        greet(place.me, shards, rep, reps)
+        loads[0].wait()
+        u2.depth_start()
+        loads[1].wait()
+        u4.side_start()
+        uo.near_start()
+        loads[2].wait()
+        early.start()
+
+    heads = Heads(few, q, k, v, do, o, lse, dqt, dkv)
+    blocks = length // heads.step
+
+    plan = [
+        (1, uo.near_sum), (2, early.middle), (4, u2.depth_sum), (4, u3.depth_start), (4, u4.side_sum),
+        (6, early.finish), (6, uo.side_sum), (7, u4.last_sum), (8, u3.depth_sum), (9, uo.last_sum),
+        (12, u4.depth_sum), (13, uo.depth_sum),
+    ]
+    for n in range(4):
+        first = 4 * (n + 1)
+        plan += [(first + 1, parts[n].near_sum), (first + 3, parts[n].side_sum)]
+        if n < 3:
+            plan += [(first + 5, parts[n].last_sum)]
+        if n < 2:
+            plan += [(first + 7, parts[n].depth_sum)]
+
+    def body(i, _):
+        for at, step in plan:
+            pl.when(t * blocks + i == at)(step)
+        heads.keys(i)
+        return 0
+
+    lax.fori_loop(0, blocks, body, 0)
+    dq, gq, gk, gv = group_weights(few, dqt, dkv, h1t, late, cols)
+    for n, part in enumerate((gq, gk, gv)):
+        for s in range(shards):
+            gg[t, s % 2, s // 2, n * share : (n + 1) * share, :] = part[s * share : (s + 1) * share, :]
+    for s in range(shards):
+        gg[t, s % 2, s // 2, 3 * share :, :] = jnp.zeros((GROUP_ROWS - 3 * share, LANES), BF16)
+    for n in range(5):
+        pl.when(t == n)(parts[n].near_start)
+    group_inputs(few, dq, dkv, wq, wk, wv, dh1)
+
+    @pl.when(t == groups - 1)
+    def _():
+        parts[4].near_sum()
+        parts[3].last_sum()
+        parts[2].depth_sum()
+        back_finish(few, dh1, xp, vec, g1, late, gtp)
+        later.start()
+        parts[4].side_sum()
+        parts[3].depth_sum()
+        unpermute(slot[0:1, :], gtp, gtok)
+        parts[4].last_sum()
+        later.middle()
+        for n in range(CHUNKS):
+            if n >= 2:
+                (u2, u3, u4)[n - 2].finish()
+            src = done_ref.at[n] if n < 2 else ffin.at[n - 2]
+            for b in range(shards):
+                gup_out[:, b * width + n * LANES : b * width + (n + 1) * LANES] = src[
+                    b * share : (b + 1) * share, :
+                ].astype(F32)
+            gdn_out[n * LANES : (n + 1) * LANES, :] = jnp.transpose(src[width:, :].astype(F32))
+        uo.finish()
+        for b in range(CHUNKS):
+            gout_out[:, b * LANES : (b + 1) * LANES] = ofin[b * share : (b + 1) * share, :].astype(F32)
+        parts[4].depth_sum()
+        later.finish()
+        for n in range(5):
+            parts[n].finish()
+            for m in range(3):
+                gqkv_out[:, m * width + n * LANES : m * width + (n + 1) * LANES] = gfin[
+                    n, m * share : (m + 1) * share, :
+                ].astype(F32)
+            parts[n].a.wait_send()
+        uo.a.wait_send()
+
+
+def back_reduce(few, shards, reps, qkv, do, o, lse, h1, xp, vecs, wqkv, g1, slot, early, done, own, plane, gout):
+    length, width = h1.shape
+    share = width // shards
+    chips = shards // 2
+    rows = 2 * width
+    groups = width // LANES
+    hidden = shards * width
+    sds = jax.ShapeDtypeStruct
+    whole, cols, in_specs, scratch = back_specs(few, length, width)
+    hbm = pl.BlockSpec(memory_space=pl.ANY)
+    dma = pltpu.SemaphoreType.DMA
+    vm = lambda *shape: pltpu.VMEM(shape + (LANES,), BF16)
+    spare = gout.shape[2]
+
+    def buffers(rows):
+        return [vm(4, rows // 2), vm(2, rows // 2), vm(reps - 1, rows // 4), vm(rows)]
+
+    many = lambda n, refs: [pltpu.VMEM((n,) + r.shape, BF16) for r in refs]
+    fside, flast, fdepth, ffin = buffers(rows)
+    return pl.pallas_call(
+        functools.partial(back_reduce_kernel, few, shards, reps),
+        grid=(groups,),
+        in_specs=in_specs + [whole(16, width), whole(2, rows, LANES), hbm, hbm, hbm],
+        out_specs=[
+            whole(length, width), whole(share, hidden), whole(width, width), whole(share, 3 * width),
+            whole(share, width), whole(16, width), whole(8, width),
+        ],
+        out_shape=(
+            sds((length, width), BF16),
+            sds((share, hidden), F32),
+            sds((width, width), F32),
+            sds((share, 3 * width), F32),
+            sds((share, width), F32),
+            sds((16, width), F32),
+            sds((8, width), F32),
+        ),
+        scratch_shapes=scratch
+        + [
+            pltpu.VMEM((8, width), F32),
+            vm(2, rows), vm(chips, rows), fside, flast,
+        ]
+        + many(3, [fdepth, ffin])
+        + [vm(chips, spare), vm(chips, spare)] + buffers(spare)
+        + [vm(5, 2, chips, GROUP_ROWS), vm(5, chips, GROUP_ROWS)] + many(5, buffers(GROUP_ROWS))
+        + [
+            dma((9, Unit.COPIES)), dma((9, Unit.COPIES)), dma((3,)),
+            pltpu.VMEM((shards, 16, width), F32),
+            pltpu.VMEM((reps, 16, width), F32),
+            pltpu.VMEM((shards, 8, width), F32),
+            pltpu.VMEM((reps, 8, width), F32),
+            dma((shards - 1,)), dma((shards - 1,)), dma((reps - 1,)), dma((reps - 1,)),
+            dma((shards - 1,)), dma((shards - 1,)), dma((reps - 1,)), dma((reps - 1,)),
+        ],
+        compiler_params=pltpu.CompilerParams(
+            vmem_limit_bytes=60 * MB, collective_id=4, has_side_effects=True
+        ),
+        name="back_reduce",
+    )(qkv, qkv, qkv, do, o, lse, h1, xp, vecs, wqkv, wqkv, wqkv, g1, slot, early, done, own, plane, gout)
+
+
 def local(
     reps, shards,
     tokens, masked, cotangent, norm1_gain, norm1_shift, w_qkv, bias_query, bias_value, w_out,
@@ -1055,7 +1535,7 @@
             )
             if close:
                 gtok, gup, gdn, gqkv, gout, early, late = reduce_backward(
-                    few, shards, reps, 1 if few == FEW else 2,
+                    few, shards, reps, 1,
                     qkv, do, o, lse, h1, xp, vecs, wqkv, g1, slot, early, gout, gup, gdn,
                 )
                 return res, gtok, gup, gdn, gqkv, gout, early, late
@@ -1066,7 +1546,18 @@
 
         return run
 
-    res, gtok, *grads, early, late = lax.cond(small_enough, backward(FEW), backward(length))
+    if close:
+        res, g1, do, part, early, done, own, plane = ffn_reduce(
+            FEW, shards, reps, x1, cot, slot, mask, vecs, bup, wup, wdn, wout, o
+        )
+        short = (res,) + tuple(
+            back_reduce(
+                FEW, shards, reps, qkv, do, o, lse, h1, xp, vecs, wqkv, g1, slot, early, done, own, plane, part
+            )
+        )
+    res, gtok, *grads, early, late = lax.cond(
+        small_enough, (lambda: short) if close else backward(FEW), backward(length)
+    )
 
     if close:
         gup, gdn, gqkv, gout = grads

time: 315 us -> 292 us (0.927)
  Pallas kernels: 287 us -> 270 us
  loops' own time: 10 us -> 1.22 us
    pallas_call x2, Pallas kernels: 195 us -> 177 us  [the longest x1 107 us: back_reduce(): pl.pallas_call(functools.partial(back_reduce_kernel, few, shards, reps),...]
    another operation x1, loops' own time: 10 us -> 1.22 us  [local(): lax.cond(small_enough, (lambda: short) if close else backward(FEW), backw...]
    unnamed x15 -> x16, local copies, waits for them, and re-layouts: 7.32 us -> 8.63 us
where the time goes in v4:
time: 292 us; the launch traced here: 288 us
  Pallas kernels  270 us (92%)
  local copies, waits for them, and re-layouts  12.9 us (4%)
    pallas_call x1, Pallas kernels, back_reduce(): pl.pallas_call(functools.partial(back_reduce_kernel, few, shards, reps),...  107 us
    pallas_call x1, Pallas kernels, gather_attn(): pl.pallas_call(functools.partial(gather_attn_kernel, reps), in_specs=[vme...  93.1 us
    pallas_call x1, Pallas kernels, ffn_reduce(): pl.pallas_call(functools.partial(ffn_reduce_kernel, few, shards, reps), g...  70.5 us
    unnamed x16, local copies, waits for them, and re-layouts  8.63 us

profile of v4, /device:TPU:0, one launch (start us, length us, event | category | flops | bytes accessed | tf_op | source)
XLA Modules:
  0.0 288.1 jit_solution(7871367163485228782)
XLA Ops:
  0.6 0.7 convert_element_type.13.mask_ref
  1.3 0.8 stack.35
  2.1 1.3 fusion.2.pack_ref
  3.4 93.1 %gather_attn.1 = (f32[8,1024]{1,0:T(8,128)}, bf16[1024,640]{1,0:T(8,128)(2,1)}, bf16[1024,640]{1,0:T(8,128)(2,1)}, bf16[1024,1920]{1,0:T(8,128)(2,1)S(1)}, bf16[...) custom-call(bf16[1024,640]{1,0:T(8,128)(2,1)} %bitcast.38, ...), custom_call_target="tpu_custom_call" | custom-call | tf_op jit(solution)/shard_map/gather_attn/pallas_call | solution.py:356
  97.0 70.5 %ffn_reduce.1 = (bf16[1024,640]{1,0:T(8,128)(2,1)}, f32[384,640]{1,0:T(8,128)}, bf16[384,640]{1,0:T(8,128)(2,1)}, bf16[2,4,448,128]{3,2,1,0:T(8,128)(2,1)}, f32[...) custom-call(f32[1024,640]{1,0:T(8,128)} %get-tuple-element.128.x1_re, ...), custom_call_target="tpu_custom_call" | custom-call | tf_op jit(solution)/shard_map/ffn_reduce/pallas_call | solution.py:1255
  167.5 106.9 %back_reduce.1 = (bf16[1024,640]{1,0:T(8,128)(2,1)}, f32[80,5120]{1,0:T(8,128)}, f32[640,640]{1,0:T(8,128)}, f32[80,1920]{1,0:T(8,128)}, f32[80,640]{1,0:T(8,128)}, /*index=5*/f32[16,640]{1,0:T(8,128)}, f32[8,640]{1,0:T(8,128)}) custom-call(bf16[1024,1920]{1,0:T(8,128)(2,1)S(1)} %get-tuple-element.136.q.k.v, ...), custom_call_target="tpu_custom_call" | custom-call | tf_op jit(solution)/shard_map/back_reduce/pallas_call | solution.py:1451
  274.4 1.2 conditional.1
  275.7 0.0 copy-start.2
  275.7 0.8 slice.37
  276.5 0.7 slice.38
  277.2 0.1 fusion.3
  277.3 0.5 slice_bitcast_fusion
  277.9 0.7 slice.46
  278.6 0.7 dynamic_slice.7
  279.3 2.5 copy.53
  281.8 0.0 copy-done.2
  281.8 1.1 copy.54
  282.8 0.4 copy-done.3
  283.2 0.8 copy.55
  284.0 0.0 copy-done.4
  284.0 0.7 copy.56
  284.7 1.2 copy.57
  285.9 0.9 copy-done.1
  286.7 1.2 copy.58
  (6 shorter events, 0.0 us)
Async XLA Ops:
  275.7 6.1 %copy-start.2 = (bf16[1024,640]{1,0:T(8,128)(2,1)S(1)}, bf16[1024,640]{1,0:T(8,128)(2,1)}, u32[]{:S(2)}) copy-start(bf16[1024,640]{1,0:T(8,128)(2,1)} %get-tuple-element.157) | copy-start | bytes 3932164
  281.8 1.5 copy-start.3
  281.8 2.3 copy-start.4
  281.8 3.0 %copy-start = (f32[80,5120]{1,0:T(8,128)S(1)}, f32[80,5120]{1,0:T(8,128)}, u32[]{:S(2)}) copy-start(f32[80,5120]{1,0:T(8,128)} %get-tuple-element.214) | copy-start | bytes 4915204
  284.7 2.0 copy-start.1

commit v5 on v4

--- a/solution.py
+++ b/solution.py
@@ -1032,18 +1032,14 @@
 
 
 class Unit:
-    COPIES = 13
-
-    def __init__(self, place, rep, reps, other, acc, near, side, last, depth, fin, send, recv):
-        self.rep, self.reps = rep, reps
-        self.acc, self.near, self.side, self.last, self.depth, self.fin = acc, near, side, last, depth, fin
+    COPIES = 10
+
+    def __init__(self, place, rep, other, acc, near, side, last, own, depth, fin, send, recv):
+        self.acc, self.near, self.side, self.last = acc, near, side, last
+        self.own, self.depth, self.fin = own, depth, fin
         chip = place.me // 2
         cx, cy, cd = place.xn // 2, place.yn // 2, place.dg // 2
         self.chip, self.cx, self.cy = chip, cx, cy
-        self.rows = rows = acc.shape[1]
-        half, self.quarter = rows // 2, rows // 4
-        low, high = pl.ds(0, half), pl.ds(half, half)
-        self.low, self.high = low, high
         fsdp = lambda d: {"fsdp": d}
 
         def copy(i, src, dst, to):
@@ -1052,6 +1048,8 @@
         if other is not None:
             self.a = copy(0, other, near, fsdp(place.sib))
         if side is not None:
+            half = acc.shape[1] // 2
+            self.low, self.high = low, high = pl.ds(0, half), pl.ds(half, half)
             self.b = [
                 copy(1, acc.at[cd, low], side.at[1], fsdp(place.xn)),
                 copy(2, acc.at[cd, high], side.at[3], fsdp(place.yn)),
@@ -1062,18 +1060,15 @@
                 copy(5, acc.at[cy, low], last.at[0], fsdp(place.yn)),
                 copy(6, acc.at[cx, high], last.at[1], fsdp(place.xn)),
             ]
+        if own is None:
+            self.own = own = acc.at[chip]
         if depth is not None:
-            peers = [(rep + d) % reps for d in range(1, reps)]
-            own = acc.at[chip] if other is not None or side is not None else acc.at[0]
-            self.own = own
-            self.d = [copy(7 + i, own.at[self.part(z)], depth.at[i], {"rep": z}) for i, z in enumerate(peers)]
-            self.e = [
-                copy(10 + i, fin.at[self.part(rep)], fin.at[self.part(rep)], {"rep": z})
-                for i, z in enumerate(peers)
-            ]
-
-    def part(self, z):
-        return pl.ds(pl.multiple_of(z * self.quarter, 16), self.quarter)
+            inner = (rep == 1) | (rep == 2)
+            self.inner, self.outer = inner, jnp.logical_not(inner)
+            pair = {"rep": rep + 1 - 2 * (rep % 2)}
+            self.d = copy(7, own, depth.at[0], pair)
+            self.e = copy(8, own, depth.at[1], {"rep": 3 - rep})
+            self.f = copy(9, fin, fin, pair)
 
     def near_start(self):
         self.a.start()
@@ -1112,27 +1107,48 @@
         self.add(self.chip, self.low, self.last.at[0])
         self.add(self.chip, self.high, self.last.at[1])
 
-    def depth_start(self):
-        for x in self.d:
-            x.start()
+    def z1_start(self):
+        pl.when(self.outer)(self.d.start)
 
     def last_sum(self):
         self.last_add()
-        self.depth_start()
-
-    def depth_sum(self):
-        mine = self.part(self.rep)
-        total = self.own[mine, :].astype(F32)
-        for i in range(self.reps - 1):
-            self.d[i].wait()
-            total = total + self.depth[i].astype(F32)
-        self.fin[mine, :] = total.astype(BF16)
-        for x in self.e:
-            x.start()
-
-    def finish(self):
-        for x in self.e:
-            x.wait()
+        self.z1_start()
+
+    def z1_done(self):
+        pl.when(self.outer)(self.d.wait_send)
+
+        @pl.when(self.inner)
+        def _():
+            self.d.wait_recv()
+            self.own[...] = self.own[...] + self.depth[0]
+
+    def z2_start(self):
+        pl.when(self.inner)(self.e.start)
+
+    def z1z2(self):
+        self.z1_done()
+        self.z2_start()
+
+    def z2z3(self):
+        @pl.when(self.inner)
+        def _():
+            self.e.wait()
+            self.fin[...] = self.own[...] + self.depth[1]
+            self.f.start()
+
+    def z3_done(self):
+        pl.when(self.inner)(self.f.wait_send)
+        pl.when(self.outer)(self.f.wait_recv)
+
+
+def per_shard(rows, shards, share):
+    out = []
+    for n in range(shards):
+        at = lax.broadcasted_iota(jnp.int32, (rows.shape[1], LANES), 0) - n * share
+        lane = lax.broadcasted_iota(jnp.int32, (rows.shape[1], LANES), 1)
+        spot = jnp.where((at == lane) & (lane < share), 1.0, 0.0).astype(BF16)
+        out.append(dot(rows, spot).astype(BF16))
+    return out
 
 
 def greet(me, shards, rep, reps):
@@ -1154,8 +1170,8 @@
 ):
     bups, wups, wdns = refs[:shards], refs[shards : 2 * shards], refs[2 * shards : 3 * shards]
     (
-        res_ref, g1_ref, do_ref, gout_ref, small_ref, fin_ref, own_ref, plane_ref,
-        acc, h2, h2t, gy, gyt, dh2, outp, g, near, side, last, depth, fin, send, recv,
+        res_ref, g1_ref, do_ref, gout_ref, state_ref, plane_ref,
+        acc, h2, h2t, gy, gyt, dh2, outp, small_ref, g, near, side, last, depth, fin, send, recv,
     ) = refs[3 * shards :]
     j = pl.program_id(0)
     length, width = x1_ref.shape
@@ -1166,13 +1182,13 @@
     core = place.me % 2
     units = []
     for u in range(CHUNKS):
+        xy = u < 4
         z = u < 2
-        xy = u < 4
         units.append(
             Unit(
-                place, rep, reps, g.at[u, 1 - core], g.at[u, core], near.at[u],
-                side.at[u] if xy else None, last.at[u] if xy else None,
-                depth.at[u] if z else None, fin.at[u] if z else None, send.at[u], recv.at[u],
+                place, rep, g.at[u, 1 - core], g.at[u, core], near.at[u],
+                side.at[u] if xy else None, last.at[u] if xy else None, None,
+                depth.at[u] if z else None, fin if z else None, send.at[u], recv.at[u],
             )
         )
 
@@ -1187,9 +1203,6 @@
         greet(place.me, shards, rep, reps)
         ffn_start(blocks, x1_ref, cot_ref, slot_ref, mask_ref, vec_ref, acc, h2, h2t, gy, gyt, dh2)
 
-    at(2, units[0].last_sum)
-    at(3, units[1].last_sum, units[0].depth_sum)
-    at(4, units[2].last_add, units[1].depth_sum)
     wup = jnp.concatenate([w[...] for w in wups], axis=1)
     wdn = jnp.concatenate([w[...] for w in wdns], axis=0)
     bup = jnp.concatenate([b[...] for b in bups], axis=1)
@@ -1210,11 +1223,15 @@
             for u in range(CHUNKS):
                 at(u, units[u].near_start)
         if n == 1:
-            for u in range(4):
-                at(u + 1, units[u].side_sum)
+            at(2, units[0].last_sum)
+            at(3, units[0].z1z2, units[1].last_sum)
+            at(4, units[0].z2z3, units[2].last_add)
         if n == 2:
-            for u in range(4):
-                at(u, units[u].near_sum)
+            for u in range(CHUNKS):
+                if u:
+                    at(u, units[u - 1].side_sum)
+                at(u, units[u].near_sum if u < 4 else units[u].near_add)
+            at(4, units[1].z1_done)
 
     @pl.when(j == CHUNKS - 1)
     def _():
@@ -1226,16 +1243,21 @@
                 gout_ref[s % 2, s // 2, b * share : (b + 1) * share, :] = gout[
                     s * share : (s + 1) * share, b * LANES : (b + 1) * LANES
                 ].astype(BF16)
-            spare = gout_ref.shape[2] - CHUNKS * share
-            gout_ref[s % 2, s // 2, CHUNKS * share :, :] = jnp.zeros((spare, LANES), BF16)
-        units[4].near_add()
+        rows = CHUNKS * share
+        vectors = per_shard(small_ref[8:16, :].astype(BF16), shards, share)
+        for s in range(shards):
+            gout_ref[s % 2, s // 2, rows : rows + 8, :] = vectors[s]
+            bias = [small_ref[s : s + 1, b * LANES : (b + 1) * LANES] for b in range(CHUNKS)]
+            bias = jnp.concatenate(bias + [jnp.zeros((8 - CHUNKS, LANES), F32)], axis=0)
+            gout_ref[s % 2, s // 2, rows + 8 : rows + 16, :] = bias.astype(BF16)
+            spare = gout_ref.shape[2] - rows - 16
+            gout_ref[s % 2, s // 2, rows + 16 :, :] = jnp.zeros((spare, LANES), BF16)
         plane_ref[...] = g[4, core]
         units[3].last_add()
-        for n, u in enumerate((2, 3)):
-            own_ref[n] = g[u, core, units[u].chip]
-        for u in range(2):
-            units[u].finish()
-            fin_ref[u] = fin[u]
+        for u in range(1, 4):
+            state_ref[u] = g[u, core, units[u].chip]
+        units[0].z3_done()
+        state_ref[0] = fin[...]
         for u in range(CHUNKS):
             units[u].a.wait_send()
 
@@ -1264,16 +1286,14 @@
         + [pick(s, (LANES, width), False) for s in range(shards)],
         out_specs=[
             whole(length, width), whole(few, width), whole(few, width), whole(2, chips, spare, LANES),
-            whole(16, width), whole(2, rows, LANES), whole(2, rows, LANES), whole(chips, rows, LANES),
+            whole(4, rows, LANES), whole(chips, rows, LANES),
         ],
         out_shape=(
             sds((length, width), BF16),
             sds((few, width), F32),
             sds((few, width), BF16),
             sds((2, chips, spare, LANES), BF16),
-            sds((16, width), F32),
-            sds((2, rows, LANES), BF16),
-            sds((2, rows, LANES), BF16),
+            sds((4, rows, LANES), BF16),
             sds((chips, rows, LANES), BF16),
         ),
         scratch_shapes=[
@@ -1284,12 +1304,13 @@
             pltpu.VMEM((width, few), BF16),
             pltpu.VMEM((few, width), F32),
             pltpu.VMEM((length, width), BF16),
+            pltpu.VMEM((16, width), F32),
             pltpu.VMEM((CHUNKS, 2, chips, rows, LANES), BF16),
             pltpu.VMEM((CHUNKS, chips, rows, LANES), BF16),
             pltpu.VMEM((4, 4, rows // 2, LANES), BF16),
             pltpu.VMEM((4, 2, rows // 2, LANES), BF16),
-            pltpu.VMEM((2, reps - 1, rows // 4, LANES), BF16),
-            pltpu.VMEM((2, rows, LANES), BF16),
+            pltpu.VMEM((2, 2, rows, LANES), BF16),
+            pltpu.VMEM((rows, LANES), BF16),
             dma((CHUNKS, Unit.COPIES)), dma((CHUNKS, Unit.COPIES)),
         ],
         compiler_params=pltpu.CompilerParams(
@@ -1304,77 +1325,81 @@
 
 def back_reduce_kernel(
     few, shards, reps,
-    q, k, v, do, o, lse, h1, xp, vec, wq, wk, wv, g1, slot, early_ref, done_ref, own_in, plane_in, gout_in,
-    gtok, gup_out, gdn_out, gqkv_out, gout_out, early_out, late_out,
+    q, k, v, do, o, lse, h1, xp, vec, wq, wk, wv, g1, slot, state_in, plane_in, gout_in,
+    gtok, gup_out, gdn_out, gqkv_out, gout_out, vec_out,
     h1t, dh1, dqt, dkv, gtp, late,
     own, plane, fside, flast, fdepth, ffin,
     onear, oacc, oside, olast, odepth, ofin,
     gg, gnear, gside, glast, gdepth, gfin,
+    sg, snear, sside, slast, sdepth, sfin,
     send, recv, local,
-    enear, edepth, lnear, ldepth, es1, er1, es2, er2, ls1, lr1, ls2, lr2,
 ):
     t = pl.program_id(0)
     groups = pl.num_programs(0)
     length, width = h1.shape
     share = width // shards
-    chips = shards // 2
     cols = pl.ds(pl.multiple_of(t * LANES, LANES), LANES)
     place = Place()
     rep = lax.axis_index("rep")
     core = place.me % 2
     sems = lambda n: (send.at[n], recv.at[n])
-    make = functools.partial(Unit, place, rep, reps)
-    u2 = make(None, own.at[pl.ds(0, 1)], None, None, None, fdepth.at[0], ffin.at[0], *sems(0))
-    u3 = make(None, own.at[pl.ds(1, 1)], None, None, None, fdepth.at[1], ffin.at[1], *sems(1))
-    u4 = make(None, plane, None, fside, flast, fdepth.at[2], ffin.at[2], *sems(2))
-    uo = make(gout_in.at[1 - core], oacc, onear, oside, olast, odepth, ofin, *sems(3))
-    parts = []
-    for n in range(5):
-        parts.append(
-            make(
-                gg.at[n, 1 - core], gg.at[n, core], gnear.at[n], gside.at[n], glast.at[n], gdepth.at[n],
-                gfin.at[n], *sems(4 + n)
-            )
+    make = functools.partial(Unit, place, rep)
+    u1, u2, u3 = [
+        make(None, own, None, None, None, own.at[n], fdepth.at[n - 1], ffin.at[n - 1], *sems(n - 1))
+        for n in range(1, 4)
+    ]
+    u4 = make(None, plane, None, fside, flast, None, fdepth.at[3], ffin.at[3], *sems(3))
+    uo = make(gout_in.at[1 - core], oacc, onear, oside, olast, None, odepth, ofin, *sems(4))
+    us = make(sg.at[1 - core], sg.at[core], snear, sside, slast, None, sdepth, sfin, *sems(5))
+    parts = [
+        make(
+            gg.at[n, 1 - core], gg.at[n, core], gnear.at[n], gside.at[n], glast.at[n], None, gdepth.at[n],
+            gfin.at[n], *sems(6 + n)
         )
+        for n in range(5)
+    ]
     loads = [
-        pltpu.make_async_copy(own_in, own, local.at[0]),
+        pltpu.make_async_copy(state_in, own, local.at[0]),
         pltpu.make_async_copy(plane_in, plane, local.at[1]),
         pltpu.make_async_copy(gout_in.at[core], oacc, local.at[2]),
     ]
-    early = Small(place.me, shards, rep, reps, early_ref, enear, edepth, early_out, (es1, er1, es2, er2))
-    later = Small(place.me, shards, rep, reps, late, lnear, ldepth, late_out, (ls1, lr1, ls2, lr2))
 
     @pl.when(t == 0)
     def _():
         for x in loads:
             x.start()
-        transpose_rows(h1, h1t)
-        dh1[...] = jnp.zeros_like(dh1)
-        late[...] = jnp.zeros_like(late)
         greet(place.me, shards, rep, reps)
         loads[0].wait()
-        u2.depth_start()
+        u1.z2_start()
+        u2.z1_start()
         loads[1].wait()
         u4.side_start()
         uo.near_start()
         loads[2].wait()
-        early.start()
+        transpose_rows(h1, h1t)
+        dh1[...] = jnp.zeros_like(dh1)
+        late[...] = jnp.zeros_like(late)
 
     heads = Heads(few, q, k, v, do, o, lse, dqt, dkv)
     blocks = length // heads.step
 
     plan = [
-        (1, uo.near_sum), (2, early.middle), (4, u2.depth_sum), (4, u3.depth_start), (4, u4.side_sum),
-        (6, early.finish), (6, uo.side_sum), (7, u4.last_sum), (8, u3.depth_sum), (9, uo.last_sum),
-        (12, u4.depth_sum), (13, uo.depth_sum),
+        (2, uo.near_sum),
+        (5, u1.z2z3), (5, u2.z1z2), (5, u3.z1_start), (5, u4.side_sum), (7, uo.side_sum),
+        (9, u4.last_add), (10, u1.z3_done), (10, u2.z2z3), (10, u3.z1z2), (10, u4.z1_start),
+        (11, uo.last_sum), (13, uo.z1z2), (15, u2.z3_done), (15, u3.z2z3), (15, u4.z1z2), (16, uo.z2z3),
+        (18, uo.z3_done), (19, u3.z3_done), (19, u4.z2z3),
     ]
-    for n in range(4):
-        first = 4 * (n + 1)
-        plan += [(first + 1, parts[n].near_sum), (first + 3, parts[n].side_sum)]
-        if n < 3:
-            plan += [(first + 5, parts[n].last_sum)]
-        if n < 2:
-            plan += [(first + 7, parts[n].depth_sum)]
+    chain = ("near_sum", "side_sum", "last_sum", "z1z2", "z2z3")
+    rest = [[] for _ in range(5)]
+    for n in range(5):
+        for when, name in zip((2, 5, 7, 9, 11), chain):
+            slot_at = 4 * (n + 1) + when
+            if slot_at < 20:
+                plan.append((slot_at, getattr(parts[n], name)))
+            else:
+                rest[n].append(getattr(parts[n], name))
+    plan.sort(key=lambda entry: entry[0])
 
     def body(i, _):
         for at, step in plan:
@@ -1393,43 +1418,68 @@
         pl.when(t == n)(parts[n].near_start)
     group_inputs(few, dq, dkv, wq, wk, wv, dh1)
 
+    def step(n):
+        if rest[n]:
+            rest[n].pop(0)()
+
     @pl.when(t == groups - 1)
     def _():
-        parts[4].near_sum()
-        parts[3].last_sum()
-        parts[2].depth_sum()
+        step(4)
+        step(3)
+        step(2)
+        step(1)
         back_finish(few, dh1, xp, vec, g1, late, gtp)
-        later.start()
-        parts[4].side_sum()
-        parts[3].depth_sum()
+        vectors = per_shard(jnp.concatenate([late[...], jnp.zeros_like(late)], axis=0).astype(BF16), shards, share)
+        for s in range(shards):
+            sg[s % 2, s // 2, :16, :] = vectors[s]
+            sg[s % 2, s // 2, 16:, :] = jnp.zeros((SMALL_ROWS - 16, LANES), BF16)
+        us.near_start()
+        step(4)
+        step(3)
+        step(2)
+        step(1)
+        us.near_sum()
         unpermute(slot[0:1, :], gtp, gtok)
-        parts[4].last_sum()
-        later.middle()
+        step(4)
+        step(3)
+        step(2)
+        us.side_sum()
+        u4.z3_done()
         for n in range(CHUNKS):
-            if n >= 2:
-                (u2, u3, u4)[n - 2].finish()
-            src = done_ref.at[n] if n < 2 else ffin.at[n - 2]
+            src = ffin.at[n - 1] if n else own.at[0]
             for b in range(shards):
                 gup_out[:, b * width + n * LANES : b * width + (n + 1) * LANES] = src[
                     b * share : (b + 1) * share, :
                 ].astype(F32)
             gdn_out[n * LANES : (n + 1) * LANES, :] = jnp.transpose(src[width:, :].astype(F32))
-        uo.finish()
+        step(4)
+        step(3)
+        us.last_sum()
         for b in range(CHUNKS):
             gout_out[:, b * LANES : (b + 1) * LANES] = ofin[b * share : (b + 1) * share, :].astype(F32)
-        parts[4].depth_sum()
-        later.finish()
+        vec_out[0:16, :] = ofin[CHUNKS * share : CHUNKS * share + 16, :].astype(F32)
+        step(3)
+        us.z1z2()
+        step(4)
+        us.z2z3()
         for n in range(5):
-            parts[n].finish()
+            assert not rest[n]
+            parts[n].z3_done()
             for m in range(3):
                 gqkv_out[:, m * width + n * LANES : m * width + (n + 1) * LANES] = gfin[
                     n, m * share : (m + 1) * share, :
                 ].astype(F32)
             parts[n].a.wait_send()
+        us.z3_done()
+        vec_out[16:32, :] = sfin[0:16, :].astype(F32)
         uo.a.wait_send()
-
-
-def back_reduce(few, shards, reps, qkv, do, o, lse, h1, xp, vecs, wqkv, g1, slot, early, done, own, plane, gout):
+        us.a.wait_send()
+
+
+SMALL_ROWS = 32
+
+
+def back_reduce(few, shards, reps, qkv, do, o, lse, h1, xp, vecs, wqkv, g1, slot, state, plane, gout):
     length, width = h1.shape
     share = width // shards
     chips = shards // 2
@@ -1444,17 +1494,17 @@
     spare = gout.shape[2]
 
     def buffers(rows):
-        return [vm(4, rows // 2), vm(2, rows // 2), vm(reps - 1, rows // 4), vm(rows)]
+        return [vm(4, rows // 2), vm(2, rows // 2), vm(2, rows), vm(rows)]
 
     many = lambda n, refs: [pltpu.VMEM((n,) + r.shape, BF16) for r in refs]
     fside, flast, fdepth, ffin = buffers(rows)
     return pl.pallas_call(
         functools.partial(back_reduce_kernel, few, shards, reps),
         grid=(groups,),
-        in_specs=in_specs + [whole(16, width), whole(2, rows, LANES), hbm, hbm, hbm],
+        in_specs=in_specs + [hbm, hbm, hbm],
         out_specs=[
             whole(length, width), whole(share, hidden), whole(width, width), whole(share, 3 * width),
-            whole(share, width), whole(16, width), whole(8, width),
+            whole(share, width), whole(32, LANES),
         ],
         out_shape=(
             sds((length, width), BF16),
@@ -1462,31 +1512,23 @@
             sds((width, width), F32),
             sds((share, 3 * width), F32),
             sds((share, width), F32),
-            sds((16, width), F32),
-            sds((8, width), F32),
+            sds((32, LANES), F32),
         ),
         scratch_shapes=scratch
         + [
             pltpu.VMEM((8, width), F32),
-            vm(2, rows), vm(chips, rows), fside, flast,
+            vm(4, rows), vm(chips, rows), fside, flast,
         ]
-        + many(3, [fdepth, ffin])
+        + many(4, [fdepth, ffin])
         + [vm(chips, spare), vm(chips, spare)] + buffers(spare)
         + [vm(5, 2, chips, GROUP_ROWS), vm(5, chips, GROUP_ROWS)] + many(5, buffers(GROUP_ROWS))
-        + [
-            dma((9, Unit.COPIES)), dma((9, Unit.COPIES)), dma((3,)),
-            pltpu.VMEM((shards, 16, width), F32),
-            pltpu.VMEM((reps, 16, width), F32),
-            pltpu.VMEM((shards, 8, width), F32),
-            pltpu.VMEM((reps, 8, width), F32),
-            dma((shards - 1,)), dma((shards - 1,)), dma((reps - 1,)), dma((reps - 1,)),
-            dma((shards - 1,)), dma((shards - 1,)), dma((reps - 1,)), dma((reps - 1,)),
-        ],
+        + [vm(2, chips, SMALL_ROWS), vm(chips, SMALL_ROWS)] + buffers(SMALL_ROWS)
+        + [dma((11, Unit.COPIES)), dma((11, Unit.COPIES)), dma((3,))],
         compiler_params=pltpu.CompilerParams(
             vmem_limit_bytes=60 * MB, collective_id=4, has_side_effects=True
         ),
         name="back_reduce",
-    )(qkv, qkv, qkv, do, o, lse, h1, xp, vecs, wqkv, wqkv, wqkv, g1, slot, early, done, own, plane, gout)
+    )(qkv, qkv, qkv, do, o, lse, h1, xp, vecs, wqkv, wqkv, wqkv, g1, slot, state, plane, gout)
 
 
 def local(
@@ -1497,7 +1539,7 @@
     seqs, length, width = tokens.shape
     hidden = w_up.shape[1]
     share = w_qkv.shape[0]
-    close = shards == 8 and share % 16 == 0 and share <= LANES and w_down.shape[0] == width
+    close = shards == 8 and reps == 4 and share % 16 == 0 and share <= LANES and w_down.shape[0] == width
     x = tokens.reshape(seqs * length, width)
     cot = cotangent.reshape(seqs * length, width)
     mask = masked.astype(F32)
@@ -1546,37 +1588,46 @@
 
         return run
 
+    me = lax.axis_index("fsdp")
+    own = bias_up.shape[0]
+
+    def pick(late, early):
+        gbup = lax.dynamic_slice_in_dim(early[:8].reshape(hidden), me * own, own)
+        return lax.dynamic_slice_in_dim(jnp.concatenate([late[:4], early[8:12]]), me * share, share, axis=1), gbup
+
     if close:
-        res, g1, do, part, early, done, own, plane = ffn_reduce(
+        res, g1, do, part, state, plane = ffn_reduce(
             FEW, shards, reps, x1, cot, slot, mask, vecs, bup, wup, wdn, wout, o
         )
-        short = (res,) + tuple(
-            back_reduce(
-                FEW, shards, reps, qkv, do, o, lse, h1, xp, vecs, wqkv, g1, slot, early, done, own, plane, part
-            )
+        gtok, gup, gdn, gqkv, gout, small = back_reduce(
+            FEW, shards, reps, qkv, do, o, lse, h1, xp, vecs, wqkv, g1, slot, state, plane, part
         )
-    res, gtok, *grads, early, late = lax.cond(
-        small_enough, (lambda: short) if close else backward(FEW), backward(length)
-    )
-
-    if close:
-        gup, gdn, gqkv, gout = grads
+
+        def redo():
+            *outs, early, late = backward(length)()
+            mine, gbup = pick(late, early)
+            rows = jnp.concatenate([mine[4:], jnp.zeros((4, share), F32)])
+            tail = jnp.concatenate([mine[:4], jnp.zeros((12, share), F32)])
+            wide = lambda x: jnp.pad(x, ((0, 0), (0, LANES - share)))
+            ups = jnp.pad(gbup.reshape(-1, LANES), ((0, 8 - own // LANES), (0, 0)))
+            return (*outs, jnp.concatenate([wide(rows), ups, wide(tail)]))
+
+        res, gtok, gup, gdn, gqkv, gout, small = lax.cond(
+            small_enough, lambda: (res, gtok, gup, gdn, gqkv, gout, small), redo
+        )
+        mine = [small[n, :share] for n in (16, 17, 18, 19, 0, 1, 2, 3)]
+        gbup = small[8 : 8 + own // LANES].reshape(own)
     else:
         def scatter(g, dim):
             part = lax.psum_scatter(g, "fsdp", scatter_dimension=dim, tiled=True)
             return lax.psum(part, "rep").astype(F32)
 
-        gup, gdn, gattn = grads
+        res, gtok, gup, gdn, gattn, early, late = lax.cond(small_enough, backward(FEW), backward(length))
         gup = scatter(gup, 0)
         gdn = scatter(gdn.transpose(0, 2, 1).reshape(hidden, width), 0)
         gattn = scatter(gattn, 0)
         gout, gqkv = gattn[:, :width], gattn[:, width:]
-        early = lax.psum(early, ("rep", "fsdp"))
-        late = lax.psum(late, ("rep", "fsdp"))
-    me = lax.axis_index("fsdp")
-    own = bias_up.shape[0]
-    gbup = lax.dynamic_slice_in_dim(early[:8].reshape(hidden), me * own, own)
-    mine = lax.dynamic_slice_in_dim(jnp.concatenate([late[:4], early[8:12]]), me * share, share, axis=1)
+        mine, gbup = pick(lax.psum(late, ("rep", "fsdp")), lax.psum(early, ("rep", "fsdp")))
     return (
         res.reshape(seqs, length, width),
         gtok.reshape(seqs, length, width),

time: 292 us -> 262 us (0.90)
  Pallas kernels: 270 us -> 242 us
    pallas_call x1, Pallas kernels: 107 us -> 80.7 us  [back_reduce(): pl.pallas_call(functools.partial(back_reduce_kernel, few, shards, reps),...]
    pallas_call x1, Pallas kernels: 70.5 us -> 67.3 us  [ffn_reduce(): pl.pallas_call(functools.partial(ffn_reduce_kernel, few, shards, reps), g...]
    unnamed x16 -> x36, local copies, waits for them, and re-layouts: 8.63 us -> 8.72 us
where the time goes in v5:
time: 262 us; the launch traced here: 258 us
  Pallas kernels  242 us (92%)
  local copies, waits for them, and re-layouts  11 us (4%)
    pallas_call x1, Pallas kernels, gather_attn(): pl.pallas_call(functools.partial(gather_attn_kernel, reps), in_specs=[vme...  94.3 us
    pallas_call x1, Pallas kernels, back_reduce(): pl.pallas_call(functools.partial(back_reduce_kernel, few, shards, reps),...  80.7 us
    pallas_call x1, Pallas kernels, ffn_reduce(): pl.pallas_call(functools.partial(ffn_reduce_kernel, few, shards, reps), g...  67.3 us
    unnamed x36, local copies, waits for them, and re-layouts  8.72 us

profile of v5, /device:TPU:0, one launch (start us, length us, event | category | flops | bytes accessed | tf_op | source)
XLA Modules:
  0.0 258.1 jit_solution(13503327034150991006)
XLA Ops:
  0.6 0.7 convert_element_type.19.mask_ref
  1.3 0.8 stack.35
  2.1 1.3 fusion.3.pack_ref
  3.4 94.3 %gather_attn.1 = (f32[8,1024]{1,0:T(8,128)}, bf16[1024,640]{1,0:T(8,128)(2,1)}, bf16[1024,640]{1,0:T(8,128)(2,1)}, bf16[1024,1920]{1,0:T(8,128)(2,1)}, bf16[1024...) custom-call(bf16[1024,640]{1,0:T(8,128)(2,1)} %bitcast.56, ...), custom_call_target="tpu_custom_call" | custom-call | tf_op jit(solution)/shard_map/gather_attn/pallas_call | solution.py:356
  98.3 67.3 %ffn_reduce.1 = (bf16[1024,640]{1,0:T(8,128)(2,1)}, f32[384,640]{1,0:T(8,128)}, bf16[384,640]{1,0:T(8,128)(2,1)}, bf16[2,4,448,128]{3,2,1,0:T(8,128)(2,1)}, bf16...) custom-call(f32[1024,640]{1,0:T(8,128)} %get-tuple-element.203.x1_ref, bf16[1024,640]{1,0:T(8,128)(2,1)} %bitcast.54, ...), custom_call_target="tpu_custom_call" | custom-call | tf_op jit(solution)/shard_map/ffn_reduce/pallas_call | solution.py:1277
  165.5 0.0 copy-done
  165.6 80.7 %back_reduce.1 = (bf16[1024,640]{1,0:T(8,128)(2,1)}, f32[80,5120]{1,0:T(8,128)}, f32[640,640]{1,0:T(8,128)}, f32[80,1920]{1,0:T(8,128)}, f32[80,640]{1,0:T(8,128)}, /*index=5*/f32[32,128]{1,0:T(8,128)}) custom-call(bf16[1024,1920]{1,0:T(8,128)(2,1)S(1)} %copy-done, bf16[1024,1920]{1,0:T(8,128)(2,1)S(1)} %copy-done, bf16[1024,1920]{1,0:T(8,128)(2,1)S(1)} %copy-done, ...), custom_call_target="tpu_custom_call" | custom-call | tf_op jit(solution)/shard_map/back_reduce/pallas_call | solution.py:1501
  246.3 2.8 %conditional.1 = (bf16[1024,640]{1,0:T(8,128)(2,1)}, bf16[1024,640]{1,0:T(8,128)(2,1)}, f32[80,5120]{1,0:T(8,128)}, f32[640,640]{1,0:T(8,128)}, f32[80,1920]{1,0...) conditional(s32[]{:T(128)} %bitcast.30, ...), branch_computations={%region_0.1_spmd, %region_1.2_spmd} | conditional | flops 648 | bytes 156380 | solution.py:1615
  247.5 0.8 slice_bitcast_fusion.9
  248.4 0.7 slice_bitcast_fusion.8
  249.1 0.0 copy-start.10
  249.1 0.0 copy-start.11
  249.1 0.0 copy-start.12
  249.1 0.0 copy-start.13
  249.1 0.0 copy-start.14
  249.1 2.6 %copy.67 = bf16[1,1024,640]{2,1,0:T(8,128)(2,1)} copy(bf16[1,1024,640]{2,1,0:T(8,128)(2,1)} %bitcast.58) | data formatting | bytes 2621440
  251.7 1.1 copy.68
  252.8 0.0 copy-done.7
  252.8 0.3 copy-done.4
  253.2 0.8 copy.69
  254.0 0.7 copy.70
  254.7 1.2 copy.71
  255.8 0.9 copy-done.2
  256.7 1.2 copy.72
  (21 shorter events, 0.0 us)
Async XLA Ops:
  98.3 67.3 %copy-start = (bf16[1024,1920]{1,0:T(8,128)(2,1)S(1)}, bf16[1024,1920]{1,0:T(8,128)(2,1)}, u32[]{:S(2)}) copy-start(bf16[1024,1920]{1,0:T(8,128)(2,1)} %get-tuple-element.211.q.k.v) | copy-start | bytes 11796484
  249.0 3.7 %copy-start.6 = (f32[640]{0:T(1024)}, f32[640]{0:T(1024)S(1)}, u32[]{:S(2)}) copy-start(f32[640]{0:T(1024)S(1)} %get-tuple-element.316) | copy-start | bytes 7684
  249.0 3.7 %copy-start.7 = (f32[80]{0:T(128)}, f32[80]{0:T(128)S(1)}, u32[]{:S(2)}) copy-start(f32[80]{0:T(128)S(1)} %get-tuple-element.318) | copy-start | bytes 964
  249.0 3.8 %copy-start.8 = (f32[80]{0:T(128)}, f32[80]{0:T(128)S(1)}, u32[]{:S(2)}) copy-start(f32[80]{0:T(128)S(1)} %get-tuple-element.314) | copy-start | bytes 964
  249.0 3.8 %copy-start.9 = (f32[80]{0:T(128)}, f32[80]{0:T(128)S(1)}, u32[]{:S(2)}) copy-start(f32[80]{0:T(128)S(1)} %get-tuple-element.313) | copy-start | bytes 964
  249.1 3.7 %copy-start.10 = (f32[80]{0:T(128)}, f32[80]{0:T(128)S(1)}, u32[]{:S(2)}) copy-start(f32[80]{0:T(128)S(1)} %get-tuple-element.312) | copy-start | bytes 964
  249.1 3.7 %copy-start.11 = (f32[80]{0:T(128)}, f32[80]{0:T(128)S(1)}, u32[]{:S(2)}) copy-start(f32[80]{0:T(128)S(1)} %get-tuple-element.310) | copy-start | bytes 964
  249.1 3.7 %copy-start.12 = (f32[80]{0:T(128)}, f32[80]{0:T(128)S(1)}, u32[]{:S(2)}) copy-start(f32[80]{0:T(128)S(1)} %get-tuple-element.309) | copy-start | bytes 964
  249.1 3.7 %copy-start.13 = (f32[80]{0:T(128)}, f32[80]{0:T(128)S(1)}, u32[]{:S(2)}) copy-start(f32[80]{0:T(128)S(1)} %get-tuple-element.307) | copy-start | bytes 964
  249.1 3.7 %copy-start.14 = (f32[80]{0:T(128)}, f32[80]{0:T(128)S(1)}, u32[]{:S(2)}) copy-start(f32[80]{0:T(128)S(1)} %get-tuple-element.306) | copy-start | bytes 964
  249.1 2.6 %copy-start.3 = (bf16[1024,640]{1,0:T(8,128)(2,1)S(1)}, bf16[1024,640]{1,0:T(8,128)(2,1)}, u32[]{:S(2)}) copy-start(bf16[1024,640]{1,0:T(8,128)(2,1)} %get-tuple-element.229) | copy-start | bytes 3932164
  251.7 1.5 copy-start.4
  251.7 2.3 copy-start.5
  251.7 3.0 %copy-start.1 = (f32[80,5120]{1,0:T(8,128)S(1)}, f32[80,5120]{1,0:T(8,128)}, u32[]{:S(2)}) copy-start(f32[80,5120]{1,0:T(8,128)} %get-tuple-element.315) | copy-start | bytes 4915204
  254.7 2.0 copy-start.2

commit v6 on v5

--- a/solution.py
+++ b/solution.py
@@ -43,7 +43,7 @@
 
 def cdf_parts(u):
     z = jnp.abs(u)
-    t = 1.0 / (1.0 + 0.23164189 * z)
+    t = pl.reciprocal(1.0 + 0.23164189 * z, approx=True)
     e = jnp.exp2(u * u * (-0.5 * LOG2E))
     poly = t * (
         0.127414796 + t * (-0.142248368 + t * (0.7107068705 + t * (-0.7265760135 + t * 0.5307027145)))
@@ -127,7 +127,7 @@
     lax.fori_loop(0, length // step, body, 0)
 
 
-def attend(qkv_ref, o_ref, lse_ref, beside):
+def attend(qkv_ref, o_ref, lse_ref, beside, ahead):
     length, width = o_ref.shape
     step = 256
     c = SCALE * LOG2E
@@ -137,6 +137,7 @@
         beside(n)
         t = n // (length // step)
         i = n % (length // step)
+        pl.when(i == 0)(lambda: ahead(t))
         rows = pl.ds(pl.multiple_of(i * step, step), step)
         q = qkv_ref[rows, pl.ds(pl.multiple_of(t * LANES, LANES), LANES)]
         k = qkv_ref[:, pl.ds(pl.multiple_of(width + t * LANES, LANES), LANES)]
@@ -181,7 +182,7 @@
     permute_rows(tokens_ref, slot, xp_ref)
     first_norm(xp_ref, vec_ref, h1_ref)
     project(h1_ref, vec_ref, wqkv_ref, qkv_ref)
-    attend(qkv_ref, o_ref, lse_ref, lambda n: None)
+    attend(qkv_ref, o_ref, lse_ref, lambda n: None, lambda t: None)
     join(xp_ref, o_ref, wout_ref, vec_ref, x1_ref)
 
 
@@ -205,10 +206,10 @@
 
 
 class Gather:
-    def __init__(self, place, own, full, cut, send, recv, local):
-        self.place = place
+    def __init__(self, place, own, full, cut, send, recv, local, cols=slice(None)):
         rows = own.shape[0]
-        at = lambda s, lo=0, hi=rows: full.at[pl.ds(pl.multiple_of(s * rows + lo, 16), hi - lo), :]
+        own = own.at[:, cols]
+        at = lambda s, lo=0, hi=rows: full.at[pl.ds(pl.multiple_of(s * rows + lo, 16), hi - lo), cols]
         me, sib, xn, yn, dg = place.me, place.sib, place.xn, place.yn, place.dg
         moves = [
             (own, at(me), sib), (own, at(me), xn), (own, at(me), yn),
@@ -249,12 +250,99 @@
             copy.wait_send()
 
 
+class WideGather:
+    COPIES = 14
+
+    def __init__(self, place, rep, own, full, send, recv, local):
+        rows, cols = own.shape
+        dim, tile = (0, 16) if rows >= cols else (1, 128)
+        size = own.shape[dim]
+        base = 0
+        third = size // tile // 3 * tile
+        both = size - 2 * third
+        wide = third + both
+        even = rep % 2
+        mult = lambda n: pl.multiple_of(n, tile)
+
+        def cut(ref, s, lo, n):
+            lo = base + lo
+            if dim == 0:
+                return ref.at[pl.ds(mult(s * rows + lo), n), :]
+            return ref.at[pl.ds(pl.multiple_of(s * rows, 16), rows), pl.ds(mult(lo), n)]
+
+        at = functools.partial(cut, full)
+        w, mine, others = even * third, even * wide, (1 - even) * wide
+        first = max(wide // 2 // tile * tile, third)
+        second = wide - first
+        assert second >= third
+        me, sib, xn, yn, dg = place.me, place.sib, place.xn, place.yn, place.dg
+        all_of = lambda s: at(s, 0, size)
+        fsdp = lambda d: {"fsdp": d}
+        pair = {"rep": rep + 1 - 2 * even}
+        piece = cut(own, 0, w, wide)
+        whole = cut(own, 0, 0, size)
+        moves = [
+            (whole, all_of(me), fsdp(sib)),
+            (piece, at(me, w, wide), fsdp(xn)),
+            (piece, at(me, w, wide), fsdp(yn)),
+            (at(xn, w, first),) * 2 + (fsdp(yn),),
+            (at(yn, w + first, second),) * 2 + (fsdp(xn),),
+            (at(xn, mine, third),) * 2 + (pair,),
+            (at(yn, mine, third),) * 2 + (pair,),
+            (at(dg, mine, third),) * 2 + (pair,),
+            (at(xn, w, wide),) * 2 + (fsdp(sib),),
+            (at(yn, w, wide),) * 2 + (fsdp(sib),),
+            (at(dg, w, wide),) * 2 + (fsdp(sib),),
+            (at(xn, others, third),) * 2 + (fsdp(sib),),
+            (at(yn, others, third),) * 2 + (fsdp(sib),),
+            (at(dg, others, third),) * 2 + (fsdp(sib),),
+        ]
+        self.copies = [remote(src, dst, send.at[i], recv.at[i], to) for i, (src, dst, to) in enumerate(moves)]
+        self.local = pltpu.make_async_copy(whole, all_of(me), local)
+
+    def start(self, *which):
+        for i in which:
+            self.copies[i].start()
+
+    def arrived(self, *which):
+        for i in which:
+            self.copies[i].wait_recv()
+
+    def first(self):
+        self.start(1, 2, 0)
+        self.local.start()
+
+    def second(self):
+        self.arrived(1)
+        self.start(3, 5, 8)
+        self.arrived(2)
+        self.start(4, 6, 9)
+
+    def third(self):
+        self.arrived(3, 4)
+        self.start(7, 10)
+
+    def fourth(self):
+        self.arrived(5, 6)
+        self.start(11, 12)
+
+    def fifth(self):
+        self.arrived(7)
+        self.start(13)
+
+    def finish(self):
+        self.arrived(0, 8, 9, 10, 11, 12, 13)
+        self.local.wait()
+        for copy in self.copies:
+            copy.wait_send()
+
+
 def gather_attn_kernel(
     reps,
     tokens_ref, mask_ref, pack_ref, wqkv_in, wout_in, wup_in, wdn_in,
     slot_ref, xp_ref, h1_ref, qkv_ref, o_ref, lse_ref, x1_ref, vec_ref, bup_ref, over_ref,
     wqkv_ref, wout_ref, wup_ref, wdn_ref,
-    packs, overs, send, recv, local, psend, precv, rsend, rrecv,
+    packs, overs, wown, send, recv, local, psend, precv, rsend, rrecv,
 ):
     width = tokens_ref.shape[1]
     share = wqkv_in.shape[0]
@@ -275,15 +363,20 @@
     slot_ref[...] = slot
     row = lax.broadcasted_iota(jnp.int32, (16, LANES), 0)
     over = jnp.where(count[:1] > FEW, 1.0, 0.0)
+    for n in range(3 * width // LANES):
+        t, m = n // 3, n % 3
+        wown[:, n * LANES : (n + 1) * LANES] = wqkv_in[:, m * width + t * LANES : m * width + (t + 1) * LANES]
     packs[me] = jnp.where(row == 13, over, pack_ref[...].astype(F32)).astype(BF16)
     pl.semaphore_wait(barrier, shards + reps - 2)
 
-    gathers = []
-    for n, (own, full, cut) in enumerate(
-        ((wqkv_in, wqkv_ref, 48), (wout_in, wout_ref, 32), (wup_in, wup_ref, 48), (wdn_in, wdn_ref, 320))
-    ):
-        gathers.append(Gather(place, own, full, cut, send.at[n], recv.at[n], local.at[n]))
-    qkv, out, up, down = gathers
+    sems = lambda n: (send.at[n], recv.at[n], local.at[n])
+    early = 2 * 3 * LANES
+    qkv = Gather(place, wown, wqkv_ref, 48, *sems(0), cols=slice(0, early))
+    rest = Gather(place, wown, wqkv_ref, 32, *sems(1), cols=slice(early, 3 * width))
+    out = Gather(place, wout_in, wout_ref, 48, *sems(2))
+    up = WideGather(place, rep, wup_in, wup_ref, *sems(3))
+    down = WideGather(place, rep, wdn_in, wdn_ref, *sems(4))
+    qkv.first()
     vectors = []
     for d in range(1, shards):
         copy = remote(
@@ -291,8 +384,10 @@
         )
         copy.start()
         vectors.append(copy)
-    qkv.first()
     permute_rows(tokens_ref, slot, xp_ref)
+    qkv.second()
+    rest.first()
+    up.first()
     for copy in vectors:
         copy.wait_recv()
     all_over = packs[0]
@@ -304,9 +399,6 @@
         copy = remote(overs.at[rep], overs.at[rep], rsend.at[d - 1], rrecv.at[d - 1], {"rep": (rep + d) % reps})
         copy.start()
         flags.append(copy)
-    qkv.second()
-    out.first()
-    up.first()
     vecs = jnp.zeros((16, width), F32)
     for s in range(shards):
         pack = packs[s]
@@ -321,16 +413,31 @@
     first_norm(xp_ref, vec_ref, h1_ref)
     qkv.third()
     qkv.finish()
-    project(h1_ref, vec_ref, wqkv_ref, qkv_ref)
+
+    plan = (
+        (3, rest.second), (4, down.first), (5, out.first), (6, up.second), (7, rest.third), (8, rest.finish),
+        (9, out.second), (11, up.third), (12, up.fourth), (13, out.third), (13, down.second), (14, up.fifth),
+        (18, down.third), (19, down.fourth),
+    )
 
     def beside(n):
-        for at, step in (
-            (0, out.second), (2, out.third), (4, up.second), (5, down.first), (9, up.third), (14, down.second),
-            (18, down.third),
-        ):
+        for at, step in plan:
             pl.when(n == at)(step)
 
-    attend(qkv_ref, o_ref, lse_ref, beside)
+    def ahead(t):
+        step = 512
+        cols = pl.ds(pl.multiple_of(t * 3 * LANES, LANES), 3 * LANES)
+        at = [pl.multiple_of(n * width + t * LANES, LANES) for n in range(3)]
+        bq = vec_ref[2:3, pl.ds(at[0], LANES)]
+        bv = vec_ref[3:4, pl.ds(at[0], LANES)]
+        bias = jnp.concatenate([bq, jnp.zeros_like(bq), bv], axis=1)
+        for start in range(0, h1_ref.shape[0], step):
+            rows = slice(start, start + step)
+            part = (dot(h1_ref[rows, :], wqkv_ref[:, cols]) + bias).astype(BF16)
+            for n in range(3):
+                qkv_ref[rows, pl.ds(at[n], LANES)] = part[:, n * LANES : (n + 1) * LANES]
+
+    attend(qkv_ref, o_ref, lse_ref, beside, ahead)
     out.finish()
     join(xp_ref, o_ref, wout_ref, vec_ref, x1_ref)
     for copy in flags:
@@ -341,6 +448,7 @@
     for z in range(1, reps):
         worst = jnp.maximum(worst, overs[z])
     over_ref[...] = worst[13:14, :].astype(F32)
+    down.fifth()
     up.finish()
     down.finish()
 
@@ -355,7 +463,7 @@
     dma = pltpu.SemaphoreType.DMA
     return pl.pallas_call(
         functools.partial(gather_attn_kernel, reps),
-        in_specs=[vmem] * 3 + [hbm] * 4,
+        in_specs=[vmem] * 7,
         out_specs=[vmem] * 12 + [hbm] * 2,
         out_shape=(
             sds((8, length), F32),
@@ -376,7 +484,8 @@
         scratch_shapes=[
             pltpu.VMEM((shards, 16, LANES), BF16),
             pltpu.VMEM((reps, 16, LANES), BF16),
-            dma((4, 9)), dma((4, 9)), dma((4,)),
+            pltpu.VMEM(w_qkv.shape, BF16),
+            dma((5, WideGather.COPIES)), dma((5, WideGather.COPIES)), dma((5,)),
             dma((shards - 1,)), dma((shards - 1,)),
             dma((reps - 1,)), dma((reps - 1,)),
         ],
@@ -691,7 +800,7 @@
         unpermute(slot[0:1, :], gtp, gtok)
 
 
-def back_specs(few, length, width):
+def back_specs(few, length, width, grouped=False):
     groups = width // LANES
     whole = lambda *shape: pl.BlockSpec(shape, lambda t: (0,) * len(shape))
     cols = lambda rows, first: pl.BlockSpec((rows, LANES), lambda t: (0, first + t))
@@ -705,9 +814,12 @@
         whole(length, width),
         whole(length, width),
         whole(8, width),
-        cols(width, 0),
-        cols(width, groups),
-        cols(width, 2 * groups),
+    ]
+    if grouped:
+        in_specs += [pl.BlockSpec((width, LANES), lambda t, n=n: (0, 3 * t + n)) for n in range(3)]
+    else:
+        in_specs += [cols(width, n * groups) for n in range(3)]
+    in_specs += [
         whole(few, width),
         whole(8, length),
     ]
@@ -978,7 +1090,7 @@
     share = width // shards
     chips = shards // 2
     sds = jax.ShapeDtypeStruct
-    whole, cols, in_specs, scratch = back_specs(few, length, width)
+    whole, cols, in_specs, scratch = back_specs(few, length, width, True)
     hbm = pl.BlockSpec(memory_space=pl.ANY)
     dma = pltpu.SemaphoreType.DMA
     block = (share, width)
@@ -1139,6 +1251,43 @@
     def z3_done(self):
         pl.when(self.inner)(self.f.wait_send)
         pl.when(self.outer)(self.f.wait_recv)
+
+
+class Direct:
+    def __init__(self, me, shards, rep, reps, src, near, depth, send, recv):
+        self.me, self.shards, self.rep, self.reps = me, shards, rep, reps
+        self.src, self.near, self.depth = src, near, depth
+        self.first = []
+        for d in range(1, shards):
+            to = (me + d) % shards
+            self.first.append(
+                remote(src.at[to % 2, to // 2], near.at[me], send.at[d - 1], recv.at[d - 1], {"fsdp": to})
+            )
+        self.second = []
+        for d in range(1, reps):
+            n = shards - 2 + d
+            self.second.append(remote(depth.at[rep], depth.at[rep], send.at[n], recv.at[n], {"rep": (rep + d) % reps}))
+
+    def start(self):
+        for x in self.first:
+            x.start()
+
+    def middle(self):
+        total = self.src[self.me % 2, self.me // 2].astype(F32)
+        for d in range(1, self.shards):
+            self.first[d - 1].wait()
+            total = total + self.near[(self.me + self.shards - d) % self.shards].astype(F32)
+        self.depth[self.rep] = total.astype(BF16)
+        for x in self.second:
+            x.start()
+
+    def finish(self):
+        for x in self.second:
+            x.wait()
+        total = self.depth[0].astype(F32)
+        for z in range(1, self.reps):
+            total = total + self.depth[z].astype(F32)
+        return total
 
 
 def per_shard(rows, shards, share):
@@ -1331,8 +1480,8 @@
     own, plane, fside, flast, fdepth, ffin,
     onear, oacc, oside, olast, odepth, ofin,
     gg, gnear, gside, glast, gdepth, gfin,
-    sg, snear, sside, slast, sdepth, sfin,
-    send, recv, local,
+    dnear, ddepth, sg, snear, sdepth,
+    send, recv, local, dsend, drecv,
 ):
     t = pl.program_id(0)
     groups = pl.num_programs(0)
@@ -1350,14 +1499,18 @@
     ]
     u4 = make(None, plane, None, fside, flast, None, fdepth.at[3], ffin.at[3], *sems(3))
     uo = make(gout_in.at[1 - core], oacc, onear, oside, olast, None, odepth, ofin, *sems(4))
-    us = make(sg.at[1 - core], sg.at[core], snear, sside, slast, None, sdepth, sfin, *sems(5))
     parts = [
         make(
             gg.at[n, 1 - core], gg.at[n, core], gnear.at[n], gside.at[n], glast.at[n], None, gdepth.at[n],
-            gfin.at[n], *sems(6 + n)
+            gfin.at[n], *sems(5 + n)
         )
-        for n in range(5)
+        for n in range(3)
     ]
+    direct = functools.partial(Direct, place.me, shards, rep, reps)
+    parts += [
+        direct(gg.at[3 + n], dnear.at[n], ddepth.at[n], dsend.at[n], drecv.at[n]) for n in range(2)
+    ]
+    us = direct(sg, snear, sdepth, dsend.at[2], drecv.at[2])
     loads = [
         pltpu.make_async_copy(state_in, own, local.at[0]),
         pltpu.make_async_copy(plane_in, plane, local.at[1]),
@@ -1391,14 +1544,15 @@
         (18, uo.z3_done), (19, u3.z3_done), (19, u4.z2z3),
     ]
     chain = ("near_sum", "side_sum", "last_sum", "z1z2", "z2z3")
-    rest = [[] for _ in range(5)]
-    for n in range(5):
+    rest = []
+    for n in range(3):
         for when, name in zip((2, 5, 7, 9, 11), chain):
             slot_at = 4 * (n + 1) + when
             if slot_at < 20:
                 plan.append((slot_at, getattr(parts[n], name)))
             else:
-                rest[n].append(getattr(parts[n], name))
+                rest.append(getattr(parts[n], name))
+    plan.append((19, parts[3].middle))
     plan.sort(key=lambda entry: entry[0])
 
     def body(i, _):
@@ -1415,35 +1569,22 @@
     for s in range(shards):
         gg[t, s % 2, s // 2, 3 * share :, :] = jnp.zeros((GROUP_ROWS - 3 * share, LANES), BF16)
     for n in range(5):
-        pl.when(t == n)(parts[n].near_start)
+        pl.when(t == n)(parts[n].near_start if n < 3 else parts[n].start)
     group_inputs(few, dq, dkv, wq, wk, wv, dh1)
-
-    def step(n):
-        if rest[n]:
-            rest[n].pop(0)()
 
     @pl.when(t == groups - 1)
     def _():
-        step(4)
-        step(3)
-        step(2)
-        step(1)
+        z1z2, z2z3 = rest
+        z1z2()
         back_finish(few, dh1, xp, vec, g1, late, gtp)
         vectors = per_shard(jnp.concatenate([late[...], jnp.zeros_like(late)], axis=0).astype(BF16), shards, share)
         for s in range(shards):
-            sg[s % 2, s // 2, :16, :] = vectors[s]
-            sg[s % 2, s // 2, 16:, :] = jnp.zeros((SMALL_ROWS - 16, LANES), BF16)
-        us.near_start()
-        step(4)
-        step(3)
-        step(2)
-        step(1)
-        us.near_sum()
+            sg[s % 2, s // 2] = vectors[s]
+        us.start()
+        z2z3()
+        parts[4].middle()
         unpermute(slot[0:1, :], gtp, gtok)
-        step(4)
-        step(3)
-        step(2)
-        us.side_sum()
+        us.middle()
         u4.z3_done()
         for n in range(CHUNKS):
             src = ffin.at[n - 1] if n else own.at[0]
@@ -1452,31 +1593,23 @@
                     b * share : (b + 1) * share, :
                 ].astype(F32)
             gdn_out[n * LANES : (n + 1) * LANES, :] = jnp.transpose(src[width:, :].astype(F32))
-        step(4)
-        step(3)
-        us.last_sum()
         for b in range(CHUNKS):
             gout_out[:, b * LANES : (b + 1) * LANES] = ofin[b * share : (b + 1) * share, :].astype(F32)
         vec_out[0:16, :] = ofin[CHUNKS * share : CHUNKS * share + 16, :].astype(F32)
-        step(3)
-        us.z1z2()
-        step(4)
-        us.z2z3()
         for n in range(5):
-            assert not rest[n]
-            parts[n].z3_done()
+            if n < 3:
+                parts[n].z3_done()
+                parts[n].a.wait_send()
+                done = gfin[n].astype(F32)
+            else:
+                done = parts[n].finish()
             for m in range(3):
-                gqkv_out[:, m * width + n * LANES : m * width + (n + 1) * LANES] = gfin[
-                    n, m * share : (m + 1) * share, :
-                ].astype(F32)
-            parts[n].a.wait_send()
-        us.z3_done()
-        vec_out[16:32, :] = sfin[0:16, :].astype(F32)
+                gqkv_out[:, m * width + n * LANES : m * width + (n + 1) * LANES] = done[m * share : (m + 1) * share, :]
+        vec_out[16:32, :] = us.finish()
         uo.a.wait_send()
-        us.a.wait_send()
-
-
-SMALL_ROWS = 32
+
+
+SMALL_ROWS = 16
 
 
 def back_reduce(few, shards, reps, qkv, do, o, lse, h1, xp, vecs, wqkv, g1, slot, state, plane, gout):
@@ -1487,7 +1620,7 @@
     groups = width // LANES
     hidden = shards * width
     sds = jax.ShapeDtypeStruct
-    whole, cols, in_specs, scratch = back_specs(few, length, width)
+    whole, cols, in_specs, scratch = back_specs(few, length, width, True)
     hbm = pl.BlockSpec(memory_space=pl.ANY)
     dma = pltpu.SemaphoreType.DMA
     vm = lambda *shape: pltpu.VMEM(shape + (LANES,), BF16)
@@ -1521,9 +1654,11 @@
         ]
         + many(4, [fdepth, ffin])
         + [vm(chips, spare), vm(chips, spare)] + buffers(spare)
-        + [vm(5, 2, chips, GROUP_ROWS), vm(5, chips, GROUP_ROWS)] + many(5, buffers(GROUP_ROWS))
-        + [vm(2, chips, SMALL_ROWS), vm(chips, SMALL_ROWS)] + buffers(SMALL_ROWS)
-        + [dma((11, Unit.COPIES)), dma((11, Unit.COPIES)), dma((3,))],
+        + [vm(5, 2, chips, GROUP_ROWS), vm(3, chips, GROUP_ROWS)] + many(3, buffers(GROUP_ROWS))
+        + [vm(2, shards, GROUP_ROWS), vm(2, reps, GROUP_ROWS)]
+        + [vm(2, chips, SMALL_ROWS), vm(shards, SMALL_ROWS), vm(reps, SMALL_ROWS)]
+        + [dma((8, Unit.COPIES)), dma((8, Unit.COPIES)), dma((3,))]
+        + [dma((3, shards + reps - 2)), dma((3, shards + reps - 2))],
         compiler_params=pltpu.CompilerParams(
             vmem_limit_bytes=60 * MB, collective_id=4, has_side_effects=True
         ),

time: 262 us -> 247 us (0.943)
  Pallas kernels: 242 us -> 227 us
    pallas_call x1, Pallas kernels: 94.3 us -> 83.1 us  [gather_attn(): pl.pallas_call(functools.partial(gather_attn_kernel, reps), in_specs=[vme...]
    pallas_call x1, Pallas kernels: 80.7 us -> 76.7 us  [back_reduce(): pl.pallas_call(functools.partial(back_reduce_kernel, few, shards, reps),...]
where the time goes in v6:
time: 247 us; the launch traced here: 243 us
  Pallas kernels  227 us (92%)
  local copies, waits for them, and re-layouts  11 us (4%)
    pallas_call x1, Pallas kernels, gather_attn(): pl.pallas_call(functools.partial(gather_attn_kernel, reps), in_specs=[vme...  83.1 us
    pallas_call x1, Pallas kernels, back_reduce(): pl.pallas_call(functools.partial(back_reduce_kernel, few, shards, reps),...  76.7 us
    pallas_call x1, Pallas kernels, ffn_reduce(): pl.pallas_call(functools.partial(ffn_reduce_kernel, few, shards, reps), g...  67.6 us
    unnamed x36, local copies, waits for them, and re-layouts  8.72 us

profile of v6, /device:TPU:0, one launch (start us, length us, event | category | flops | bytes accessed | tf_op | source)
XLA Modules:
  0.0 243.2 jit_solution(4858083671904004895)
XLA Ops:
  0.6 0.7 convert_element_type.19.mask_ref
  1.3 0.8 stack.35
  2.1 1.3 fusion.3.pack_ref
  3.4 83.1 %gather_attn.1 = (f32[8,1024]{1,0:T(8,128)}, bf16[1024,640]{1,0:T(8,128)(2,1)}, bf16[1024,640]{1,0:T(8,128)(2,1)}, bf16[1024,1920]{1,0:T(8,128)(2,1)}, bf16[1024...) custom-call(bf16[1024,640]{1,0:T(8,128)(2,1)} %bitcast.56, ...), custom_call_target="tpu_custom_call" | custom-call | tf_op jit(solution)/shard_map/gather_attn/pallas_call | solution.py:464
  87.1 67.6 %ffn_reduce.1 = (bf16[1024,640]{1,0:T(8,128)(2,1)}, f32[384,640]{1,0:T(8,128)}, bf16[384,640]{1,0:T(8,128)(2,1)}, bf16[2,4,448,128]{3,2,1,0:T(8,128)(2,1)}, bf16...) custom-call(f32[1024,640]{1,0:T(8,128)} %get-tuple-element.203.x1_ref, bf16[1024,640]{1,0:T(8,128)(2,1)} %bitcast.54, ...), custom_call_target="tpu_custom_call" | custom-call | tf_op jit(solution)/shard_map/ffn_reduce/pallas_call | solution.py:1426
  154.7 76.7 %back_reduce.1 = (bf16[1024,640]{1,0:T(8,128)(2,1)}, f32[80,5120]{1,0:T(8,128)}, f32[640,640]{1,0:T(8,128)}, f32[80,1920]{1,0:T(8,128)}, f32[80,640]{1,0:T(8,128)}, /*index=5*/f32[32,128]{1,0:T(8,128)}) custom-call(bf16[1024,1920]{1,0:T(8,128)(2,1)S(1)} %copy-done, bf16[1024,1920]{1,0:T(8,128)(2,1)S(1)} %copy-done, bf16[1024,1920]{1,0:T(8,128)(2,1)S(1)} %copy-done, ...), custom_call_target="tpu_custom_call" | custom-call | tf_op jit(solution)/shard_map/back_reduce/pallas_call | solution.py:1634
  231.4 2.8 %conditional.1 = (bf16[1024,640]{1,0:T(8,128)(2,1)}, bf16[1024,640]{1,0:T(8,128)(2,1)}, f32[80,5120]{1,0:T(8,128)}, f32[640,640]{1,0:T(8,128)}, f32[80,1920]{1,0...) conditional(s32[]{:T(128)} %bitcast.30, ...), branch_computations={%region_0.1_spmd, %region_1.2_spmd} | conditional | flops 648 | bytes 156380 | solution.py:1750
  232.6 0.8 slice_bitcast_fusion.9
  233.5 0.7 slice_bitcast_fusion.8
  234.2 0.0 copy-start.10
  234.2 0.0 copy-start.11
  234.2 0.0 copy-start.12
  234.2 0.0 copy-start.13
  234.2 0.0 copy-start.14
  234.2 2.6 %copy.67 = bf16[1,1024,640]{2,1,0:T(8,128)(2,1)} copy(bf16[1,1024,640]{2,1,0:T(8,128)(2,1)} %bitcast.58) | data formatting | bytes 2621440
  236.8 1.1 copy.68
  237.9 0.0 copy-done.9
  237.9 0.0 copy-done.10
  238.0 0.3 copy-done.4
  238.3 0.8 copy.69
  239.1 0.7 copy.70
  239.8 1.2 copy.71
  241.0 0.9 copy-done.2
  241.8 1.2 copy.72
  (21 shorter events, 0.0 us)
Async XLA Ops:
  87.1 67.6 %copy-start = (bf16[1024,1920]{1,0:T(8,128)(2,1)S(1)}, bf16[1024,1920]{1,0:T(8,128)(2,1)}, u32[]{:S(2)}) copy-start(bf16[1024,1920]{1,0:T(8,128)(2,1)} %get-tuple-element.211.q.k.v) | copy-start | bytes 11796484
  234.2 3.7 %copy-start.6 = (f32[640]{0:T(1024)}, f32[640]{0:T(1024)S(1)}, u32[]{:S(2)}) copy-start(f32[640]{0:T(1024)S(1)} %get-tuple-element.316) | copy-start | bytes 7684
  234.2 3.7 %copy-start.7 = (f32[80]{0:T(128)}, f32[80]{0:T(128)S(1)}, u32[]{:S(2)}) copy-start(f32[80]{0:T(128)S(1)} %get-tuple-element.318) | copy-start | bytes 964
  234.2 3.8 %copy-start.8 = (f32[80]{0:T(128)}, f32[80]{0:T(128)S(1)}, u32[]{:S(2)}) copy-start(f32[80]{0:T(128)S(1)} %get-tuple-element.314) | copy-start | bytes 964
  234.2 3.8 %copy-start.9 = (f32[80]{0:T(128)}, f32[80]{0:T(128)S(1)}, u32[]{:S(2)}) copy-start(f32[80]{0:T(128)S(1)} %get-tuple-element.313) | copy-start | bytes 964
  234.2 3.7 %copy-start.10 = (f32[80]{0:T(128)}, f32[80]{0:T(128)S(1)}, u32[]{:S(2)}) copy-start(f32[80]{0:T(128)S(1)} %get-tuple-element.312) | copy-start | bytes 964
  234.2 3.7 %copy-start.11 = (f32[80]{0:T(128)}, f32[80]{0:T(128)S(1)}, u32[]{:S(2)}) copy-start(f32[80]{0:T(128)S(1)} %get-tuple-element.310) | copy-start | bytes 964
  234.2 3.7 %copy-start.12 = (f32[80]{0:T(128)}, f32[80]{0:T(128)S(1)}, u32[]{:S(2)}) copy-start(f32[80]{0:T(128)S(1)} %get-tuple-element.309) | copy-start | bytes 964
  234.2 3.7 %copy-start.13 = (f32[80]{0:T(128)}, f32[80]{0:T(128)S(1)}, u32[]{:S(2)}) copy-start(f32[80]{0:T(128)S(1)} %get-tuple-element.307) | copy-start | bytes 964
  234.2 3.7 %copy-start.14 = (f32[80]{0:T(128)}, f32[80]{0:T(128)S(1)}, u32[]{:S(2)}) copy-start(f32[80]{0:T(128)S(1)} %get-tuple-element.306) | copy-start | bytes 964
  234.2 2.6 %copy-start.3 = (bf16[1024,640]{1,0:T(8,128)(2,1)S(1)}, bf16[1024,640]{1,0:T(8,128)(2,1)}, u32[]{:S(2)}) copy-start(bf16[1024,640]{1,0:T(8,128)(2,1)} %get-tuple-element.229) | copy-start | bytes 3932164
  236.8 1.5 copy-start.4
  236.8 2.3 copy-start.5
  236.8 3.0 %copy-start.1 = (f32[80,5120]{1,0:T(8,128)S(1)}, f32[80,5120]{1,0:T(8,128)}, u32[]{:S(2)}) copy-start(f32[80,5120]{1,0:T(8,128)} %get-tuple-element.315) | copy-start | bytes 4915204
  239.8 2.0 copy-start.2

commit v7 on v6

--- a/solution.py
+++ b/solution.py
@@ -1589,20 +1589,18 @@
         for n in range(CHUNKS):
             src = ffin.at[n - 1] if n else own.at[0]
             for b in range(shards):
-                gup_out[:, b * width + n * LANES : b * width + (n + 1) * LANES] = src[
-                    b * share : (b + 1) * share, :
-                ].astype(F32)
-            gdn_out[n * LANES : (n + 1) * LANES, :] = jnp.transpose(src[width:, :].astype(F32))
+                gup_out[:, b * width + n * LANES : b * width + (n + 1) * LANES] = src[b * share : (b + 1) * share, :]
+            gdn_out[n * LANES : (n + 1) * LANES, :] = jnp.transpose(src[width:, :])
         for b in range(CHUNKS):
-            gout_out[:, b * LANES : (b + 1) * LANES] = ofin[b * share : (b + 1) * share, :].astype(F32)
+            gout_out[:, b * LANES : (b + 1) * LANES] = ofin[b * share : (b + 1) * share, :]
         vec_out[0:16, :] = ofin[CHUNKS * share : CHUNKS * share + 16, :].astype(F32)
         for n in range(5):
             if n < 3:
                 parts[n].z3_done()
                 parts[n].a.wait_send()
-                done = gfin[n].astype(F32)
+                done = gfin[n]
             else:
-                done = parts[n].finish()
+                done = parts[n].finish().astype(BF16)
             for m in range(3):
                 gqkv_out[:, m * width + n * LANES : m * width + (n + 1) * LANES] = done[m * share : (m + 1) * share, :]
         vec_out[16:32, :] = us.finish()
@@ -1641,10 +1639,10 @@
         ],
         out_shape=(
             sds((length, width), BF16),
-            sds((share, hidden), F32),
-            sds((width, width), F32),
-            sds((share, 3 * width), F32),
-            sds((share, width), F32),
+            sds((share, hidden), BF16),
+            sds((width, width), BF16),
+            sds((share, 3 * width), BF16),
+            sds((share, width), BF16),
             sds((32, LANES), F32),
         ),
         scratch_shapes=scratch
@@ -1739,17 +1737,19 @@
         )
 
         def redo():
-            *outs, early, late = backward(length)()
+            res, gtok, *outs, early, late = backward(length)()
+            outs = [x.astype(BF16) for x in outs]
             mine, gbup = pick(late, early)
             rows = jnp.concatenate([mine[4:], jnp.zeros((4, share), F32)])
             tail = jnp.concatenate([mine[:4], jnp.zeros((12, share), F32)])
             wide = lambda x: jnp.pad(x, ((0, 0), (0, LANES - share)))
             ups = jnp.pad(gbup.reshape(-1, LANES), ((0, 8 - own // LANES), (0, 0)))
-            return (*outs, jnp.concatenate([wide(rows), ups, wide(tail)]))
+            return (res, gtok, *outs, jnp.concatenate([wide(rows), ups, wide(tail)]))
 
         res, gtok, gup, gdn, gqkv, gout, small = lax.cond(
             small_enough, lambda: (res, gtok, gup, gdn, gqkv, gout, small), redo
         )
+        gup, gdn, gqkv, gout = [x.astype(F32) for x in (gup, gdn, gqkv, gout)]
         mine = [small[n, :share] for n in (16, 17, 18, 19, 0, 1, 2, 3)]
         gbup = small[8 : 8 + own // LANES].reshape(own)
     else:

time: 247 us -> 245 us (level)
  local copies, waits for them, and re-layouts: 11 us -> 6.84 us
    unnamed x36 -> x20, local copies, waits for them, and re-layouts: 8.72 us -> 4.67 us
where the time goes in v7:
time: 245 us; the launch traced here: 241 us
  Pallas kernels  227 us (93%)
  local copies, waits for them, and re-layouts  6.84 us (3%)
  other arithmetic  4.3 us (2%)
    pallas_call x1, Pallas kernels, gather_attn(): pl.pallas_call(functools.partial(gather_attn_kernel, reps), in_specs=[vme...  83.1 us
    pallas_call x1, Pallas kernels, back_reduce(): pl.pallas_call(functools.partial(back_reduce_kernel, few, shards, reps),...  75.9 us
    pallas_call x1, Pallas kernels, ffn_reduce(): pl.pallas_call(functools.partial(ffn_reduce_kernel, few, shards, reps), g...  67.5 us

profile of v7, /device:TPU:0, one launch (start us, length us, event | category | flops | bytes accessed | tf_op | source)
XLA Modules:
  0.0 240.9 jit_solution(1384765519329624870)
XLA Ops:
  0.6 0.7 convert_element_type.71.mask_ref
  1.3 0.8 stack.35
  2.1 1.3 fusion.3.pack_ref
  3.4 83.1 %gather_attn.1 = (f32[8,1024]{1,0:T(8,128)}, bf16[1024,640]{1,0:T(8,128)(2,1)}, bf16[1024,640]{1,0:T(8,128)(2,1)}, bf16[1024,1920]{1,0:T(8,128)(2,1)}, bf16[1024...) custom-call(bf16[1024,640]{1,0:T(8,128)(2,1)} %bitcast.56, ...), custom_call_target="tpu_custom_call" | custom-call | tf_op jit(solution)/shard_map/gather_attn/pallas_call | solution.py:464
  87.2 67.5 %ffn_reduce.1 = (bf16[1024,640]{1,0:T(8,128)(2,1)}, f32[384,640]{1,0:T(8,128)}, bf16[384,640]{1,0:T(8,128)(2,1)}, bf16[2,4,448,128]{3,2,1,0:T(8,128)(2,1)}, bf16...) custom-call(f32[1024,640]{1,0:T(8,128)} %get-tuple-element.207.x1_ref, bf16[1024,640]{1,0:T(8,128)(2,1)} %bitcast.54, ...), custom_call_target="tpu_custom_call" | custom-call | tf_op jit(solution)/shard_map/ffn_reduce/pallas_call | solution.py:1426
  154.8 0.0 copy-done
  154.8 75.9 %back_reduce.1 = (bf16[1024,640]{1,0:T(8,128)(2,1)}, bf16[80,5120]{1,0:T(8,128)(2,1)}, bf16[640,640]{1,0:T(8,128)(2,1)}, bf16[80,1920]{1,0:T(8,128)(2,1)}, bf16[80,640]{1,0:T(8,128)(2,1)}, /*index=5*/f32[32,128]{1,0:T(8,128)}) custom-call(bf16[1024,1920]{1,0:T(8,128)(2,1)S(1)} %copy-done, bf16[1024,1920]{1,0:T(8,128)(2,1)S(1)} %copy-done, ...), custom_call_target="tpu_custom_call" | custom-call | tf_op jit(solution)/shard_map/back_reduce/pallas_call | solution.py:1632
  230.7 5.2 %conditional.1 = (bf16[1024,640]{1,0:T(8,128)(2,1)}, bf16[1024,640]{1,0:T(8,128)(2,1)}, f32[80,5120]{1,0:T(8,128)S(1)}, f32[640,640]{1,0:T(8,128)S(1)}, f32[80,1...) conditional(s32[]{:T(128)} %bitcast.30, ...), branch_computations={%region_0.1_spmd, %region_1.2_spmd} | conditional | flops 2048648 | bytes 18424676 | solution.py:1749
  232.1 0.0 copy-start.5
  232.1 1.3 convert_element_type.64
  233.5 0.0 copy-done.5
  233.5 0.1 convert_element_type.65
  233.6 0.8 copy-done.7
  234.4 0.9 convert_element_type.66
  235.3 0.0 copy-done.13
  235.3 0.5 slice_bitcast_fusion.9
  235.9 0.0 copy-start.8
  235.9 0.0 copy-start.14
  235.9 0.0 copy-start.15
  235.9 0.0 copy-start.16
  235.9 0.0 copy-start.17
  235.9 0.0 copy-start.4
  236.0 3.6 %copy.63 = bf16[1,1024,640]{2,1,0:T(8,128)(2,1)} copy(bf16[1,1024,640]{2,1,0:T(8,128)(2,1)} %bitcast.58) | data formatting | bytes 2621440
  239.5 1.1 copy.64
  (17 shorter events, 0.0 us)
Async XLA Ops:
  87.2 67.6 %copy-start = (bf16[1024,1920]{1,0:T(8,128)(2,1)S(1)}, bf16[1024,1920]{1,0:T(8,128)(2,1)}, u32[]{:S(2)}) copy-start(bf16[1024,1920]{1,0:T(8,128)(2,1)} %get-tuple-element.215.q.k.v) | copy-start | bytes 11796484
  232.1 1.4 copy-start.5
  233.5 1.0 copy-start.7
  233.5 1.8 copy-start.10
  233.5 1.8 copy-start.13
  235.9 4.7 %copy-start.1 = (f32[80,5120]{1,0:T(8,128)}, f32[80,5120]{1,0:T(8,128)S(1)}, u32[]{:S(2)}) copy-start(f32[80,5120]{1,0:T(8,128)S(1)} %get-tuple-element.319) | copy-start | bytes 4915204
  235.9 4.7 %copy-start.2 = (f32[640,640]{1,0:T(8,128)}, f32[640,640]{1,0:T(8,128)S(1)}, u32[]{:S(2)}) copy-start(f32[640,640]{1,0:T(8,128)S(1)} %get-tuple-element.321) | copy-start | bytes 4915204
  235.9 4.7 %copy-start.8 = (f32[80,640]{1,0:T(8,128)}, f32[80,640]{1,0:T(8,128)S(1)}, u32[]{:S(2)}) copy-start(f32[80,640]{1,0:T(8,128)S(1)} %get-tuple-element.315) | copy-start | bytes 614404
  235.9 4.7 %copy-start.14 = (f32[640]{0:T(1024)}, f32[640]{0:T(1024)S(1)}, u32[]{:S(2)}) copy-start(f32[640]{0:T(1024)S(1)} %get-tuple-element.320) | copy-start | bytes 7684
  235.9 4.7 %copy-start.15 = (f32[80]{0:T(128)}, f32[80]{0:T(128)S(1)}, u32[]{:S(2)}) copy-start(f32[80]{0:T(128)S(1)} %get-tuple-element.322) | copy-start | bytes 964
  235.9 4.7 %copy-start.16 = (f32[80]{0:T(128)}, f32[80]{0:T(128)S(1)}, u32[]{:S(2)}) copy-start(f32[80]{0:T(128)S(1)} %get-tuple-element.318) | copy-start | bytes 964
  235.9 4.7 %copy-start.17 = (f32[80]{0:T(128)}, f32[80]{0:T(128)S(1)}, u32[]{:S(2)}) copy-start(f32[80]{0:T(128)S(1)} %get-tuple-element.317) | copy-start | bytes 964
  235.9 3.6 %copy-start.4 = (bf16[1024,640]{1,0:T(8,128)(2,1)S(1)}, bf16[1024,640]{1,0:T(8,128)(2,1)}, u32[]{:S(2)}) copy-start(bf16[1024,640]{1,0:T(8,128)(2,1)} %get-tuple-element.233) | copy-start | bytes 3932164
